TPU v7x, 32 devices: a whole 2x2x4 slice. The times are simulated.
32 devices in a mesh: tok: 8 (over y, x, core), head: 4 (over z).
Axes of the slice: x: 2, y: 2, z: 4, core: 2. Of those that a mesh axis runs over, the one named last changes fastest.
Arguments:
- tokens: bfloat16 [8192, 2048], P(('tok', 'head')), may hold values from -6 to 6
- cotangent: bfloat16 [8192, 2048], P(('tok', 'head')), may hold values from -6 to 6
- doc_lengths: int32 [4], replicated, may hold values from 1 to 4096, 8192 in all
- head_order: int32 [8], replicated, may hold values from 0 to 7, each once
- norm_gain: float32 [2048], replicated, may hold values from 0.5 to 1.5
- w_query: bfloat16 [2048, 2048], P('tok', 'head'), may hold values from -0.125 to 0.125
- w_key: bfloat16 [2048, 2048], P('tok', 'head'), may hold values from -0.125 to 0.125
- w_value: bfloat16 [2048, 4096], P('tok', 'head'), may hold values from -0.125 to 0.125
- w_gate: bfloat16 [2048, 4096], P('tok', 'head'), may hold values from -0.125 to 0.125
- group_gain: float32 [4096], P('head'), may hold values from 0.5 to 1.5
- w_out: bfloat16 [4096, 2048], P('head', 'tok'), may hold values from -0.1875 to 0.1875
- ffn_gain: float32 [2048], replicated, may hold values from 0.5 to 1.5
- w_up: bfloat16 [2048, 4096], P('tok', 'head'), may hold values from -0.125 to 0.125
- w_down: bfloat16 [4096, 2048], P('head', 'tok'), may hold values from -0.125 to 0.125
Outputs:
- layer_out: bfloat16 [8192, 2048], P(('tok', 'head'))
- tokens_grad: float32 [8192, 2048], P(('tok', 'head'))
- norm_gain_grad: float32 [2048], replicated
- w_query_grad: float32 [2048, 2048], P('tok', 'head')
- w_key_grad: float32 [2048, 2048], P('tok', 'head')
- w_value_grad: float32 [2048, 4096], P('tok', 'head')
- w_gate_grad: float32 [2048, 4096], P('tok', 'head')
- group_gain_grad: float32 [4096], P('head')
- w_out_grad: float32 [4096, 2048], P('head', 'tok')
- ffn_gain_grad: float32 [2048], replicated
- w_up_grad: float32 [2048, 4096], P('tok', 'head')
- w_down_grad: float32 [4096, 2048], P('head', 'tok')
Inputs may be any that keep to these rules, and one draw needn't show every extreme that they name: `doc_lengths`: the 4 lengths add up to 8192, and the longest is exactly 4096. `head_order`: each of 0 to 7 appears once.
All inputs are finite; a program needn't handle non-finite values.
Results may differ from a plain program's by a relative error of at most 0.019.
Values may be sent and summed in bfloat16 or wider, within the bound.
A program may use at most 384 MiB of HBM per device.

v0:
```python
import jax
import jax.numpy as jnp
from jax import lax
from jax.sharding import PartitionSpec as P

KEY = 256
VAL = 512
SPAN = 512


EPS = 1e-05
TOP_PRECISION = lax.Precision.HIGHEST
SQRT_HALF = 0.7071067811865476
INV_ROOT_TWO_PI = 0.3989422804014327


def entering(value, axis, join, neutral, backward):
    count = lax.axis_size(axis)
    place = lax.axis_index(axis)
    ahead = count - 1 - place if backward else place
    gathered = jax.tree.map(
        lambda a, kind: lax.all_gather(a.astype(kind), axis), value, (jnp.bfloat16, jnp.bfloat16)
    )
    state = jax.tree.map(lambda a, e: jnp.zeros_like(a) + jnp.asarray(e, a.dtype), value, neutral)

    def one(step, state):
        source = count - 1 - step if backward else step
        return join(
            state,
            jax.tree.map(
                lambda a, own: lax.dynamic_index_in_dim(a, source, 0, False).astype(own.dtype),
                gathered,
                value,
            ),
        )

    return lax.fori_loop(0, ahead, one, state)


def norm_forward(values, gain):
    mean = jnp.mean(values, axis=-1, keepdims=True)
    centred = values - mean
    inverse = lax.rsqrt(jnp.mean(centred * centred, axis=-1, keepdims=True) + EPS)
    unit = centred * inverse
    return (unit * gain, unit, inverse)


def norm_backward(grad_out, unit, inverse, gain):
    scaled = grad_out * gain
    first = jnp.mean(scaled, axis=-1, keepdims=True)
    second = jnp.mean(scaled * unit, axis=-1, keepdims=True)
    return (inverse * (scaled - first - unit * second), jnp.sum(grad_out * unit, axis=0))


def doc_index(row_ids, starts):
    return jnp.sum((starts[None, :] <= row_ids[:, None]).astype(jnp.int32), axis=1) - 1


def doc_position(row_ids, starts):
    first = jnp.max(jnp.where(starts[None, :] <= row_ids[:, None], starts[None, :], 0), axis=1)
    return row_ids - first


def angles(position, half):
    freq = jnp.exp(-jnp.log(10000.0) * jnp.arange(half, dtype=jnp.float32) / half)
    turn = position.astype(jnp.float32)[:, None] * freq[None, :]
    return (jnp.cos(turn)[:, None, :], jnp.sin(turn)[:, None, :])


def rotate(values, cosine, sine):
    half = values.shape[-1] // 2
    first, second = (values[..., :half], values[..., half:])
    return jnp.concatenate(
        [first * cosine - second * sine, first * sine + second * cosine], axis=-1
    )


def unrotate(grads, cosine, sine):
    half = grads.shape[-1] // 2
    first, second = (grads[..., :half], grads[..., half:])
    return jnp.concatenate(
        [first * cosine + second * sine, second * cosine - first * sine], axis=-1
    )


def span_masks(doc_ids, before, log_decay):
    size = doc_ids.shape[0]
    place = jnp.arange(size, dtype=jnp.float32)
    lag = place[:, None] - place[None, :]
    same = (doc_ids[:, None] == doc_ids[None, :]) & (lag >= 0)
    decay = jnp.where(
        same[None], jnp.exp(jnp.maximum(lag, 0.0)[None] * log_decay[:, None, None]), 0.0
    )
    entry_decay = jnp.where(
        (doc_ids == before)[:, None], jnp.exp((place + 1.0)[:, None] * log_decay[None, :]), 0.0
    )
    exit_decay = jnp.where(
        (doc_ids == doc_ids[-1])[:, None],
        jnp.exp((size - 1.0 - place)[:, None] * log_decay[None, :]),
        0.0,
    )
    cross_span_output = jnp.where(doc_ids[-1] == before, jnp.exp(size * log_decay), 0.0)
    return (decay, entry_decay, exit_decay, cross_span_output)


def advance(key_span_rows, value_span_rows, carried_state, masks):
    decay_weighted = value_span_rows.astype(jnp.float32) * masks[2][:, :, None]
    return masks[3][:, None, None] * carried_state + jnp.einsum(
        "gpn,gps->pns", key_span_rows.astype(jnp.float32), decay_weighted, precision=TOP_PRECISION
    )


def span_forward(query_span_rows, key_span_rows, value_span_rows, carried_state, masks):
    scores = jnp.einsum(
        "ihk,jhk->hij", query_span_rows, key_span_rows, preferred_element_type=jnp.float32
    )
    probs = (scores * masks[0]).astype(jnp.bfloat16)
    intra = jnp.einsum("hij,jhv->ihv", probs, value_span_rows, preferred_element_type=jnp.float32)
    between_span_term = (
        jnp.einsum(
            "djc,jcx->djx",
            query_span_rows.astype(jnp.float32),
            carried_state,
            precision=TOP_PRECISION,
        )
        * masks[1][:, :, None]
    )
    return (
        intra + between_span_term,
        advance(key_span_rows, value_span_rows, carried_state, masks),
    )


def span_backward(
    query_span_rows, key_span_rows, value_span_rows, grad_b, carried_state, future_spans_term, masks
):
    decay, entry_decay, exit_decay, cross_span_output = masks
    scores = jnp.einsum(
        "ihk,jhk->hij", query_span_rows, key_span_rows, preferred_element_type=jnp.float32
    )
    probs = (scores * decay).astype(jnp.bfloat16)
    prob_grad = jnp.einsum(
        "ihv,jhv->hij", grad_b, value_span_rows, preferred_element_type=jnp.float32
    )
    score_grad = (prob_grad * decay).astype(jnp.bfloat16)
    query_slice_part = jnp.einsum(
        "hij,jhk->ihk", score_grad, key_span_rows, preferred_element_type=jnp.float32
    )
    key_slice_part = jnp.einsum(
        "hij,ihk->jhk", score_grad, query_span_rows, preferred_element_type=jnp.float32
    )
    value_part = jnp.einsum("hij,ihv->jhv", probs, grad_b, preferred_element_type=jnp.float32)
    decayed_reach = grad_b.astype(jnp.float32) * entry_decay[:, :, None]
    query_slice_part = query_slice_part + jnp.einsum(
        "jbx,bcx->jbc", decayed_reach, carried_state, precision=TOP_PRECISION
    )
    decay_weighted = value_span_rows.astype(jnp.float32) * exit_decay[:, :, None]
    key_slice_part = key_slice_part + jnp.einsum(
        "frq,rzq->frz", decay_weighted, future_spans_term, precision=TOP_PRECISION
    )
    value_part = value_part + exit_decay[:, :, None] * jnp.einsum(
        "ysw,swc->ysc",
        key_span_rows.astype(jnp.float32),
        future_spans_term,
        precision=TOP_PRECISION,
    )
    earlier = cross_span_output[:, None, None] * future_spans_term + jnp.einsum(
        "lsy,lsp->syp", query_span_rows.astype(jnp.float32), decayed_reach, precision=TOP_PRECISION
    )
    return (query_slice_part, key_slice_part, value_part, earlier)


def link(earlier, future_spans_term):
    return (
        earlier[0] * future_spans_term[0],
        future_spans_term[0][:, None, None] * earlier[1] + future_spans_term[1],
    )


def block_rows(array, block):
    return array[block * SPAN : (block + 1) * SPAN]


def gelu_slope(hidden_pre):
    return (
        0.5 * (1.0 + lax.erf(hidden_pre * SQRT_HALF))
        + hidden_pre * jnp.exp(-0.5 * hidden_pre * hidden_pre) * INV_ROOT_TWO_PI
    )


def local(
    tokens,
    cotangent,
    doc_lengths,
    head_order,
    norm_gain,
    w_query,
    w_key,
    w_value,
    w_gate,
    group_gain,
    w_out,
    ffn_gain,
    w_up,
    w_down,
):
    local_heads = w_query.shape[1] // KEY
    head_rank = lax.axis_index("head")
    tok_rank = lax.axis_index("tok")
    tokens_f = tokens.astype(jnp.float32)
    normed1, unit1, inverse1 = norm_forward(tokens_f, norm_gain)
    group = lax.all_gather(normed1.astype(jnp.bfloat16), "head", axis=0, tiled=True)
    group_rows = group.shape[0]
    query_full, key_full, value_full, gate_full, out_local, up_local, down_local = (
        lax.all_gather(w_query, "tok", axis=0, tiled=True),
        lax.all_gather(w_key, "tok", axis=0, tiled=True),
        lax.all_gather(w_value, "tok", axis=0, tiled=True),
        lax.all_gather(w_gate, "tok", axis=0, tiled=True),
        lax.all_gather(w_out, "tok", axis=1, tiled=True),
        lax.all_gather(w_up, "tok", axis=0, tiled=True),
        lax.all_gather(w_down, "tok", axis=1, tiled=True),
    )
    ends = jnp.cumsum(doc_lengths)
    starts = ends - doc_lengths
    first_row = tok_rank * group_rows
    row_ids = first_row + jnp.arange(group_rows, dtype=jnp.int32)
    doc_ids = doc_index(row_ids, starts)
    previous = doc_index(jnp.reshape(first_row - 1, (1,)), starts)[0]
    cosine, sine = angles(doc_position(row_ids, starts), KEY // 2)
    ranks = lax.dynamic_slice_in_dim(head_order, head_rank * local_heads, local_heads)
    log_decay = jnp.log1p(-jnp.exp2(-(5.0 + ranks.astype(jnp.float32))))
    query_proj = jnp.dot(group, query_full, preferred_element_type=jnp.float32).reshape(
        group_rows, local_heads, KEY
    )
    key_proj = jnp.dot(group, key_full, preferred_element_type=jnp.float32).reshape(
        group_rows, local_heads, KEY
    )
    queries = rotate(query_proj, cosine, sine).astype(jnp.bfloat16)
    keys = rotate(key_proj, cosine, sine).astype(jnp.bfloat16)
    values = (
        jnp.dot(group, value_full, preferred_element_type=jnp.float32)
        .astype(jnp.bfloat16)
        .reshape(group_rows, local_heads, VAL)
    )
    gate = jnp.dot(group, gate_full, preferred_element_type=jnp.float32).reshape(
        group_rows, local_heads, VAL
    )
    blocks = group_rows // SPAN
    masks = []
    for block in range(blocks):
        before = previous if block == 0 else doc_ids[block * SPAN - 1]
        masks.append(span_masks(block_rows(doc_ids, block), before, log_decay))
    through = jnp.ones((local_heads,), jnp.float32)
    summary = jnp.zeros((local_heads, KEY, VAL), jnp.float32)
    for block in range(blocks):
        summary = advance(block_rows(keys, block), block_rows(values, block), summary, masks[block])
        through = through * masks[block][3]
    identity = (
        jnp.ones((local_heads,), jnp.float32),
        jnp.zeros((local_heads, KEY, VAL), jnp.float32),
    )
    incoming = entering((through, summary), "tok", link, identity, False)[1]
    states = [incoming]
    outputs = []
    for block in range(blocks):
        produced, following = span_forward(
            block_rows(queries, block),
            block_rows(keys, block),
            block_rows(values, block),
            states[-1],
            masks[block],
        )
        outputs.append(produced)
        states.append(following)
    retained = jnp.concatenate(outputs, axis=0)
    head_gain = group_gain.reshape(local_heads, VAL)
    grouped, unit_g, inverse_g = norm_forward(retained, head_gain)
    sigma = jax.nn.sigmoid(gate)
    swish = gate * sigma
    mixed = (swish * grouped).reshape(group_rows, local_heads * VAL).astype(jnp.bfloat16)
    mixed_rows = lax.all_to_all(mixed, "head", split_axis=0, concat_axis=1, tiled=True)
    out_full, up_full, down_full = (
        lax.all_gather(out_local, "head", axis=0, tiled=True),
        lax.all_gather(up_local, "head", axis=1, tiled=True),
        lax.all_gather(down_local, "head", axis=0, tiled=True),
    )
    resid = tokens_f + jnp.dot(mixed_rows, out_full, preferred_element_type=jnp.float32)
    normed2, unit2, inverse2 = norm_forward(resid, ffn_gain)
    lifted2 = normed2.astype(jnp.bfloat16)
    hidden_pre = jnp.dot(lifted2, up_full, preferred_element_type=jnp.float32)
    hidden = jax.nn.gelu(hidden_pre, approximate=False).astype(jnp.bfloat16)
    layer_out = (resid + jnp.dot(hidden, down_full, preferred_element_type=jnp.float32)).astype(
        jnp.bfloat16
    )
    down_grad = jnp.einsum("rf,rd->fd", hidden, cotangent, preferred_element_type=jnp.float32)
    hidden_grad = jnp.einsum("rd,fd->rf", cotangent, down_full, preferred_element_type=jnp.float32)
    pre_grad = (hidden_grad * gelu_slope(hidden_pre)).astype(jnp.bfloat16)
    up_grad = jnp.einsum("rf,rd->fd", pre_grad, lifted2, preferred_element_type=jnp.float32)
    lifted2_grad = jnp.einsum("rf,df->rd", pre_grad, up_full, preferred_element_type=jnp.float32)
    resid_part, ffn_gain_local = norm_backward(lifted2_grad, unit2, inverse2, ffn_gain)
    resid_grad = cotangent.astype(jnp.float32) + resid_part
    branch_grad = resid_grad.astype(jnp.bfloat16)
    out_grad = jnp.einsum("rc,rd->cd", mixed_rows, branch_grad, preferred_element_type=jnp.float32)
    mixed_grad = jnp.einsum(
        "rd,cd->rc", branch_grad, out_full, preferred_element_type=jnp.float32
    ).astype(jnp.bfloat16)
    out_term, up_term, down_term = (
        lax.psum_scatter(
            out_grad.astype(jnp.bfloat16), "head", scatter_dimension=0, tiled=True
        ).astype(jnp.float32),
        lax.psum_scatter(
            up_grad.astype(jnp.bfloat16), "head", scatter_dimension=0, tiled=True
        ).astype(jnp.float32),
        lax.psum_scatter(
            down_grad.astype(jnp.bfloat16), "head", scatter_dimension=0, tiled=True
        ).astype(jnp.float32),
    )
    head_grad = (
        lax.all_to_all(mixed_grad, "head", split_axis=1, concat_axis=0, tiled=True)
        .astype(jnp.float32)
        .reshape(group_rows, local_heads, VAL)
    )
    gate_grad = (
        (head_grad * grouped * (sigma + swish * (1.0 - sigma)))
        .astype(jnp.bfloat16)
        .reshape(group_rows, local_heads * VAL)
    )
    retained_grad, group_gain_local = norm_backward(head_grad * swish, unit_g, inverse_g, head_gain)
    ret_grad = retained_grad.astype(jnp.bfloat16)
    pending = jnp.zeros((local_heads, KEY, VAL), jnp.float32)
    for block in reversed(range(blocks)):
        decayed_reach = (
            block_rows(ret_grad, block).astype(jnp.float32) * masks[block][1][:, :, None]
        )
        pending = masks[block][3][:, None, None] * pending + jnp.einsum(
            "lsy,lsp->syp",
            block_rows(queries, block).astype(jnp.float32),
            decayed_reach,
            precision=TOP_PRECISION,
        )
    outgoing = entering((through, pending), "tok", link, identity, True)[1]
    future_spans_term = outgoing
    query_parts, key_parts, value_parts = ([], [], [])
    for block in reversed(range(blocks)):
        query_slice_part, key_slice_part, value_part, future_spans_term = span_backward(
            block_rows(queries, block),
            block_rows(keys, block),
            block_rows(values, block),
            block_rows(ret_grad, block),
            states[block],
            future_spans_term,
            masks[block],
        )
        query_parts.append(query_slice_part)
        key_parts.append(key_slice_part)
        value_parts.append(value_part)
    query_grad = (
        unrotate(jnp.concatenate(query_parts[::-1], axis=0), cosine, sine)
        .astype(jnp.bfloat16)
        .reshape(group_rows, local_heads * KEY)
    )
    key_grad = (
        unrotate(jnp.concatenate(key_parts[::-1], axis=0), cosine, sine)
        .astype(jnp.bfloat16)
        .reshape(group_rows, local_heads * KEY)
    )
    value_grad = (
        jnp.concatenate(value_parts[::-1], axis=0)
        .astype(jnp.bfloat16)
        .reshape(group_rows, local_heads * VAL)
    )
    group_grad = jnp.einsum("rc,dc->rd", query_grad, query_full, preferred_element_type=jnp.float32)
    group_grad = group_grad + jnp.einsum(
        "rc,dc->rd", key_grad, key_full, preferred_element_type=jnp.float32
    )
    group_grad = group_grad + jnp.einsum(
        "rc,dc->rd", value_grad, value_full, preferred_element_type=jnp.float32
    )
    group_grad = group_grad + jnp.einsum(
        "rc,dc->rd", gate_grad, gate_full, preferred_element_type=jnp.float32
    )
    row_grad = lax.psum_scatter(
        group_grad.astype(jnp.bfloat16), "head", scatter_dimension=0, tiled=True
    ).astype(jnp.float32)
    query_term = jnp.einsum("rc,rd->cd", query_grad, group, preferred_element_type=jnp.float32)
    key_term = jnp.einsum("rc,rd->cd", key_grad, group, preferred_element_type=jnp.float32)
    value_term = jnp.einsum("rc,rd->cd", value_grad, group, preferred_element_type=jnp.float32)
    gate_term = jnp.einsum("rc,rd->cd", gate_grad, group, preferred_element_type=jnp.float32)
    summed = (
        lax.psum_scatter(
            query_term.astype(jnp.bfloat16), "tok", scatter_dimension=1, tiled=True
        ).astype(jnp.float32),
        lax.psum_scatter(
            key_term.astype(jnp.bfloat16), "tok", scatter_dimension=1, tiled=True
        ).astype(jnp.float32),
        lax.psum_scatter(
            value_term.astype(jnp.bfloat16), "tok", scatter_dimension=1, tiled=True
        ).astype(jnp.float32),
        lax.psum_scatter(
            gate_term.astype(jnp.bfloat16), "tok", scatter_dimension=1, tiled=True
        ).astype(jnp.float32),
        lax.psum_scatter(
            out_term.astype(jnp.bfloat16), "tok", scatter_dimension=1, tiled=True
        ).astype(jnp.float32),
        lax.psum_scatter(
            up_term.astype(jnp.bfloat16), "tok", scatter_dimension=1, tiled=True
        ).astype(jnp.float32),
        lax.psum_scatter(
            down_term.astype(jnp.bfloat16), "tok", scatter_dimension=1, tiled=True
        ).astype(jnp.float32),
    )
    input_part, norm_gain_local = norm_backward(row_grad, unit1, inverse1, norm_gain)
    tokens_grad = resid_grad + input_part
    own_width = group_gain.shape[0]
    padded = jnp.zeros((own_width * lax.axis_size("head"),), jnp.float32)
    padded = lax.dynamic_update_slice_in_dim(
        padded, group_gain_local.reshape(own_width), head_rank * own_width, 0
    )
    norm_sum, ffn_sum, group_sum = lax.psum(
        (norm_gain_local, ffn_gain_local, padded), ("tok", "head")
    )
    group_gain_grad = lax.dynamic_slice_in_dim(group_sum, head_rank * own_width, own_width)
    return (
        layer_out,
        tokens_grad,
        norm_sum,
        summed[0].T,
        summed[1].T,
        summed[2].T,
        summed[3].T,
        group_gain_grad,
        summed[4],
        ffn_sum,
        summed[5].T,
        summed[6],
    )


def solution(mesh):
    return jax.shard_map(
        local,
        mesh=mesh,
        in_specs=(
            P(("tok", "head"), None),
            P(("tok", "head"), None),
            P(),
            P(),
            P(),
            P("tok", "head"),
            P("tok", "head"),
            P("tok", "head"),
            P("tok", "head"),
            P("head"),
            P("head", "tok"),
            P(),
            P("tok", "head"),
            P("head", "tok"),
        ),
        out_specs=(
            P(("tok", "head"), None),
            P(("tok", "head"), None),
            P(),
            P("tok", "head"),
            P("tok", "head"),
            P("tok", "head"),
            P("tok", "head"),
            P("head"),
            P("head", "tok"),
            P(),
            P("tok", "head"),
            P("head", "tok"),
        ),
        check_vma=False,
    )
```

profile of v0, /device:TPU:0, one launch (start us, length us, event | category | flops | bytes accessed | tf_op | source)
XLA Modules:
  0.0 2757.2 jit_solution(15393705383641021835)
XLA Ops:
  25.7 14.8 all-gather.25.cloned.1.call-done
  40.5 82.9 %all-gather.17.cloned.1.call-done = bf16[1024,2048]{1,0:T(8,128)(2,1)} async-done(((bf16[256,2048]{1,0:T(8,128)(2,1)}), bf16[1024,2048]{1,0:T(8,128)(2,1)}) %all-gather.17.cloned.1.call-update) | async-done | bytes 4194320 | tf_op jit(solution)/shard_map/all_gather | solution.py:212
  131.8 20.0 all-gather.23.cloned.1.call-done
  167.0 23.4 all-gather.21.cloned.1.call-done
  190.3 8.3 convolution_convert_fusion.8
  204.3 25.2 all-gather.27.cloned.1.call-done
  229.6 38.4 %all-gather.31.cloned.1.call-done = bf16[2048,1024]{1,0:T(8,128)(2,1)} async-done(((bf16[256,1024]{1,0:T(8,128)(2,1)}), bf16[2048,1024]{1,0:T(8,128)(2,1)}) %all-gather.31.cloned.1.call-update) | async-done | bytes 4194320 | tf_op jit(solution)/shard_map/all_gather | solution.py:220
  268.1 39.3 %all-gather.35.cloned.1.call-done = bf16[1024,2048]{1,0:T(8,128)(2,1)} async-done(((bf16[1024,256]{1,0:T(8,128)(2,1)}), bf16[1024,2048]{1,0:T(8,128)(2,1)}) %all-gather.35.cloned.1.call-update) | async-done | bytes 4194320 | tf_op jit(solution)/shard_map/all_gather | solution.py:221
  308.9 13.2 all-reduce
  330.3 16.3 all-gather.39.cloned.1.call-done
  375.2 10.1 all-gather.19.cloned.1.call-done
  385.2 16.7 multiply_convert_fusion.1
  406.1 110.5 %all_to_all.32 = bf16[4,256,1024]{1,2,0:T(8,128)(2,1)} all-to-all(bf16[4,256,1024]{1,2,0:T(8,128)(2,1)} %copy.196), channel_id=1, replica_groups=mesh['tok'=8,'head'=4] {'head'}, dimensions={0} | all-to-all | bytes 4194304 | tf_op jit(solution)/shard_map/all_to_all | solution.py:281
  516.5 201.7 %all-gather.29.cloned.1.call-done = bf16[4096,2048]{1,0:T(8,128)(2,1)} async-done(((bf16[1024,2048]{1,0:T(8,128)(2,1)}), bf16[4096,2048]{1,0:T(8,128)(2,1)}) %all-gather.29.cloned.1.call-update) | async-done | bytes 16777232 | tf_op jit(solution)/shard_map/all_gather | solution.py:283
  718.2 9.0 fusion.110
  728.9 275.8 %all-gather.33.cloned.1.call-done = bf16[2048,4096]{1,0:T(8,128)(2,1)} async-done(((bf16[2048,1024]{1,0:T(8,128)(2,1)}), bf16[2048,4096]{1,0:T(8,128)(2,1)}) %all-gather.33.cloned.1.call-update) | async-done | bytes 16777232 | tf_op jit(solution)/shard_map/all_gather | solution.py:284
  1004.8 19.1 fusion.3
  1023.9 267.3 %all-gather.37.cloned.1.call-done = bf16[4096,2048]{1,0:T(8,128)(2,1)} async-done(((bf16[1024,2048]{1,0:T(8,128)(2,1)}), bf16[4096,2048]{1,0:T(8,128)(2,1)}) %all-gather.37.cloned.1.call-update) | async-done | bytes 16777232 | tf_op jit(solution)/shard_map/all_gather | solution.py:285
  1291.2 11.0 fusion
  1302.2 13.7 multiply_reduce_fusion.3
  1320.2 12.3 convolution_convert_fusion.3
  1346.0 42.9 %all-to-all-done.1 = bf16[256,4,1024]{2,0,1:T(8,128)(2,1)} async-done(((bf16[256,4,1024]{2,0,1:T(8,128)(2,1)}), bf16[256,4,1024]{2,0,1:T(8,128)(2,1)}, u32[]{:S(2)}, u32[]{:S(2)}) %all-to-all-start.1) | async-done | bytes 2097184 | tf_op jit(solution)/shard_map/all_to_all | solution.py:319
  1392.9 6.6 reshape.548
  1399.5 7.3 copy.271
  1418.9 10.1 convolution_convert_fusion.1
  1429.2 13.0 convolution_convert_fusion.2
  1443.4 9.9 convolution_convert_fusion
  1459.8 6.3 convolution_convert_fusion.4
  1484.8 14.8 while.27
  1513.5 6.2 convolution_convert_fusion.7
  1524.4 6.1 convolution_convert_fusion.6
  1539.1 6.0 convolution_convert_fusion.5
  1545.2 7.2 fusion.118
  1558.2 6.8 fusion.62
  1565.0 11.9 add_convert_fusion
  1576.9 160.4 %reduce-scatter.26.cloned.1.call-done = bf16[1024,2048]{1,0:T(8,128)(2,1)} async-done(((bf16[4096,2048]{1,0:T(8,128)(2,1)}), bf16[1024,2048]{1,0:T(8,128)(2,1)}) %reduce-scatter.26.cloned.1.call-update) | async-done | bytes 4194320 | tf_op jit(solution)/shard_map/reduce_scatter | solution.py:311
  1737.4 283.3 %reduce-scatter.22.cloned.1.call-done = bf16[1024,2048]{1,0:T(8,128)(2,1)} async-done(((bf16[4096,2048]{1,0:T(8,128)(2,1)}), bf16[1024,2048]{1,0:T(8,128)(2,1)}) %reduce-scatter.22.cloned.1.call-update) | async-done | bytes 4194320 | tf_op jit(solution)/shard_map/reduce_scatter | solution.py:308
  2021.0 283.0 %reduce-scatter.30.cloned.1.call-done = bf16[1024,2048]{1,0:T(8,128)(2,1)} async-done(((bf16[4096,2048]{1,0:T(8,128)(2,1)}), bf16[1024,2048]{1,0:T(8,128)(2,1)}) %reduce-scatter.30.cloned.1.call-update) | async-done | bytes 4194320 | tf_op jit(solution)/shard_map/reduce_scatter | solution.py:314
  2304.0 11.9 fusion.24
  2333.1 26.5 reduce-scatter.20.cloned.1.call-done
  2362.1 41.9 %reduce-scatter.14.cloned.1.call-done = bf16[512,256]{1,0:T(8,128)(2,1)} async-done(((bf16[512,2048]{1,0:T(8,128)(2,1)}), bf16[512,256]{1,0:T(8,128)(2,1)}) %reduce-scatter.14.cloned.1.call-update) | async-done | bytes 262160 | tf_op jit(solution)/shard_map/reduce_scatter | solution.py:390
  2408.0 40.9 %reduce-scatter.16.cloned.1.call-done = bf16[512,256]{1,0:T(8,128)(2,1)} async-done(((bf16[512,2048]{1,0:T(8,128)(2,1)}), bf16[512,256]{1,0:T(8,128)(2,1)}) %reduce-scatter.16.cloned.1.call-update) | async-done | bytes 262160 | tf_op jit(solution)/shard_map/reduce_scatter | solution.py:393
  2452.7 50.7 %reduce-scatter.18.cloned.1.call-done = bf16[1024,256]{1,0:T(8,128)(2,1)} async-done(((bf16[1024,2048]{1,0:T(8,128)(2,1)}), bf16[1024,256]{1,0:T(8,128)(2,1)}) %reduce-scatter.18.cloned.1.call-update) | async-done | bytes 524304 | tf_op jit(solution)/shard_map/reduce_scatter | solution.py:396
  2508.0 74.6 %reduce-scatter.12.cloned.1.call-done = bf16[256,2048]{1,0:T(8,128)(2,1)} async-done(((bf16[1024,2048]{1,0:T(8,128)(2,1)}), bf16[256,2048]{1,0:T(8,128)(2,1)}) %reduce-scatter.12.cloned.1.call-update) | async-done | bytes 1048592 | tf_op jit(solution)/shard_map/reduce_scatter | solution.py:382
  2584.8 41.8 %all-reduce.1 = (f32[2048]{0:T(1024)}, f32[4096]{0:T(1024)S(1)}, f32[2048]{0:T(1024)}) all-reduce(f32[2048]{0:T(1024)S(1)} %get-tuple-element.195, f32[4096]{0:T(1024)S(1)} %dynamic_update_slice.3, f32[2048]{0:T(1024)S(1)} %copy-done.71), channel_id=1, replica_groups=mesh['tok'=8,'head'=4] {'tok','head'}, use_global_device_ids=true, to_apply=%region_22.23 | all-reduce | flops 8192 | bytes 65536 | tf_op jit(solution)/shard_map/psum | solution.py:419
  2630.6 7.7 reduce-scatter.28.cloned.1.call-done
  2640.7 52.7 %reduce-scatter.24.cloned.1.call-done = bf16[1024,256]{1,0:T(8,128)(2,1)} async-done(((bf16[1024,2048]{1,0:T(8,128)(2,1)}), bf16[1024,256]{1,0:T(8,128)(2,1)}) %reduce-scatter.24.cloned.1.call-update) | async-done | bytes 524304 | tf_op jit(solution)/shard_map/reduce_scatter | solution.py:402
  2695.5 52.5 %reduce-scatter.32.cloned.1.call-done = bf16[1024,256]{1,0:T(8,128)(2,1)} async-done(((bf16[1024,2048]{1,0:T(8,128)(2,1)}), bf16[1024,256]{1,0:T(8,128)(2,1)}) %reduce-scatter.32.cloned.1.call-update) | async-done | bytes 524304 | tf_op jit(solution)/shard_map/reduce_scatter | solution.py:408
  (356 shorter events, 240.1 us)
Async XLA Ops:
  7.2 14.5 copy-start.79
  7.2 33.4 %all-gather.25.cloned.1.call-start = ((), (), s32[]{:S(2)}) async-start(), calls=%async_computation.17 | async-start | bytes 2359296 | tf_op jit(solution)/shard_map/all_gather | solution.py:216
  7.9 115.6 %all-gather.17.cloned.1.call-start = ((), (), s32[]{:S(2)}) async-start(), calls=%async_computation.13 | async-start | bytes 5242880 | tf_op jit(solution)/shard_map/all_gather | solution.py:212
  14.3 137.6 %all-gather.23.cloned.1.call-start = ((), (), s32[]{:S(2)}) async-start(), calls=%async_computation.16 | async-start | bytes 2359296 | tf_op jit(solution)/shard_map/all_gather | solution.py:215
  15.0 175.3 %all-gather.21.cloned.1.call-start = ((), (), s32[]{:S(2)}) async-start(), calls=%async_computation.15 | async-start | bytes 4718592 | tf_op jit(solution)/shard_map/all_gather | solution.py:217
  15.6 214.0 %all-gather.27.cloned.1.call-start = ((), (), s32[]{:S(2)}) async-start(), calls=%async_computation.18 | async-start | bytes 4718592 | tf_op jit(solution)/shard_map/all_gather | solution.py:219
  16.2 251.9 %all-gather.31.cloned.1.call-start = ((), (), s32[]{:S(2)}) async-start(), calls=%async_computation.20 | async-start | bytes 4718592 | tf_op jit(solution)/shard_map/all_gather | solution.py:220
  16.7 290.6 %all-gather.35.cloned.1.call-start = ((), (), s32[]{:S(2)}) async-start(), calls=%async_computation.22 | async-start | bytes 4718592 | tf_op jit(solution)/shard_map/all_gather | solution.py:221
  17.5 329.1 %all-gather.39.cloned.1.call-start = ((), (), s32[]{:S(2)}) async-start(), calls=%async_computation.35 | async-start | bytes 4718592 | tf_op jit(solution)/shard_map/all_gather | solution.py:22
  22.4 286.3 %copy-start.72 = (f32[2]{0:T(128)}, f32[2]{0:T(128)S(1)}, u32[]{:S(2)}) copy-start(f32[2]{0:T(128)S(1)} %get-tuple-element.224) | copy-start | bytes 28
  22.4 302.9 %copy-start.74 = (f32[2]{0:T(128)}, f32[2]{0:T(128)S(1)}, u32[]{:S(2)}) copy-start(f32[2]{0:T(128)S(1)} %get-tuple-element.225) | copy-start | bytes 28
  23.8 175.0 %copy-start.62 = (f32[512,2]{0,1:T(2,128)}, f32[512,2]{0,1:T(2,128)S(1)}, u32[]{:S(2)}) copy-start(f32[512,2]{0,1:T(2,128)S(1)} %get-tuple-element.270) | copy-start | bytes 12292
  23.8 176.4 %copy-start.64 = (f32[512,2]{0,1:T(2,128)}, f32[512,2]{0,1:T(2,128)S(1)}, u32[]{:S(2)}) copy-start(f32[512,2]{0,1:T(2,128)S(1)} %get-tuple-element.271) | copy-start | bytes 12292
  25.7 138.0 %copy-start.34 = (f32[1024,128]{1,0:T(8,128)}, f32[1024,128]{1,0:T(8,128)S(1)}, u32[]{:S(2)}) copy-start(f32[1024,128]{1,0:T(8,128)S(1)} %get-tuple-element.256) | copy-start | bytes 1572868
  25.7 138.0 %copy-start.36 = (f32[1024,128]{1,0:T(8,128)}, f32[1024,128]{1,0:T(8,128)S(1)}, u32[]{:S(2)}) copy-start(f32[1024,128]{1,0:T(8,128)S(1)} %get-tuple-element.257) | copy-start | bytes 1572868
  166.9 157.6 %copy-start.31 = (bf16[512,2,256]{2,0,1:T(8,128)(2,1)}, bf16[512,2,256]{2,0,1:T(8,128)(2,1)S(1)}, u32[]{:S(2)}) copy-start(bf16[512,2,256]{2,0,1:T(8,128)(2,1)S(1)} %get-tuple-element.253) | copy-start | bytes 1572868
  166.9 158.4 %copy-start.28 = (bf16[512,2,256]{2,0,1:T(8,128)(2,1)}, bf16[512,2,256]{2,0,1:T(8,128)(2,1)S(1)}, u32[]{:S(2)}) copy-start(bf16[512,2,256]{2,0,1:T(8,128)(2,1)S(1)} %get-tuple-element.252) | copy-start | bytes 1572868
  198.8 127.3 %copy-start.15 = (bf16[512,1024]{0,1:T(8,128)(2,1)}, bf16[512,1024]{0,1:T(8,128)(2,1)S(1)}, u32[]{:S(2)}) copy-start(bf16[512,1024]{0,1:T(8,128)(2,1)S(1)} %get-tuple-element.243) | copy-start | bytes 3145732
  198.8 129.4 %copy-start.17 = (bf16[512,1024]{0,1:T(8,128)(2,1)}, bf16[512,1024]{0,1:T(8,128)(2,1)S(1)}, u32[]{:S(2)}) copy-start(bf16[512,1024]{0,1:T(8,128)(2,1)S(1)} %get-tuple-element.242) | copy-start | bytes 3145732
  203.5 181.7 %all-gather.19.cloned.1.call-start = ((), (), s32[]{:S(2)}) async-start(), calls=%async_computation.14 | async-start | bytes 4718592 | tf_op jit(solution)/shard_map/all_gather | solution.py:218
  204.2 514.0 %all-gather.29.cloned.1.call-start = ((), (), s32[]{:S(2)}) async-start(), calls=%async_computation.19 | async-start | bytes 20971520 | tf_op jit(solution)/shard_map/all_gather | solution.py:283
  229.6 775.2 %all-gather.33.cloned.1.call-start = ((), (), s32[]{:S(2)}) async-start(), calls=%async_computation.21 | async-start | bytes 20971520 | tf_op jit(solution)/shard_map/all_gather | solution.py:284
  268.0 39.4 %copy-start.85 = (u32[32]{0:T(128)S(1)}, u32[32]{0:T(128)}, u32[]{:S(2)}) copy-start(u32[32]{0:T(128)} %constant.186) | copy-start | bytes 388
  268.0 1023.1 %all-gather.37.cloned.1.call-start = ((), (), s32[]{:S(2)}) async-start(), calls=%async_computation.23 | async-start | bytes 20971520 | tf_op jit(solution)/shard_map/all_gather | solution.py:285
  370.4 14.9 copy-start.76
  401.9 316.3 %copy-start.3 = (bf16[256,2048]{1,0:T(8,128)(2,1)S(1)}, bf16[256,2048]{1,0:T(8,128)(2,1)}, u32[]{:S(2)}) copy-start(bf16[256,2048]{1,0:T(8,128)(2,1)} %param.18) | copy-start | bytes 3145732
  718.2 286.5 %copy-start.66 = (f32[2048]{0:T(1024)S(1)}, f32[2048]{0:T(1024)}, u32[]{:S(2)}) copy-start(f32[2048]{0:T(1024)} %param.29) | copy-start | bytes 24580
  728.9 562.3 %copy-start.42 = (bf16[256,2048]{1,0:T(8,128)(2,1)S(1)}, bf16[256,2048]{1,0:T(8,128)(2,1)}, u32[]{:S(2)}) copy-start(bf16[256,2048]{1,0:T(8,128)(2,1)} %param.19) | copy-start | bytes 3145732
  1335.7 53.2 %all-to-all-start.1 = ((bf16[256,4,1024]{2,0,1:T(8,128)(2,1)}), bf16[256,4,1024]{2,0,1:T(8,128)(2,1)}, u32[]{:S(2)}, u32[]{:S(2)}) async-start(bf16[256,4,1024]{2,0,1:T(8,128)(2,1)} %bitcast.194), calls=%async_computation.1 | async-start | bytes 4194304 | tf_op jit(solution)/shard_map/all_to_all | solution.py:319
  1340.1 144.6 %all-gather.41.cloned.1.call-start = ((), (), s32[]{:S(2)}) async-start(), calls=%async_computation.36 | async-start | bytes 4718592 | tf_op jit(solution)/shard_map/all_gather | solution.py:22
  1418.8 318.5 %reduce-scatter.26.cloned.1.call-start = ((), (), s32[]{:S(2)}) async-start(), calls=%async_computation.31 | async-start | bytes 20971520 | tf_op jit(solution)/shard_map/reduce_scatter | solution.py:311
  1429.0 591.7 %reduce-scatter.22.cloned.1.call-start = ((), (), s32[]{:S(2)}) async-start(), calls=%async_computation.29 | async-start | bytes 20971520 | tf_op jit(solution)/shard_map/reduce_scatter | solution.py:308
  1442.2 861.7 %reduce-scatter.30.cloned.1.call-start = ((), (), s32[]{:S(2)}) async-start(), calls=%async_computation.33 | async-start | bytes 20971520 | tf_op jit(solution)/shard_map/reduce_scatter | solution.py:314
  1453.4 906.2 %reduce-scatter.20.cloned.1.call-start = ((), (), s32[]{:S(2)}) async-start(), calls=%async_computation.28 | async-start | bytes 4718592 | tf_op jit(solution)/shard_map/reduce_scatter | solution.py:399
  1466.1 937.9 %reduce-scatter.14.cloned.1.call-start = ((), (), s32[]{:S(2)}) async-start(), calls=%async_computation.25 | async-start | bytes 2359296 | tf_op jit(solution)/shard_map/reduce_scatter | solution.py:390
  1484.8 14.9 copy-start.65
  1519.8 929.1 %reduce-scatter.16.cloned.1.call-start = ((), (), s32[]{:S(2)}) async-start(), calls=%async_computation.26 | async-start | bytes 2359296 | tf_op jit(solution)/shard_map/reduce_scatter | solution.py:393
  1530.6 972.8 %reduce-scatter.18.cloned.1.call-start = ((), (), s32[]{:S(2)}) async-start(), calls=%async_computation.27 | async-start | bytes 4718592 | tf_op jit(solution)/shard_map/reduce_scatter | solution.py:396
  1545.1 1037.5 %reduce-scatter.12.cloned.1.call-start = ((), (), s32[]{:S(2)}) async-start(), calls=%async_computation.24 | async-start | bytes 5242880 | tf_op jit(solution)/shard_map/reduce_scatter | solution.py:382
  1576.9 1061.4 %reduce-scatter.28.cloned.1.call-start = ((), (), s32[]{:S(2)}) async-start(), calls=%async_computation.32 | async-start | bytes 4718592 | tf_op jit(solution)/shard_map/reduce_scatter | solution.py:405
  1737.3 956.1 %reduce-scatter.24.cloned.1.call-start = ((), (), s32[]{:S(2)}) async-start(), calls=%async_computation.30 | async-start | bytes 4718592 | tf_op jit(solution)/shard_map/reduce_scatter | solution.py:402
  2020.7 727.2 %reduce-scatter.32.cloned.1.call-start = ((), (), s32[]{:S(2)}) async-start(), calls=%async_computation.34 | async-start | bytes 4718592 | tf_op jit(solution)/shard_map/reduce_scatter | solution.py:408
  2360.7 221.9 %copy-start.4 = (bf16[256,2048]{1,0:T(8,128)(2,1)S(1)}, bf16[256,2048]{1,0:T(8,128)(2,1)}, u32[]{:S(2)}) copy-start(bf16[256,2048]{1,0:T(8,128)(2,1)} %param.18) | copy-start | bytes 3145732
  2360.7 221.9 %copy-start.61 = (f32[2048]{0:T(1024)S(1)}, f32[2048]{0:T(1024)}, u32[]{:S(2)}) copy-start(f32[2048]{0:T(1024)} %param.22) | copy-start | bytes 24580
  2360.8 221.9 %copy-start.68 = (f32[256]{0:T(256)S(1)}, f32[256]{0:T(256)}, u32[]{:S(2)}) copy-start(f32[256]{0:T(256)} %copy-done.67) | copy-start | bytes 3076
  2360.8 221.9 %copy-start.70 = (f32[256]{0:T(256)S(1)}, f32[256]{0:T(256)}, u32[]{:S(2)}) copy-start(f32[256]{0:T(256)} %copy-done.69) | copy-start | bytes 3076
  2405.8 179.0 %copy-start.71 = (f32[2048]{0:T(1024)S(1)}, f32[2048]{0:T(1024)}, u32[]{:S(2)}) copy-start(f32[2048]{0:T(1024)} %get-tuple-element.190) | copy-start | bytes 24580
  2405.8 221.5 %copy-start.11 = (f32[256,2048]{1,0:T(8,128)S(1)}, f32[256,2048]{1,0:T(8,128)}, u32[]{:S(2)}) copy-start(f32[256,2048]{1,0:T(8,128)} %multiply_add_fusion) | copy-start | bytes 6291460
  (63 other events, 234.4 us)
Sparse Core Ops, SparseCore 0:
  9.9 30.5 all-gather.24
  42.7 80.7 all-gather.16
  125.4 26.4 all-gather.22
  153.6 36.7 all-gather.20
  192.1 37.4 all-gather.26
  231.3 36.7 all-gather.30
  269.9 37.4 all-gather.34
  309.8 36.7 all-gather.38
  348.5 36.7 all-gather.18
  386.6 331.5 all-gather.28
  719.8 284.9 all-gather.32
  1006.2 284.9 all-gather.36
  1419.0 35.7 all-gather.40
  1457.0 280.2 reduce-scatter.25
  1739.6 281.0 reduce-scatter.21
  2022.9 281.0 reduce-scatter.29
  2307.5 52.0 reduce-scatter.19
  2362.8 41.2 reduce-scatter.13
  2407.6 41.2 reduce-scatter.15
  2452.1 51.2 reduce-scatter.17
  2505.8 76.7 reduce-scatter.11
  2586.0 52.2 reduce-scatter.27
  2642.0 51.3 reduce-scatter.23
  2696.6 51.2 reduce-scatter.31
where the time goes:
time: 2770 us; the launch traced here: 2760 us
  waiting for transfers between devices  2140 us (77%)
  matrix products  253 us (9%)
  blocking collectives  165 us (6%)
  local copies, waits for them, and re-layouts  95.7 us (3%)
  other arithmetic  79.2 us (3%)
    reduce_scatter x1, waiting for transfers between devices, local(): lax.psum_scatter(out_grad.astype(jnp.bfloat16), 'head', scatter_dimension...  283 us
    reduce_scatter x1, waiting for transfers between devices, local(): lax.psum_scatter(down_grad.astype(jnp.bfloat16), 'head', scatter_dimensio...  283 us
    all_gather x1, waiting for transfers between devices, local(): lax.all_gather(up_local, 'head', axis=1, tiled=True)  276 us
    all_gather x1, waiting for transfers between devices, local(): lax.all_gather(down_local, 'head', axis=0, tiled=True)  267 us
    all_gather x1, waiting for transfers between devices, local(): lax.all_gather(out_local, 'head', axis=0, tiled=True)  202 us
    reduce_scatter x1, waiting for transfers between devices, local(): lax.psum_scatter(up_grad.astype(jnp.bfloat16), 'head', scatter_dimension=...  160 us
    all_to_all x1, blocking collectives, local(): lax.all_to_all(mixed, 'head', split_axis=0, concat_axis=1, tiled=True)  110 us
    all_gather x1, waiting for transfers between devices, local(): lax.all_gather(normed1.astype(jnp.bfloat16), 'head', axis=0, tiled=True)  82.9 us
  transfers between devices with their start and end apart: 25, of which 24 were waited for; matrix products, arithmetic and copies ran while one was open for 12% of the time, Pallas kernels for 0%

commit v1 on v0

v1 whole, which is shorter than its diff:
```python
import jax
import jax.numpy as jnp
from jax import lax
from jax.sharding import PartitionSpec as P

KEY = 256
VAL = 512
SPAN = 512

EPS = 1e-05
SQRT_HALF = 0.7071067811865476
INV_ROOT_TWO_PI = 0.3989422804014327
BF = jnp.bfloat16
F32 = jnp.float32


def mm(left, right):
    return jnp.dot(left, right, preferred_element_type=F32)


def mm_nt(left, right):
    return lax.dot_general(left, right, (((1,), (1,)), ((), ())), preferred_element_type=F32)


def mm_tn(left, right):
    return lax.dot_general(left, right, (((0,), (0,)), ((), ())), preferred_element_type=F32)


def swap(array, axis, bit):
    count = lax.axis_size(axis)
    return lax.ppermute(array, axis, [(i, i ^ bit) for i in range(count)])


def shift(array):
    count = lax.axis_size("head")
    return lax.ppermute(array, "head", [(i, (i + 1) % count) for i in range(count)])


def paired():
    return lax.axis_size("tok") == 8


def reorder(array):
    if not paired():
        return array
    me = lax.axis_index("tok")
    width = array.shape[-1] // 8
    return jnp.concatenate(
        [
            lax.dynamic_slice_in_dim(array, (me ^ r) * width, width, array.ndim - 1)
            for r in range(8)
        ],
        axis=-1,
    )


def halves(array):
    half = array.shape[0] // 2
    return array[:half], array[half:]


def tok_gather(shard, axis):
    if not paired():
        return lax.all_gather(shard, "tok", axis=axis, tiled=True)
    along_x = swap(shard, "tok", 2)
    along_y = swap(shard, "tok", 4)
    far = jnp.concatenate(
        [swap(halves(along_x)[0], "tok", 4), swap(halves(along_y)[1], "tok", 2)], axis=0
    )
    own = [shard, along_x, along_y, far]
    pieces = []
    for piece in own:
        pieces += [piece, swap(piece, "tok", 1)]
    return jnp.concatenate(pieces, axis=axis)


def tok_scatter(pieces):
    pieces = [p.astype(BF) for p in pieces]
    if not paired():
        return lax.psum_scatter(jnp.stack(pieces), "tok", scatter_dimension=0).astype(F32)
    kept = [
        pieces[r].astype(F32) + swap(pieces[r + 1], "tok", 1).astype(F32) for r in (0, 2, 4, 6)
    ]
    zero, two, four, six = kept
    six_a, six_b = halves(six.astype(BF))
    two_a, two_b = halves(two)
    four_a, four_b = halves(four)
    four_a = four_a + swap(six_a, "tok", 2).astype(F32)
    two_b = two_b + swap(six_b, "tok", 4).astype(F32)
    two = jnp.concatenate([two_a, two_b], axis=0).astype(BF)
    four = jnp.concatenate([four_a, four_b], axis=0).astype(BF)
    return zero + swap(two, "tok", 2).astype(F32) + swap(four, "tok", 4).astype(F32)


def head_gather(rows):
    count = lax.axis_size("head")
    me = lax.axis_index("head")
    size = rows.shape[0]
    whole = jnp.zeros((count * size,) + rows.shape[1:], rows.dtype)
    whole = lax.dynamic_update_slice_in_dim(whole, rows, me * size, 0)
    for step in range(1, count):
        rows = shift(rows)
        source = lax.rem(me - step + count, count)
        whole = lax.dynamic_update_slice_in_dim(whole, rows, source * size, 0)
    return whole


def head_scatter(term):
    count = lax.axis_size("head")
    me = lax.axis_index("head")
    total = term(lax.rem(me + count - 1, count))
    for step in range(1, count):
        arrived = shift(total.astype(BF))
        owner = lax.rem(me + 2 * count - 1 - step, count)
        total = term(owner) + arrived.astype(F32)
    return total


def rows_of(array, index, size):
    return lax.dynamic_slice_in_dim(array, index * size, size, 0)


def sum_small(vector, axis):
    count = lax.axis_size(axis)
    bit = 1
    while bit < count:
        vector = vector + swap(vector, axis, bit)
        bit *= 2
    return vector


def norm_forward(values, gain):
    mean = jnp.mean(values, axis=-1, keepdims=True)
    centred = values - mean
    inverse = lax.rsqrt(jnp.mean(centred * centred, axis=-1, keepdims=True) + EPS)
    unit = centred * inverse
    return (unit * gain, unit, inverse)


def norm_backward(grad_out, unit, inverse, gain):
    scaled = grad_out * gain
    first = jnp.mean(scaled, axis=-1, keepdims=True)
    second = jnp.mean(scaled * unit, axis=-1, keepdims=True)
    return (inverse * (scaled - first - unit * second), jnp.sum(grad_out * unit, axis=0))


def doc_index(row_ids, starts):
    return jnp.sum((starts[None, :] <= row_ids[:, None]).astype(jnp.int32), axis=1) - 1


def doc_position(row_ids, starts):
    first = jnp.max(jnp.where(starts[None, :] <= row_ids[:, None], starts[None, :], 0), axis=1)
    return row_ids - first


def angles(position, half):
    freq = jnp.exp(-jnp.log(10000.0) * jnp.arange(half, dtype=F32) / half)
    turn = position.astype(F32)[:, None] * freq[None, :]
    return (jnp.cos(turn), jnp.sin(turn))


def rotate(values, cosine, sine):
    half = values.shape[-1] // 2
    first, second = (values[..., :half], values[..., half:])
    return jnp.concatenate(
        [first * cosine - second * sine, first * sine + second * cosine], axis=-1
    )


def unrotate(grads, cosine, sine):
    return rotate(grads, cosine, -sine)


def span_masks(doc_ids, before, log_decay):
    size = doc_ids.shape[0]
    place = jnp.arange(size, dtype=F32)
    lag = place[:, None] - place[None, :]
    same = (doc_ids[:, None] == doc_ids[None, :]) & (lag >= 0)
    decay = jnp.where(same, jnp.exp(jnp.maximum(lag, 0.0) * log_decay), 0.0)
    reach = jnp.where(doc_ids == before, jnp.exp((place + 1.0) * log_decay), 0.0)[:, None]
    leave = jnp.where(doc_ids == doc_ids[-1], jnp.exp((size - 1.0 - place) * log_decay), 0.0)[
        :, None
    ]
    across = jnp.where(doc_ids[-1] == before, jnp.exp(size * log_decay), 0.0)
    return (decay, reach, leave, across)


def gelu_slope(hidden_pre):
    return (
        0.5 * (1.0 + lax.erf(hidden_pre * SQRT_HALF))
        + hidden_pre * jnp.exp(-0.5 * hidden_pre * hidden_pre) * INV_ROOT_TWO_PI
    )


def local(
    tokens,
    cotangent,
    doc_lengths,
    head_order,
    norm_gain,
    w_query,
    w_key,
    w_value,
    w_gate,
    group_gain,
    w_out,
    ffn_gain,
    w_up,
    w_down,
):
    heads = w_query.shape[1] // KEY
    head_count = lax.axis_size("head")
    tok_count = lax.axis_size("tok")
    z = lax.axis_index("head")
    tok = lax.axis_index("tok")
    rows = tokens.shape[0]
    group_rows = rows * head_count
    blocks = group_rows // SPAN
    width = tokens.shape[1]
    part = width // tok_count

    tokens_f = reorder(tokens).astype(F32)
    cot_own = reorder(cotangent)
    gain1 = reorder(norm_gain)
    gain2 = reorder(ffn_gain)
    normed1, unit1, inverse1 = norm_forward(tokens_f, gain1)
    group = head_gather(normed1.astype(BF))
    qkvg_full = tok_gather(jnp.concatenate([w_query, w_key, w_value, w_gate], axis=1), 0)
    qk = w_query.shape[1]
    vg = w_value.shape[1]
    query_full = qkvg_full[:, :qk]
    key_full = qkvg_full[:, qk : 2 * qk]
    value_full = qkvg_full[:, 2 * qk : 2 * qk + vg]
    gate_full = qkvg_full[:, 2 * qk + vg :]
    out_full = tok_gather(w_out, 1)
    up_two = jnp.concatenate([w_up, swap(w_up, "head", 2)], axis=1)
    down_two = jnp.concatenate([w_down, swap(w_down, "head", 2)], axis=0)
    up_full = tok_gather(up_two, 0)
    down_full = tok_gather(down_two, 1)
    cot_pair = jnp.concatenate([cot_own, swap(cot_own, "head", 1)], axis=0)

    ends = jnp.cumsum(doc_lengths)
    starts = ends - doc_lengths
    first_row = tok * group_rows
    row_ids = first_row + jnp.arange(group_rows, dtype=jnp.int32)
    doc_ids = doc_index(row_ids, starts)
    previous = doc_index(jnp.reshape(first_row - 1, (1,)), starts)[0]
    group_last = doc_index((jnp.arange(tok_count, dtype=jnp.int32) + 1) * group_rows - 1, starts)
    cosine, sine = angles(doc_position(row_ids, starts), KEY // 2)
    ranks = lax.dynamic_slice_in_dim(head_order, z * heads, heads)
    log_decay = jnp.log1p(-jnp.exp2(-(5.0 + ranks.astype(F32))))

    query_proj = mm(group, query_full)
    key_proj = mm(group, key_full)
    value_proj = mm(group, value_full)
    gate = mm(group, gate_full)

    def head_of(array, head, size):
        return array[:, head * size : (head + 1) * size]

    def block_of(array, block):
        return array[block * SPAN : (block + 1) * SPAN]

    q, k, v, masks = [], [], [], []
    for h in range(heads):
        q.append(rotate(head_of(query_proj, h, KEY), cosine, sine).astype(BF))
        k.append(rotate(head_of(key_proj, h, KEY), cosine, sine).astype(BF))
        v.append(head_of(value_proj, h, VAL).astype(BF))
        masks.append(
            [
                span_masks(
                    block_of(doc_ids, b),
                    previous if b == 0 else doc_ids[b * SPAN - 1],
                    log_decay[h],
                )
                for b in range(blocks)
            ]
        )

    group_order = jnp.arange(tok_count, dtype=jnp.int32)

    def weigh(lag, last, h):
        return jnp.where(
            (lag >= 0) & (group_last == last),
            jnp.exp(jnp.maximum(lag, 0).astype(F32) * group_rows * log_decay[h]),
            0.0,
        )

    ends_of = []
    added = []
    for h in range(heads):
        state = jnp.zeros((KEY, VAL), F32)
        terms = []
        for b in range(blocks):
            term = mm_tn(block_of(k[h], b), (block_of(v[h], b) * masks[h][b][2]).astype(BF))
            terms.append(term)
            state = masks[h][b][3] * state + term
        added.append(terms)
        ends_of.append(state.astype(BF))
    all_states = lax.all_gather(jnp.concatenate(ends_of, axis=0), "tok", axis=0)
    lag = tok - 1 - group_order
    states = []
    retained = []
    for h in range(heads):
        weights = weigh(lag, previous, h)
        state = jnp.sum(
            all_states[:, h * KEY : (h + 1) * KEY].astype(F32) * weights[:, None, None], axis=0
        )
        mine = []
        outs = []
        for b in range(blocks):
            mine.append(state.astype(BF))
            qb, kb, vb = block_of(q[h], b), block_of(k[h], b), block_of(v[h], b)
            decay, reach, leave, across = masks[h][b]
            probs = (mm_nt(qb, kb) * decay).astype(BF)
            outs.append(mm(probs, vb) + reach * mm(qb, mine[-1]))
            state = across * state + added[h][b]
        states.append(mine)
        retained.append(jnp.concatenate(outs, axis=0))

    mixed_parts, unit_g, inverse_g, grouped, swish, sigma = [], [], [], [], [], []
    for h in range(heads):
        g, u, i = norm_forward(retained[h], head_of(group_gain[None, :], h, VAL))
        gate_h = head_of(gate, h, VAL)
        s = jax.nn.sigmoid(gate_h)
        unit_g.append(u)
        inverse_g.append(i)
        grouped.append(g)
        sigma.append(s)
        swish.append(gate_h * s)
        mixed_parts.append((swish[-1] * g).astype(BF))
    mixed = jnp.concatenate(mixed_parts, axis=1)

    out_sum = head_scatter(lambda i: mm(rows_of(mixed, i, rows), out_full))
    resid = tokens_f + out_sum
    normed2, unit2, inverse2 = norm_forward(resid, gain2)
    lifted2 = normed2.astype(BF)
    lifted2_pair = jnp.concatenate([lifted2, swap(lifted2, "head", 1)], axis=0)
    hidden_pre = mm(lifted2_pair, up_full)
    hidden = jax.nn.gelu(hidden_pre, approximate=False).astype(BF)
    hidden_grad = mm_nt(cot_pair, down_full)
    pre_grad = (hidden_grad * gelu_slope(hidden_pre)).astype(BF)
    far_grad = mm_nt(pre_grad[rows:], up_full).astype(BF)
    lifted2_grad = mm_nt(pre_grad[:rows], up_full) + swap(far_grad, "head", 1).astype(F32)
    resid_part, ffn_gain_local = norm_backward(lifted2_grad, unit2, inverse2, gain2)
    resid_grad = cot_own.astype(F32) + resid_part
    branch_own = resid_grad.astype(BF)
    branch = head_gather(branch_own)

    far_out = mm(hidden[rows:], down_full).astype(BF)
    layer_out = reorder(
        (resid + mm(hidden[:rows], down_full) + swap(far_out, "head", 1).astype(F32)).astype(BF)
    )

    def piece(array, r):
        return array[:, r * part : (r + 1) * part]

    slots = range(tok_count)
    down_two_grad = tok_scatter([mm_tn(hidden, piece(cot_pair, r)) for r in slots])
    half = down_two_grad.shape[0] // 2
    w_down_grad = down_two_grad[:half] + swap(
        down_two_grad[half:].astype(BF), "head", 2
    ).astype(F32)
    up_two_grad = tok_scatter([mm_tn(piece(lifted2_pair, r), pre_grad) for r in slots])
    half = up_two_grad.shape[1] // 2
    w_up_grad = up_two_grad[:, :half] + swap(
        up_two_grad[:, half:].astype(BF), "head", 2
    ).astype(F32)

    mixed_grad = mm_nt(branch, out_full).astype(BF)
    w_out_grad = tok_scatter([mm_tn(mixed, piece(branch, r)) for r in slots])

    gate_parts, ret_grad, group_gain_parts = [], [], []
    for h in range(heads):
        head_grad = head_of(mixed_grad, h, VAL).astype(F32)
        gate_parts.append(
            (head_grad * grouped[h] * (sigma[h] + swish[h] * (1.0 - sigma[h]))).astype(BF)
        )
        back, gain_term = norm_backward(
            head_grad * swish[h], unit_g[h], inverse_g[h], head_of(group_gain[None, :], h, VAL)
        )
        ret_grad.append(back.astype(BF))
        group_gain_parts.append(gain_term)
    gate_grad = jnp.concatenate(gate_parts, axis=1)
    w_gate_grad = tok_scatter([mm_tn(piece(group, r), gate_grad) for r in slots])

    pending_of, pending_terms = [], []
    for h in range(heads):
        pending = jnp.zeros((KEY, VAL), F32)
        terms = [None] * blocks
        for b in reversed(range(blocks)):
            terms[b] = mm_tn(
                block_of(q[h], b), (block_of(ret_grad[h], b) * masks[h][b][1]).astype(BF)
            )
            pending = masks[h][b][3] * pending + terms[b]
        pending_terms.append(terms)
        pending_of.append(pending.astype(BF))
    all_pending = lax.all_gather(jnp.concatenate(pending_of, axis=0), "tok", axis=0)
    lag_back = group_order - 1 - tok
    shifted_last = doc_index(group_order * group_rows - 1, starts)
    q_parts, k_parts, v_parts = [], [], []
    for h in range(heads):
        weights = jnp.where(
            (lag_back >= 0) & (shifted_last == doc_ids[-1]),
            jnp.exp(jnp.maximum(lag_back, 0).astype(F32) * group_rows * log_decay[h]),
            0.0,
        )
        later = jnp.sum(
            all_pending[:, h * KEY : (h + 1) * KEY].astype(F32) * weights[:, None, None], axis=0
        )
        qg, kg, vg_ = [None] * blocks, [None] * blocks, [None] * blocks
        for b in reversed(range(blocks)):
            qb, kb, vb = block_of(q[h], b), block_of(k[h], b), block_of(v[h], b)
            rb = block_of(ret_grad[h], b)
            decay, reach, leave, across = masks[h][b]
            probs = (mm_nt(qb, kb) * decay).astype(BF)
            score_grad = (mm_nt(rb, vb) * decay).astype(BF)
            later_b = later.astype(BF)
            qg[b] = mm(score_grad, kb) + reach * mm_nt(rb, states[h][b])
            kg[b] = mm_tn(score_grad, qb) + leave * mm_nt(vb, later_b)
            vg_[b] = mm_tn(probs, rb) + leave * mm(kb, later_b)
            later = across * later + pending_terms[h][b]
        q_parts.append(unrotate(jnp.concatenate(qg, axis=0), cosine, sine).astype(BF))
        k_parts.append(unrotate(jnp.concatenate(kg, axis=0), cosine, sine).astype(BF))
        v_parts.append(jnp.concatenate(vg_, axis=0).astype(BF))
    all_grad = jnp.concatenate(q_parts + k_parts + v_parts + [gate_grad], axis=1)
    row_grad = head_scatter(lambda i: mm_nt(rows_of(all_grad, i, rows), qkvg_full))
    input_part, norm_gain_local = norm_backward(row_grad, unit1, inverse1, gain1)
    tokens_grad = reorder(resid_grad + input_part)
    qkv_grad = all_grad[:, : 2 * qk + vg]
    w_qkv_grad = tok_scatter([mm_tn(piece(group, r), qkv_grad) for r in slots])
    w_query_grad = w_qkv_grad[:, :qk]
    w_key_grad = w_qkv_grad[:, qk : 2 * qk]
    w_value_grad = w_qkv_grad[:, 2 * qk :]

    group_gain_grad = sum_small(jnp.concatenate(group_gain_parts, axis=0), "tok")
    ffn_sum = sum_small(sum_small(reorder(ffn_gain_local), "tok"), "head")
    norm_sum = sum_small(sum_small(reorder(norm_gain_local), "tok"), "head")
    return (
        layer_out,
        tokens_grad,
        norm_sum,
        w_query_grad,
        w_key_grad,
        w_value_grad,
        w_gate_grad,
        group_gain_grad,
        w_out_grad,
        ffn_sum,
        w_up_grad,
        w_down_grad,
    )


def solution(mesh):
    rows = P(("tok", "head"), None)
    inward = P("tok", "head")
    outward = P("head", "tok")
    return jax.shard_map(
        local,
        mesh=mesh,
        in_specs=(
            rows, rows, P(), P(), P(), inward, inward, inward, inward, P("head"),
            outward, P(), inward, outward,
        ),
        out_specs=(
            rows, rows, P(), inward, inward, inward, inward, P("head"),
            outward, P(), inward, outward,
        ),
        check_vma=False,
    )
```

time: 2770 us -> 897 us (0.32)
  waiting for transfers between devices: 2140 us -> 378 us
  blocking collectives: 165 us -> 0 us
  starting transfers between devices: 6.18 us -> 77.3 us
  matrix products: 253 us -> 225 us
    reduce_scatter x11 -> x0, waiting for transfers between devices: 1070 us -> none  [the longest x1 283 us: local(): lax.psum_scatter(out_grad.astype(jnp.bfloat16), 'head', scatter_dimension...]
    all_gather x13 -> x2, waiting for transfers between devices: 1020 us -> 0.01 us  [the longest x1 0.01 us: local(): all_states = lax.all_gather(jnp.concatenate(ends_of, axis=0), 'tok', axis=0)]
    ppermute x0 -> x105, waiting for transfers between devices: none -> 378 us  [the longest x93 235 us: swap(): return lax.ppermute(array, axis, [(i, i ^ bit) for i in range(count)])]
    all_to_all x1 -> x0, blocking collectives: 110 us -> none  [local(): lax.all_to_all(mixed, 'head', split_axis=0, concat_axis=1, tiled=True)]
    ppermute x0 -> x105, starting transfers between devices: none -> 76.8 us  [the longest x93 60.8 us: swap(): return lax.ppermute(array, axis, [(i, i ^ bit) for i in range(count)])]
    unnamed x184 -> x408, local copies, waits for them, and re-layouts: 27.9 us -> 93.8 us
    all_to_all x1 -> x0, waiting for transfers between devices: 42.9 us -> none  [local(): lax.all_to_all(mixed_grad, 'head', split_axis=1, concat_axis=0, tiled=True)]
    psum x1 -> x0, blocking collectives: 41.8 us -> none  [local(): lax.psum((norm_gain_local, ffn_gain_local, padded), ('tok', 'head'))]
  transfers between devices with their start and end apart: 25 -> 107, of which waited for: 24 -> 42; matrix products, arithmetic and copies ran while one was open for 12% -> 32% of each run, Pallas kernels for 0% -> 0%
where the time goes in v1:
time: 897 us; the launch traced here: 891 us
  waiting for transfers between devices  378 us (42%)
  matrix products  225 us (25%)
  local copies, waits for them, and re-layouts  123 us (14%)
  starting transfers between devices  77.3 us (9%)
  other arithmetic  65.3 us (7%)
  between operations  23 us (3%)
    ppermute x93, waiting for transfers between devices, swap(): return lax.ppermute(array, axis, [(i, i ^ bit) for i in range(count)])  235 us
    ppermute x12, waiting for transfers between devices, shift(): lax.ppermute(array, 'head', [(i, (i + 1) % count) for i in range(count)])  143 us
    unnamed x408, local copies, waits for them, and re-layouts  93.8 us
    dot_general x24, matrix products, mm_nt(): lax.dot_general(left, right, (((1,), (1,)), ((), ())), preferred_element_...  86.1 us
    dot_general x56, matrix products, mm_tn(): lax.dot_general(left, right, (((0,), (0,)), ((), ())), preferred_element_...  80.3 us
    ppermute x93, starting transfers between devices, swap(): return lax.ppermute(array, axis, [(i, i ^ bit) for i in range(count)])  60.8 us
    dot_general x27, matrix products, mm(): return jnp.dot(left, right, preferred_element_type=F32)  58.1 us
    unnamed x15, other arithmetic  22.7 us
  transfers between devices with their start and end apart: 107, of which 42 were waited for; matrix products, arithmetic and copies ran while one was open for 32% of the time, Pallas kernels for 0%

profile of v1, /device:TPU:0, one launch (start us, length us, event | category | flops | bytes accessed | tf_op | source)
XLA Modules:
  0.0 891.3 jit_solution(9317232002378427865)
XLA Ops:
  36.3 16.5 %collective-permute-done = bf16[256,2048]{1,0:T(8,128)(2,1)S(1)} collective-permute-done((bf16[256,2048]{1,0:T(8,128)(2,1)S(1)}, bf16[256,2048]{1,0:T(8,128)(2,1)S(1)}, u32[]{:S(2)}, u32[]{:S(2)}) %collective-permute-start) | collective-permute-done | bytes 1048608 | tf_op jit(solution)/shard_map/ppermute | solution.py:36
  62.5 6.3 collective-permute-done.4
  74.8 4.1 collective-permute-done.1
  84.8 4.4 collective-permute-done.8
  91.9 12.4 %collective-permute-done.2 = bf16[256,2048]{1,0:T(8,128)(2,1)S(1)} collective-permute-done((bf16[256,2048]{1,0:T(8,128)(2,1)S(1)}, bf16[256,2048]{1,0:T(8,128)(2,1)S(1)}, u32[]{:S(2)}, u32[]{:S(2)}) %collective-permute-start.2) | collective-permute-done | bytes 1048608 | tf_op jit(solution)/shard_map/ppermute | solution.py:36
  113.5 4.1 fusion.79
  121.1 4.8 fusion.81
  126.0 3.3 fusion.220
  159.2 11.1 %collective-permute-done.32 = bf16[1024,256]{1,0:T(8,128)(2,1)} collective-permute-done((bf16[1024,256]{1,0:T(8,128)(2,1)}, bf16[1024,256]{1,0:T(8,128)(2,1)}, u32[]{:S(2)}, u32[]{:S(2)}) %collective-permute-start.32) | collective-permute-done | bytes 524320 | tf_op jit(solution)/shard_map/ppermute | solution.py:31
  174.4 7.1 collective-permute-done.23
  202.3 8.3 fusion.11
  210.6 3.3 multiply_reduce_fusion.2
  242.3 10.7 %collective-permute-done.19 = bf16[256,2048]{1,0:T(8,128)(2,1)S(1)} collective-permute-done((bf16[256,2048]{1,0:T(8,128)(2,1)S(1)}, bf16[256,2048]{1,0:T(8,128)(2,1)S(1)}, u32[]{:S(2)}, u32[]{:S(2)}) %collective-permute-start.19) | collective-permute-done | bytes 1048608 | tf_op jit(solution)/shard_map/ppermute | solution.py:36
  260.4 21.9 %collective-permute-done.20 = bf16[256,2048]{1,0:T(8,128)(2,1)S(1)} collective-permute-done((bf16[256,2048]{1,0:T(8,128)(2,1)S(1)}, bf16[256,2048]{1,0:T(8,128)(2,1)S(1)}, u32[]{:S(2)}, u32[]{:S(2)}) %collective-permute-start.20) | collective-permute-done | bytes 1048608 | tf_op jit(solution)/shard_map/ppermute | solution.py:36
  289.1 37.8 %collective-permute-done.21 = bf16[256,2048]{1,0:T(8,128)(2,1)S(1)} collective-permute-done((bf16[256,2048]{1,0:T(8,128)(2,1)S(1)}, bf16[256,2048]{1,0:T(8,128)(2,1)S(1)}, u32[]{:S(2)}, u32[]{:S(2)}) %collective-permute-start.21) | collective-permute-done | bytes 1048608 | tf_op jit(solution)/shard_map/ppermute | solution.py:36
  332.3 21.7 %collective-permute-done.22 = bf16[256,2048]{1,0:T(8,128)(2,1)S(1)} collective-permute-done((bf16[256,2048]{1,0:T(8,128)(2,1)S(1)}, bf16[256,2048]{1,0:T(8,128)(2,1)S(1)}, u32[]{:S(2)}, u32[]{:S(2)}) %collective-permute-start.22) | collective-permute-done | bytes 1048608 | tf_op jit(solution)/shard_map/ppermute | solution.py:31
  354.0 16.7 %fusion.2 = (bf16[512,2048]{1,0:T(8,128)(2,1)S(1)}, f32[512,2048]{1,0:T(8,128)}) fusion(bf16[2048,2048]{1,0:T(8,128)(2,1)} %constant_dynamic-update-slice_fusion.36, bf16[256,2048]{1,0:T(8,128)(2,1)S(1)} %collective-permute-done.22, bf16[256,2048]{1,0:T(8,128)(2,1)S(1)} %multiply_convert_fusion.2), kind=kOutput, calls=%fused_computation.38 | convolution fusion | flops 4367319040 | bytes 16777216 | tf_op jit(solution)/shard_map/dot_general | solution.py:18
  370.7 3.4 convolution_convert_fusion.27
  374.3 9.2 %fusion.8 = bf16[512,2048]{1,0:T(8,128)(2,1)S(1)} fusion(f32[512,2048]{1,0:T(8,128)} %get-tuple-element.148, bf16[2048,2048]{1,0:T(8,128)(2,1)} %copy-done.109, bf16[256,2048]{1,0:T(8,128)(2,1)} %collective-permute-done.42, bf16[256,2048]{1,0:T(8,128)(2,1)S(1)} %copy-done.13), kind=kOutput, calls=%fused_computation.44 | convolution fusion | flops 4309647360 | bytes 16777216 | tf_op jit(solution)/shard_map/dot_general | solution.py:22
  383.6 6.7 convolution_convert_fusion.26
  410.0 10.6 %collective-permute-done.43 = bf16[256,2048]{1,0:T(8,128)(2,1)S(1)} collective-permute-done((bf16[256,2048]{1,0:T(8,128)(2,1)}, bf16[256,2048]{1,0:T(8,128)(2,1)S(1)}, u32[]{:S(2)}, u32[]{:S(2)}) %collective-permute-start.43) | collective-permute-done | bytes 1048608 | tf_op jit(solution)/shard_map/ppermute | solution.py:31
  421.6 8.0 multiply_reduce_fusion.4
  430.2 6.3 fusion.58
  461.0 16.2 %collective-permute-done.85 = f32[2048]{0:T(1024)S(1)} collective-permute-done((f32[2048]{0:T(1024)S(1)}, f32[2048]{0:T(1024)S(1)}, u32[]{:S(2)}, u32[]{:S(2)}) %collective-permute-start.85) | collective-permute-done | bytes 8224 | tf_op jit(solution)/shard_map/ppermute | solution.py:31
  479.7 9.1 %collective-permute-done.102 = bf16[1024,256]{1,0:T(8,128)(2,1)S(1)} collective-permute-done((bf16[1024,256]{1,0:T(8,128)(2,1)S(1)}, bf16[1024,256]{1,0:T(8,128)(2,1)S(1)}, u32[]{:S(2)}, u32[]{:S(2)}) %collective-permute-start.102) | collective-permute-done | bytes 524320 | tf_op jit(solution)/shard_map/ppermute | solution.py:31
  494.7 20.2 %collective-permute-done.94 = bf16[256,2048]{1,0:T(8,128)(2,1)S(1)} collective-permute-done((bf16[256,2048]{1,0:T(8,128)(2,1)S(1)}, bf16[256,2048]{1,0:T(8,128)(2,1)S(1)}, u32[]{:S(2)}, u32[]{:S(2)}) %collective-permute-start.94) | collective-permute-done | bytes 1048608 | tf_op jit(solution)/shard_map/ppermute | solution.py:31
  522.8 20.1 %collective-permute-done.45 = bf16[256,2048]{1,0:T(8,128)(2,1)S(1)} collective-permute-done((bf16[256,2048]{1,0:T(8,128)(2,1)S(1)}, bf16[256,2048]{1,0:T(8,128)(2,1)S(1)}, u32[]{:S(2)}, u32[]{:S(2)}) %collective-permute-start.45) | collective-permute-done | bytes 1048608 | tf_op jit(solution)/shard_map/ppermute | solution.py:36
  542.9 9.4 %collective-permute-start.46 = (bf16[256,2048]{1,0:T(8,128)(2,1)S(1)}, bf16[256,2048]{1,0:T(8,128)(2,1)S(1)}, u32[]{:S(2)}, u32[]{:S(2)}) collective-permute-start(bf16[256,2048]{1,0:T(8,128)(2,1)S(1)} %collective-permute-done.45), channel_id=1, source_target_pairs={{0,1},{1,2},{2,3},{3,0},{4,5},{5,6},{6,7},{7,4},{8,9},{9,10},{10,1... | collective-permute-start | bytes 3145736 | tf_op jit(solution)/shard_map/ppermute | solution.py:36
  556.3 35.1 %collective-permute-done.95 = bf16[256,1024]{1,0:T(8,128)(2,1)S(1)} collective-permute-done((bf16[256,1024]{1,0:T(8,128)(2,1)S(1)}, bf16[256,1024]{1,0:T(8,128)(2,1)S(1)}, u32[]{:S(2)}, u32[]{:S(2)}) %collective-permute-start.95) | collective-permute-done | bytes 524320 | tf_op jit(solution)/shard_map/ppermute | solution.py:31
  592.5 10.0 %collective-permute-done.104 = bf16[1024,256]{1,0:T(8,128)(2,1)S(1)} collective-permute-done((bf16[1024,256]{1,0:T(8,128)(2,1)S(1)}, bf16[1024,256]{1,0:T(8,128)(2,1)S(1)}, u32[]{:S(2)}, u32[]{:S(2)}) %collective-permute-start.104) | collective-permute-done | bytes 524320 | tf_op jit(solution)/shard_map/ppermute | solution.py:31
  603.7 5.2 convolution_convert_fusion.28
  655.6 9.9 %collective-permute-done.80 = bf16[512,256]{1,0:T(8,128)(2,1)S(1)} collective-permute-done((bf16[512,256]{1,0:T(8,128)(2,1)S(1)}, bf16[512,256]{1,0:T(8,128)(2,1)S(1)}, u32[]{:S(2)}, u32[]{:S(2)}) %collective-permute-start.80) | collective-permute-done | bytes 262176 | tf_op jit(solution)/shard_map/ppermute | solution.py:31
  670.9 10.0 %collective-permute-done.72 = f32[1024]{0:T(1024)S(1)} collective-permute-done((f32[1024]{0:T(1024)S(1)}, f32[1024]{0:T(1024)S(1)}, u32[]{:S(2)}, u32[]{:S(2)}) %collective-permute-start.72) | collective-permute-done | bytes 4128 | tf_op jit(solution)/shard_map/ppermute | solution.py:31
  686.9 3.3 multiply_reduce_fusion
  728.9 9.7 %convolution_convert_fusion.25 = bf16[256,2048]{1,0:T(8,128)(2,1)} fusion(bf16[2048,3072]{1,0:T(8,128)(2,1)} %constant_dynamic-update-slice_fusion.13, bf16[1024,3072]{0,1:T(8,128)(2,1)} %copy-done.133, s32[]{:T(128)S(6)} %select_n.206), kind=kOutput, calls=%fused_computation.156 | convolution fusion | flops 3221749760 | bytes 15204356 | tf_op jit(solution)/shard_map/dot_general | solution.py:22
  750.5 6.6 collective-permute-done.69
  758.2 6.6 collective-permute-done.66
  766.2 10.0 %fusion.22 = bf16[256,2048]{1,0:T(8,128)(2,1)} fusion(bf16[2048,3072]{1,0:T(8,128)(2,1)} %constant_dynamic-update-slice_fusion.13, bf16[256,2048]{1,0:T(8,128)(2,1)} %collective-permute-done.47, bf16[1024,3072]{0,1:T(8,128)(2,1)} %copy-done.133, s32[]{:T(128)S(6)} %select_n.231), kind=kOutput, calls=%fused_computation.94 | convolution fusion | flops 3222798336 | bytes 16252932 | tf_op jit(solution)/shard_map/dot_general | solution.py:22
  788.5 5.8 collective-permute-done.61
  795.1 6.9 collective-permute-done.58
  806.0 13.9 %collective-permute-done.48 = bf16[256,2048]{1,0:T(8,128)(2,1)S(1)} collective-permute-done((bf16[256,2048]{1,0:T(8,128)(2,1)S(1)}, bf16[256,2048]{1,0:T(8,128)(2,1)S(1)}, u32[]{:S(2)}, u32[]{:S(2)}) %collective-permute-start.48) | collective-permute-done | bytes 1048608 | tf_op jit(solution)/shard_map/ppermute | solution.py:36
  821.5 9.7 %fusion.21 = bf16[256,2048]{1,0:T(8,128)(2,1)} fusion(bf16[2048,3072]{1,0:T(8,128)(2,1)} %constant_dynamic-update-slice_fusion.13, bf16[256,2048]{1,0:T(8,128)(2,1)} %copy-done.151, bf16[1024,3072]{0,1:T(8,128)(2,1)} %copy-done.133, s32[]{:T(128)S(6)} %select_n.230), kind=kOutput, calls=%fused_computation.93 | convolution fusion | flops 3222798336 | bytes 16252932 | tf_op jit(solution)/shard_map/dot_general | solution.py:22
  834.5 9.5 %collective-permute-done.59 = bf16[256,2048]{1,0:T(8,128)(2,1)} collective-permute-done((bf16[256,2048]{1,0:T(8,128)(2,1)}, bf16[256,2048]{1,0:T(8,128)(2,1)}, u32[]{:S(2)}, u32[]{:S(2)}) %collective-permute-start.59) | collective-permute-done | bytes 1048608 | tf_op jit(solution)/shard_map/ppermute | solution.py:31
  844.0 3.7 fusion.35
  849.9 6.0 collective-permute-done.49
  856.0 9.4 %fusion.70 = (f32[2048]{0:T(1024)S(1)}, f32[256]{0:T(256)S(1)}, f32[256]{0:T(256)S(1)}, f32[256,2048]{1,0:T(8,128)S(1)}) fusion(bf16[256,2048]{1,0:T(8,128)(2,1)S(1)} %copy-done.7, f32[256]{0:T(256)S(1)} %copy-done.135, f32[256]{0:T(256)S(1)} %copy-done.131, f32[2048]{0:T(1024)S(1)} %copy-done.120, bf16[256,2048]{1,0:T(8,128)(2,1)} %collective-permute-done.49, ...), kind=kOutput, calls=%fused_computation.170 | convolution fusion | flops 3226990080 | bytes 18370564 | tf_op jit(solution)/shard_map/dot_general | solution.py:22
  875.5 3.6 collective-permute-done.53
  879.1 4.5 collective-permute-done.54
  (854 shorter events, 375.4 us)
Async XLA Ops:
  7.2 203.4 %all-gather.5.cloned.1.call-start = ((), (), s32[]{:S(2)}) async-start(), calls=%async_computation | async-start | bytes 4718592 | tf_op jit(solution)/shard_map/all_gather | solution.py:300
  24.6 28.2 %collective-permute-start = (bf16[256,2048]{1,0:T(8,128)(2,1)S(1)}, bf16[256,2048]{1,0:T(8,128)(2,1)S(1)}, u32[]{:S(2)}, u32[]{:S(2)}) collective-permute-start(bf16[256,2048]{1,0:T(8,128)(2,1)S(1)} %get-tuple-element.68), channel_id=1, source_target_pairs={{0,1},{1,2},{2,3},{3,0},{4,5},{5,6},{6,7},{7,4},{8,9},{9,10},{10,1... | collective-permute-start | bytes 3145736 | tf_op jit(solution)/shard_map/ppermute | solution.py:36
  31.6 42.7 %collective-permute-start.3 = (bf16[256,3072]{1,0:T(8,128)(2,1)}, bf16[256,3072]{1,0:T(8,128)(2,1)}, u32[]{:S(2)}, u32[]{:S(2)}) collective-permute-start(bf16[256,3072]{1,0:T(8,128)(2,1)} %get-tuple-element.115), channel_id=1, source_target_pairs={{0,4},{4,0},{8,12},{12,8},{16,20},{20,16},{24,28},{28,24},{1,5},{5... | collective-permute-start | bytes 4718600 | tf_op jit(solution)/shard_map/ppermute | solution.py:31
  31.6 37.1 %collective-permute-start.4 = (bf16[256,3072]{1,0:T(8,128)(2,1)}, bf16[256,3072]{1,0:T(8,128)(2,1)}, u32[]{:S(2)}, u32[]{:S(2)}) collective-permute-start(bf16[256,3072]{1,0:T(8,128)(2,1)} %get-tuple-element.115), channel_id=1, source_target_pairs={{0,8},{4,12},{8,0},{12,4},{16,24},{20,28},{24,16},{28,20},{1,9},{5... | collective-permute-start | bytes 4718600 | tf_op jit(solution)/shard_map/ppermute | solution.py:31
  33.1 38.4 %collective-permute-start.6 = (bf16[256,3072]{1,0:T(8,128)(2,1)}, bf16[256,3072]{1,0:T(8,128)(2,1)}, u32[]{:S(2)}, u32[]{:S(2)}) collective-permute-start(bf16[256,3072]{1,0:T(8,128)(2,1)} %get-tuple-element.115), channel_id=1, source_target_pairs={{0,16},{4,20},{8,24},{12,28},{16,0},{20,4},{24,8},{28,12},{1,17},{... | collective-permute-start | bytes 4718600 | tf_op jit(solution)/shard_map/ppermute | solution.py:31
  74.3 30.1 %collective-permute-start.5 = (bf16[256,3072]{1,0:T(8,128)(2,1)}, bf16[256,3072]{1,0:T(8,128)(2,1)S(1)}, u32[]{:S(2)}, u32[]{:S(2)}) collective-permute-start(bf16[256,3072]{1,0:T(8,128)(2,1)} %collective-permute-done.4), channel_id=1, source_target_pairs={{0,4},{4,0},{8,12},{12,8},{16,20},{20,16},{24,28},{28,24},{1,5},{5... | collective-permute-start | bytes 4718600 | tf_op jit(solution)/shard_map/ppermute | solution.py:31
  74.3 34.7 %collective-permute-start.7 = (bf16[256,3072]{1,0:T(8,128)(2,1)}, bf16[256,3072]{1,0:T(8,128)(2,1)S(1)}, u32[]{:S(2)}, u32[]{:S(2)}) collective-permute-start(bf16[256,3072]{1,0:T(8,128)(2,1)} %collective-permute-done.6), channel_id=1, source_target_pairs={{0,4},{4,0},{8,12},{12,8},{16,20},{20,16},{24,28},{28,24},{1,5},{5... | collective-permute-start | bytes 4718600 | tf_op jit(solution)/shard_map/ppermute | solution.py:31
  131.8 555.1 %all-gather.7.cloned.1.call-start = ((), (), s32[]{:S(2)}) async-start(), calls=%async_computation.1 | async-start | bytes 4718592 | tf_op jit(solution)/shard_map/all_gather | solution.py:398
  134.9 35.4 %collective-permute-start.32 = (bf16[1024,256]{1,0:T(8,128)(2,1)}, bf16[1024,256]{1,0:T(8,128)(2,1)}, u32[]{:S(2)}, u32[]{:S(2)}) collective-permute-start(bf16[1024,256]{1,0:T(8,128)(2,1)} %param.27), channel_id=1, source_target_pairs={{0,2},{1,3},{2,0},{3,1},{4,6},{5,7},{6,4},{7,5},{8,10},{9,11},{10,... | collective-permute-start | bytes 1572872 | tf_op jit(solution)/shard_map/ppermute | solution.py:31
  134.9 46.5 %collective-permute-start.23 = (bf16[256,1024]{1,0:T(8,128)(2,1)}, bf16[256,1024]{1,0:T(8,128)(2,1)}, u32[]{:S(2)}, u32[]{:S(2)}) collective-permute-start(bf16[256,1024]{1,0:T(8,128)(2,1)} %param.26), channel_id=1, source_target_pairs={{0,2},{1,3},{2,0},{3,1},{4,6},{5,7},{6,4},{7,5},{8,10},{9,11},{10,... | collective-permute-start | bytes 1572872 | tf_op jit(solution)/shard_map/ppermute | solution.py:31
  153.5 30.2 %collective-permute-start.16 = (bf16[512,256]{1,0:T(8,128)(2,1)S(1)}, bf16[512,256]{1,0:T(8,128)(2,1)S(1)}, u32[]{:S(2)}, u32[]{:S(2)}) collective-permute-start(bf16[512,256]{1,0:T(8,128)(2,1)S(1)} %slice.656), channel_id=1, source_target_pairs={{0,16},{4,20},{8,24},{12,28},{16,0},{20,4},{24,8},{28,12},{1,17},{... | collective-permute-start | bytes 786440 | tf_op jit(solution)/shard_map/ppermute | solution.py:31
  155.7 28.5 %collective-permute-start.17 = (bf16[512,256]{1,0:T(8,128)(2,1)S(1)}, bf16[512,256]{1,0:T(8,128)(2,1)S(1)}, u32[]{:S(2)}, u32[]{:S(2)}) collective-permute-start(bf16[512,256]{1,0:T(8,128)(2,1)S(1)} %slice.657), channel_id=1, source_target_pairs={{0,8},{4,12},{8,0},{12,4},{16,24},{20,28},{24,16},{28,20},{1,9},{5... | collective-permute-start | bytes 786440 | tf_op jit(solution)/shard_map/ppermute | solution.py:31
  157.2 28.0 %collective-permute-start.13 = (bf16[1024,256]{1,0:T(8,128)(2,1)}, bf16[1024,256]{1,0:T(8,128)(2,1)S(1)}, u32[]{:S(2)}, u32[]{:S(2)}) collective-permute-start(bf16[1024,256]{1,0:T(8,128)(2,1)} %collective-permute-done.12), channel_id=1, source_target_pairs={{0,4},{4,0},{8,12},{12,8},{16,20},{20,16},{24,28},{28,24},{1,5},{5... | collective-permute-start | bytes 1572872 | tf_op jit(solution)/shard_map/ppermute | solution.py:31
  181.4 54.4 %collective-permute-start.33 = (bf16[2048,256]{1,0:T(8,128)(2,1)}, bf16[2048,256]{1,0:T(8,128)(2,1)}, u32[]{:S(2)}, u32[]{:S(2)}) collective-permute-start(bf16[2048,256]{1,0:T(8,128)(2,1)} %get-tuple-element.103), channel_id=1, source_target_pairs={{0,4},{4,0},{8,12},{12,8},{16,20},{20,16},{24,28},{28,24},{1,5},{5... | collective-permute-start | bytes 3145736 | tf_op jit(solution)/shard_map/ppermute | solution.py:31
  183.7 40.5 %collective-permute-start.34 = (bf16[2048,256]{1,0:T(8,128)(2,1)}, bf16[2048,256]{1,0:T(8,128)(2,1)}, u32[]{:S(2)}, u32[]{:S(2)}) collective-permute-start(bf16[2048,256]{1,0:T(8,128)(2,1)} %get-tuple-element.103), channel_id=1, source_target_pairs={{0,8},{4,12},{8,0},{12,4},{16,24},{20,28},{24,16},{28,20},{1,9},{5... | collective-permute-start | bytes 3145736 | tf_op jit(solution)/shard_map/ppermute | solution.py:31
  184.2 41.7 %collective-permute-start.36 = (bf16[2048,256]{1,0:T(8,128)(2,1)}, bf16[2048,256]{1,0:T(8,128)(2,1)}, u32[]{:S(2)}, u32[]{:S(2)}) collective-permute-start(bf16[2048,256]{1,0:T(8,128)(2,1)} %get-tuple-element.103), channel_id=1, source_target_pairs={{0,16},{4,20},{8,24},{12,28},{16,0},{20,4},{24,8},{28,12},{1,17},{... | collective-permute-start | bytes 3145736 | tf_op jit(solution)/shard_map/ppermute | solution.py:31
  188.2 43.9 %collective-permute-start.25 = (bf16[256,2048]{1,0:T(8,128)(2,1)}, bf16[256,2048]{1,0:T(8,128)(2,1)}, u32[]{:S(2)}, u32[]{:S(2)}) collective-permute-start(bf16[256,2048]{1,0:T(8,128)(2,1)} %get-tuple-element.99), channel_id=1, source_target_pairs={{0,8},{4,12},{8,0},{12,4},{16,24},{20,28},{24,16},{28,20},{1,9},{5... | collective-permute-start | bytes 3145736 | tf_op jit(solution)/shard_map/ppermute | solution.py:31
  191.5 42.1 %collective-permute-start.27 = (bf16[256,2048]{1,0:T(8,128)(2,1)}, bf16[256,2048]{1,0:T(8,128)(2,1)}, u32[]{:S(2)}, u32[]{:S(2)}) collective-permute-start(bf16[256,2048]{1,0:T(8,128)(2,1)} %get-tuple-element.99), channel_id=1, source_target_pairs={{0,16},{4,20},{8,24},{12,28},{16,0},{20,4},{24,8},{28,12},{1,17},{... | collective-permute-start | bytes 3145736 | tf_op jit(solution)/shard_map/ppermute | solution.py:31
  254.3 28.0 %collective-permute-start.20 = (bf16[256,2048]{1,0:T(8,128)(2,1)S(1)}, bf16[256,2048]{1,0:T(8,128)(2,1)S(1)}, u32[]{:S(2)}, u32[]{:S(2)}) collective-permute-start(bf16[256,2048]{1,0:T(8,128)(2,1)S(1)} %fusion.24), channel_id=1, source_target_pairs={{0,1},{1,2},{2,3},{3,0},{4,5},{5,6},{6,7},{7,4},{8,9},{9,10},{10,1... | collective-permute-start | bytes 3145736 | tf_op jit(solution)/shard_map/ppermute | solution.py:36
  256.9 117.4 %collective-permute-start.42 = (bf16[256,2048]{1,0:T(8,128)(2,1)S(1)}, bf16[256,2048]{1,0:T(8,128)(2,1)}, u32[]{:S(2)}, u32[]{:S(2)}) collective-permute-start(bf16[256,2048]{1,0:T(8,128)(2,1)S(1)} %copy-done.13), channel_id=1, source_target_pairs={{0,1},{1,0},{2,3},{3,2},{4,5},{5,4},{6,7},{7,6},{8,9},{9,8},{10,11... | collective-permute-start | bytes 3145736 | tf_op jit(solution)/shard_map/ppermute | solution.py:31
  258.3 29.7 %collective-permute-start.28 = (bf16[256,2048]{1,0:T(8,128)(2,1)}, bf16[256,2048]{1,0:T(8,128)(2,1)S(1)}, u32[]{:S(2)}, u32[]{:S(2)}) collective-permute-start(bf16[256,2048]{1,0:T(8,128)(2,1)} %collective-permute-done.27), channel_id=1, source_target_pairs={{0,4},{4,0},{8,12},{12,8},{16,20},{20,16},{24,28},{28,24},{1,5},{5... | collective-permute-start | bytes 3145736 | tf_op jit(solution)/shard_map/ppermute | solution.py:31
  282.3 48.7 %collective-permute-start.40 = (bf16[2048,256]{1,0:T(8,128)(2,1)S(1)}, bf16[2048,256]{1,0:T(8,128)(2,1)S(1)}, u32[]{:S(2)}, u32[]{:S(2)}) collective-permute-start(bf16[2048,256]{1,0:T(8,128)(2,1)S(1)} %pad_maximum_fusion.10), channel_id=1, source_target_pairs={{0,4},{4,0},{8,12},{12,8},{16,20},{20,16},{24,28},{28,24},{1,5},{5... | collective-permute-start | bytes 3145736 | tf_op jit(solution)/shard_map/ppermute | solution.py:31
  283.6 43.2 %collective-permute-start.21 = (bf16[256,2048]{1,0:T(8,128)(2,1)S(1)}, bf16[256,2048]{1,0:T(8,128)(2,1)S(1)}, u32[]{:S(2)}, u32[]{:S(2)}) collective-permute-start(bf16[256,2048]{1,0:T(8,128)(2,1)S(1)} %fusion.23), channel_id=1, source_target_pairs={{0,1},{1,2},{2,3},{3,0},{4,5},{5,6},{6,7},{7,4},{8,9},{9,10},{10,1... | collective-permute-start | bytes 3145736 | tf_op jit(solution)/shard_map/ppermute | solution.py:36
  283.9 47.2 %collective-permute-start.31 = (bf16[256,2048]{1,0:T(8,128)(2,1)S(1)}, bf16[256,2048]{1,0:T(8,128)(2,1)S(1)}, u32[]{:S(2)}, u32[]{:S(2)}) collective-permute-start(bf16[256,2048]{1,0:T(8,128)(2,1)S(1)} %pad_maximum_fusion.9), channel_id=1, source_target_pairs={{0,4},{4,0},{8,12},{12,8},{16,20},{20,16},{24,28},{28,24},{1,5},{5... | collective-permute-start | bytes 3145736 | tf_op jit(solution)/shard_map/ppermute | solution.py:31
  374.1 55.7 %collective-permute-start.41 = (bf16[256,2048]{1,0:T(8,128)(2,1)}, bf16[256,2048]{1,0:T(8,128)(2,1)}, u32[]{:S(2)}, u32[]{:S(2)}) collective-permute-start(bf16[256,2048]{1,0:T(8,128)(2,1)} %convolution_convert_fusion.27), channel_id=1, source_target_pairs={{0,1},{1,0},{2,3},{3,2},{4,5},{5,4},{6,7},{7,6},{8,9},{9,8},{10,11... | collective-permute-start | bytes 3145736 | tf_op jit(solution)/shard_map/ppermute | solution.py:31
  390.3 30.4 %collective-permute-start.43 = (bf16[256,2048]{1,0:T(8,128)(2,1)}, bf16[256,2048]{1,0:T(8,128)(2,1)S(1)}, u32[]{:S(2)}, u32[]{:S(2)}) collective-permute-start(bf16[256,2048]{1,0:T(8,128)(2,1)} %convolution_convert_fusion.26), channel_id=1, source_target_pairs={{0,1},{1,0},{2,3},{3,2},{4,5},{5,4},{6,7},{7,6},{8,9},{9,8},{10,11... | collective-permute-start | bytes 3145736 | tf_op jit(solution)/shard_map/ppermute | solution.py:31
  393.7 56.4 %collective-permute-start.92 = (bf16[256,2048]{1,0:T(8,128)(2,1)}, bf16[256,2048]{1,0:T(8,128)(2,1)}, u32[]{:S(2)}, u32[]{:S(2)}) collective-permute-start(bf16[256,2048]{1,0:T(8,128)(2,1)} %convolution_convert_fusion.8), channel_id=1, source_target_pairs={{0,4},{4,0},{8,12},{12,8},{16,20},{20,16},{24,28},{28,24},{1,5},{5... | collective-permute-start | bytes 3145736 | tf_op jit(solution)/shard_map/ppermute | solution.py:31
  395.4 41.6 %collective-permute-start.89 = (bf16[256,2048]{1,0:T(8,128)(2,1)}, bf16[256,2048]{1,0:T(8,128)(2,1)}, u32[]{:S(2)}, u32[]{:S(2)}) collective-permute-start(bf16[256,2048]{1,0:T(8,128)(2,1)} %convolution_convert_fusion.10), channel_id=1, source_target_pairs={{0,4},{4,0},{8,12},{12,8},{16,20},{20,16},{24,28},{28,24},{1,5},{5... | collective-permute-start | bytes 3145736 | tf_op jit(solution)/shard_map/ppermute | solution.py:31
  397.7 56.6 %collective-permute-start.88 = (bf16[256,2048]{1,0:T(8,128)(2,1)}, bf16[256,2048]{1,0:T(8,128)(2,1)}, u32[]{:S(2)}, u32[]{:S(2)}) collective-permute-start(bf16[256,2048]{1,0:T(8,128)(2,1)} %convolution_convert_fusion.12), channel_id=1, source_target_pairs={{0,4},{4,0},{8,12},{12,8},{16,20},{20,16},{24,28},{28,24},{1,5},{5... | collective-permute-start | bytes 3145736 | tf_op jit(solution)/shard_map/ppermute | solution.py:31
  421.6 70.9 %collective-permute-start.87 = (bf16[256,2048]{1,0:T(8,128)(2,1)}, bf16[256,2048]{1,0:T(8,128)(2,1)}, u32[]{:S(2)}, u32[]{:S(2)}) collective-permute-start(bf16[256,2048]{1,0:T(8,128)(2,1)} %convolution_convert_fusion.14), channel_id=1, source_target_pairs={{0,4},{4,0},{8,12},{12,8},{16,20},{20,16},{24,28},{28,24},{1,5},{5... | collective-permute-start | bytes 3145736 | tf_op jit(solution)/shard_map/ppermute | solution.py:31
  449.4 44.2 %collective-permute-start.44 = (bf16[256,2048]{1,0:T(8,128)(2,1)}, bf16[256,2048]{1,0:T(8,128)(2,1)S(1)}, u32[]{:S(2)}, u32[]{:S(2)}) collective-permute-start(bf16[256,2048]{1,0:T(8,128)(2,1)} %get-tuple-element.55), channel_id=1, source_target_pairs={{0,1},{1,2},{2,3},{3,0},{4,5},{5,6},{6,7},{7,4},{8,9},{9,10},{10,1... | collective-permute-start | bytes 3145736 | tf_op jit(solution)/shard_map/ppermute | solution.py:36
  489.8 29.2 %collective-permute-start.91 = (bf16[256,2048]{1,0:T(8,128)(2,1)S(1)}, bf16[256,2048]{1,0:T(8,128)(2,1)S(1)}, u32[]{:S(2)}, u32[]{:S(2)}) collective-permute-start(bf16[256,2048]{1,0:T(8,128)(2,1)S(1)} %pad_maximum_fusion.15), channel_id=1, source_target_pairs={{0,8},{4,12},{8,0},{12,4},{16,24},{20,28},{24,16},{28,20},{1,9},{5... | collective-permute-start | bytes 3145736 | tf_op jit(solution)/shard_map/ppermute | solution.py:31
  493.6 58.7 %collective-permute-start.96 = (bf16[2048,256]{1,0:T(8,128)(2,1)S(1)}, bf16[2048,256]{1,0:T(8,128)(2,1)S(1)}, u32[]{:S(2)}, u32[]{:S(2)}) collective-permute-start(bf16[2048,256]{1,0:T(8,128)(2,1)S(1)} %copy-done.147), channel_id=1, source_target_pairs={{0,4},{4,0},{8,12},{12,8},{16,20},{20,16},{24,28},{28,24},{1,5},{5... | collective-permute-start | bytes 3145736 | tf_op jit(solution)/shard_map/ppermute | solution.py:31
  493.6 58.7 %collective-permute-start.103 = (bf16[2048,256]{1,0:T(8,128)(2,1)S(1)}, bf16[2048,256]{1,0:T(8,128)(2,1)S(1)}, u32[]{:S(2)}, u32[]{:S(2)}) collective-permute-start(bf16[2048,256]{1,0:T(8,128)(2,1)S(1)} %pad_maximum_fusion.18), channel_id=1, source_target_pairs={{0,16},{4,20},{8,24},{12,28},{16,0},{20,4},{24,8},{28,12},{1,17},{... | collective-permute-start | bytes 3145736 | tf_op jit(solution)/shard_map/ppermute | solution.py:31
  493.6 58.6 %collective-permute-start.100 = (bf16[2048,256]{1,0:T(8,128)(2,1)S(1)}, bf16[2048,256]{1,0:T(8,128)(2,1)S(1)}, u32[]{:S(2)}, u32[]{:S(2)}) collective-permute-start(bf16[2048,256]{1,0:T(8,128)(2,1)S(1)} %pad_maximum_fusion.17), channel_id=1, source_target_pairs={{0,8},{4,12},{8,0},{12,4},{16,24},{20,28},{24,16},{28,20},{1,9},{5... | collective-permute-start | bytes 3145736 | tf_op jit(solution)/shard_map/ppermute | solution.py:31
  514.9 28.0 %collective-permute-start.45 = (bf16[256,2048]{1,0:T(8,128)(2,1)S(1)}, bf16[256,2048]{1,0:T(8,128)(2,1)S(1)}, u32[]{:S(2)}, u32[]{:S(2)}) collective-permute-start(bf16[256,2048]{1,0:T(8,128)(2,1)S(1)} %collective-permute-done.44), channel_id=1, source_target_pairs={{0,1},{1,2},{2,3},{3,0},{4,5},{5,6},{6,7},{7,4},{8,9},{9,10},{10,1... | collective-permute-start | bytes 3145736 | tf_op jit(solution)/shard_map/ppermute | solution.py:36
  521.3 70.1 %collective-permute-start.95 = (bf16[256,1024]{1,0:T(8,128)(2,1)S(1)}, bf16[256,1024]{1,0:T(8,128)(2,1)S(1)}, u32[]{:S(2)}, u32[]{:S(2)}) collective-permute-start(bf16[256,1024]{1,0:T(8,128)(2,1)S(1)} %slice.1224), channel_id=1, source_target_pairs={{0,2},{1,3},{2,0},{3,1},{4,6},{5,7},{6,4},{7,5},{8,10},{9,11},{10,... | collective-permute-start | bytes 1572872 | tf_op jit(solution)/shard_map/ppermute | solution.py:31
  542.9 60.7 %collective-permute-start.46 = (bf16[256,2048]{1,0:T(8,128)(2,1)S(1)}, bf16[256,2048]{1,0:T(8,128)(2,1)S(1)}, u32[]{:S(2)}, u32[]{:S(2)}) collective-permute-start(bf16[256,2048]{1,0:T(8,128)(2,1)S(1)} %collective-permute-done.45), channel_id=1, source_target_pairs={{0,1},{1,2},{2,3},{3,0},{4,5},{5,6},{6,7},{7,4},{8,9},{9,10},{10,1... | collective-permute-start | bytes 3145736 | tf_op jit(solution)/shard_map/ppermute | solution.py:36
  554.0 48.5 %collective-permute-start.104 = (bf16[1024,256]{1,0:T(8,128)(2,1)S(1)}, bf16[1024,256]{1,0:T(8,128)(2,1)S(1)}, u32[]{:S(2)}, u32[]{:S(2)}) collective-permute-start(bf16[1024,256]{1,0:T(8,128)(2,1)S(1)} %slice.1221), channel_id=1, source_target_pairs={{0,2},{1,3},{2,0},{3,1},{4,6},{5,7},{6,4},{7,5},{8,10},{9,11},{10,... | collective-permute-start | bytes 1572872 | tf_op jit(solution)/shard_map/ppermute | solution.py:31
  625.9 59.2 %collective-permute-start.74 = (bf16[1024,256]{1,0:T(8,128)(2,1)}, bf16[1024,256]{1,0:T(8,128)(2,1)S(1)}, u32[]{:S(2)}, u32[]{:S(2)}) collective-permute-start(bf16[1024,256]{1,0:T(8,128)(2,1)} %convolution_convert_fusion.35), channel_id=1, source_target_pairs={{0,4},{4,0},{8,12},{12,8},{16,20},{20,16},{24,28},{28,24},{1,5},{5... | collective-permute-start | bytes 1572872 | tf_op jit(solution)/shard_map/ppermute | solution.py:31
  739.7 41.1 %collective-permute-start.60 = (bf16[256,2048]{1,0:T(8,128)(2,1)}, bf16[256,2048]{1,0:T(8,128)(2,1)}, u32[]{:S(2)}, u32[]{:S(2)}) collective-permute-start(bf16[256,2048]{1,0:T(8,128)(2,1)} %convolution_convert_fusion.16), channel_id=1, source_target_pairs={{0,4},{4,0},{8,12},{12,8},{16,20},{20,16},{24,28},{28,24},{1,5},{5... | collective-permute-start | bytes 3145736 | tf_op jit(solution)/shard_map/ppermute | solution.py:31
  739.7 36.4 %collective-permute-start.57 = (bf16[256,2048]{1,0:T(8,128)(2,1)}, bf16[256,2048]{1,0:T(8,128)(2,1)S(1)}, u32[]{:S(2)}, u32[]{:S(2)}) collective-permute-start(bf16[256,2048]{1,0:T(8,128)(2,1)} %convolution_convert_fusion.18), channel_id=1, source_target_pairs={{0,4},{4,0},{8,12},{12,8},{16,20},{20,16},{24,28},{28,24},{1,5},{5... | collective-permute-start | bytes 3145736 | tf_op jit(solution)/shard_map/ppermute | solution.py:31
  745.4 38.7 %collective-permute-start.56 = (bf16[256,2048]{1,0:T(8,128)(2,1)}, bf16[256,2048]{1,0:T(8,128)(2,1)}, u32[]{:S(2)}, u32[]{:S(2)}) collective-permute-start(bf16[256,2048]{1,0:T(8,128)(2,1)} %convolution_convert_fusion.20), channel_id=1, source_target_pairs={{0,4},{4,0},{8,12},{12,8},{16,20},{20,16},{24,28},{28,24},{1,5},{5... | collective-permute-start | bytes 3145736 | tf_op jit(solution)/shard_map/ppermute | solution.py:31
  764.7 69.8 %collective-permute-start.55 = (bf16[256,2048]{1,0:T(8,128)(2,1)}, bf16[256,2048]{1,0:T(8,128)(2,1)}, u32[]{:S(2)}, u32[]{:S(2)}) collective-permute-start(bf16[256,2048]{1,0:T(8,128)(2,1)} %convolution_convert_fusion.22), channel_id=1, source_target_pairs={{0,4},{4,0},{8,12},{12,8},{16,20},{20,16},{24,28},{28,24},{1,5},{5... | collective-permute-start | bytes 3145736 | tf_op jit(solution)/shard_map/ppermute | solution.py:31
  765.6 39.7 %collective-permute-start.63 = (bf16[256,1024]{1,0:T(8,128)(2,1)}, bf16[256,1024]{1,0:T(8,128)(2,1)}, u32[]{:S(2)}, u32[]{:S(2)}) collective-permute-start(bf16[256,1024]{1,0:T(8,128)(2,1)} %convolution_convert_fusion.43), channel_id=1, source_target_pairs={{0,4},{4,0},{8,12},{12,8},{16,20},{20,16},{24,28},{28,24},{1,5},{5... | collective-permute-start | bytes 1572872 | tf_op jit(solution)/shard_map/ppermute | solution.py:31
  777.1 54.1 %collective-permute-start.70 = (bf16[256,1024]{1,0:T(8,128)(2,1)S(1)}, bf16[256,1024]{1,0:T(8,128)(2,1)}, u32[]{:S(2)}, u32[]{:S(2)}) collective-permute-start(bf16[256,1024]{1,0:T(8,128)(2,1)S(1)} %pad_maximum_fusion.27), channel_id=1, source_target_pairs={{0,16},{4,20},{8,24},{12,28},{16,0},{20,4},{24,8},{28,12},{1,17},{... | collective-permute-start | bytes 1572872 | tf_op jit(solution)/shard_map/ppermute | solution.py:31
  802.1 29.2 %collective-permute-start.67 = (bf16[256,1024]{1,0:T(8,128)(2,1)}, bf16[256,1024]{1,0:T(8,128)(2,1)}, u32[]{:S(2)}, u32[]{:S(2)}) collective-permute-start(bf16[256,1024]{1,0:T(8,128)(2,1)} %pad_maximum_fusion.26), channel_id=1, source_target_pairs={{0,8},{4,12},{8,0},{12,4},{16,24},{20,28},{24,16},{28,20},{1,9},{5... | collective-permute-start | bytes 1572872 | tf_op jit(solution)/shard_map/ppermute | solution.py:31
  805.3 29.2 %collective-permute-start.62 = (bf16[256,2048]{1,0:T(8,128)(2,1)}, bf16[256,2048]{1,0:T(8,128)(2,1)}, u32[]{:S(2)}, u32[]{:S(2)}) collective-permute-start(bf16[256,2048]{1,0:T(8,128)(2,1)} %pad_maximum_fusion.14), channel_id=1, source_target_pairs={{0,16},{4,20},{8,24},{12,28},{16,0},{20,4},{24,8},{28,12},{1,17},{... | collective-permute-start | bytes 3145736 | tf_op jit(solution)/shard_map/ppermute | solution.py:31
  (215 other events, 4091.1 us)
Sparse Core Ops, SparseCore 0:
  131.9 43.5 all-gather.4
  626.0 39.1 all-gather.6

commit v2 on v1

--- a/solution.py
+++ b/solution.py
@@ -1,6 +1,8 @@
 import jax
 import jax.numpy as jnp
 from jax import lax
+from jax.experimental import pallas as pl
+from jax.experimental.pallas import tpu as pltpu
 from jax.sharding import PartitionSpec as P
 
 KEY = 256
@@ -127,6 +129,610 @@
         vector = vector + swap(vector, axis, bit)
         bit *= 2
     return vector
+
+
+MESH = pl.DeviceIdType.MESH
+ANY = pl.BlockSpec(memory_space=pl.ANY)
+VMEM = pl.BlockSpec(memory_space=pltpu.VMEM)
+LIMIT = 60 * 1024 * 1024
+
+
+def flipped(index, bit):
+    return index + bit - 2 * bit * lax.rem(lax.div(index, bit), 2)
+
+
+def peers():
+    tok = lax.axis_index("tok")
+    z = lax.axis_index("head")
+    count = lax.axis_size("head")
+    return {
+        "core": {"tok": flipped(tok, 1), "head": z},
+        "x": {"tok": flipped(tok, 2), "head": z},
+        "y": {"tok": flipped(tok, 4), "head": z},
+        "up": {"tok": tok, "head": lax.rem(z + 1, count)},
+        "down": {"tok": tok, "head": lax.rem(z + count - 1, count)},
+        "pair": {"tok": tok, "head": flipped(z, 1)},
+        "cross": {"tok": tok, "head": flipped(z, 2)},
+    }
+
+
+def greet(*devices):
+    barrier = pltpu.get_barrier_semaphore()
+    for device in devices:
+        pl.semaphore_signal(barrier, inc=1, device_id=device, device_id_type=MESH)
+    pl.semaphore_wait(barrier, len(devices))
+
+
+class Moves:
+    def __init__(self, send, recv):
+        self.send, self.recv, self.made, self.over = send, recv, [], []
+
+    def go(self, src, dst, device):
+        n = len(self.made)
+        copy = pltpu.make_async_remote_copy(
+            src_ref=src,
+            dst_ref=dst,
+            send_sem=self.send.at[n],
+            recv_sem=self.recv.at[n],
+            device_id=device,
+            device_id_type=MESH,
+        )
+        copy.start()
+        self.made.append(copy)
+        return copy
+
+    def sent(self, copy):
+        copy.wait_send()
+        self.over.append(copy)
+
+    def finish(self):
+        for copy in self.made:
+            if not any(copy is gone for gone in self.over):
+                copy.wait_send()
+
+
+class Gather:
+    def __init__(self, moves, near, view):
+        self.moves, self.near, self.view = moves, near, view
+
+    def first(self):
+        go, near, view = self.moves.go, self.near, self.view
+        self.x = go(view(0), view(2), near["x"])
+        self.y = go(view(0), view(4), near["y"])
+        self.cores = [go(view(0), view(1), near["core"])]
+
+    def second(self):
+        go, near, view = self.moves.go, self.near, self.view
+        self.x.wait_recv()
+        self.far = [go(view(2, 0), view(6, 0), near["y"])]
+        self.cores.append(go(view(2), view(3), near["core"]))
+        self.y.wait_recv()
+        self.far.append(go(view(4, 1), view(6, 1), near["x"]))
+        self.cores.append(go(view(4), view(5), near["core"]))
+
+    def third(self):
+        go, near, view = self.moves.go, self.near, self.view
+        for copy in self.far:
+            copy.wait_recv()
+        self.cores.append(go(view(6), view(7), near["core"]))
+
+    def done(self):
+        for copy in self.cores:
+            copy.wait_recv()
+
+
+def enter_kernel(
+    tok_ref,
+    gain_ref,
+    cos_ref,
+    sin_ref,
+    wq_ref,
+    wk_ref,
+    wv_ref,
+    wg_ref,
+    wo_ref,
+    turned_out,
+    weights_out,
+    out_full,
+    qk_out,
+    v_out,
+    gate_out,
+    turned,
+    group,
+    weights,
+    send,
+    recv,
+    own_sem,
+    keep_sem,
+):
+    near = peers()
+    tok = lax.axis_index("tok")
+    z = lax.axis_index("head")
+    count = lax.axis_size("head")
+    rows, width = tok_ref.shape
+    part = width // 8
+    cols = weights.shape[2]
+    half = wq_ref.shape[1]
+
+    own = [
+        pltpu.make_async_copy(wq_ref, weights.at[0, pl.ds(0, part), pl.ds(0, half)], own_sem.at[0]),
+        pltpu.make_async_copy(
+            wk_ref, weights.at[0, pl.ds(0, part), pl.ds(half, half)], own_sem.at[1]
+        ),
+        pltpu.make_async_copy(wv_ref, weights.at[1, pl.ds(0, part), :], own_sem.at[2]),
+        pltpu.make_async_copy(wg_ref, weights.at[2, pl.ds(0, part), :], own_sem.at[3]),
+        pltpu.make_async_copy(wo_ref, out_full.at[:, pl.ds(0, part)], own_sem.at[4]),
+    ]
+    for copy in own:
+        copy.start()
+    greet(near["core"], near["x"], near["y"], near["up"], near["down"])
+    moves = Moves(send, recv)
+
+    def chunk_view(c):
+        def view(r, side=None):
+            if side is None:
+                return weights.at[c, pl.ds(r * part, part), :]
+            return weights.at[c, pl.ds(r * part + side * (part // 2), part // 2), :]
+
+        return view
+
+    def out_view(r, side=None):
+        if side is None:
+            return out_full.at[:, pl.ds(r * part, part)]
+        size = out_full.shape[0] // 2
+        return out_full.at[pl.ds(side * size, size), pl.ds(r * part, part)]
+
+    chunks = [Gather(moves, near, chunk_view(c)) for c in range(3)]
+    outward = Gather(moves, near, out_view)
+    own[0].wait()
+    own[1].wait()
+    chunks[0].first()
+    own[2].wait()
+    chunks[1].first()
+    own[3].wait()
+    own[4].wait()
+
+    @pl.loop(0, rows // 32)
+    def _(i):
+        at = pl.ds(pl.multiple_of(i * 32, 32), 32)
+        values = jnp.concatenate(
+            [
+                tok_ref[at, pl.ds(pl.multiple_of(place * part, part), part)]
+                for place in xor_places(tok)
+            ],
+            axis=1,
+        ).astype(F32)
+        mean = jnp.mean(values, axis=-1, keepdims=True)
+        centred = values - mean
+        inverse = lax.rsqrt(jnp.mean(centred * centred, axis=-1, keepdims=True) + EPS)
+        lifted = (centred * inverse * gain_ref[...]).astype(BF)
+        group[pl.ds(pl.multiple_of(z * rows + i * 32, 32), 32), :] = lifted
+
+    def shard(step, side):
+        owner = lax.rem(z - step + count, count)
+        size = rows // 2
+        return group.at[pl.ds(pl.multiple_of(owner * rows + side * size, size), size), :]
+
+    ring = {}
+
+    def pass_on(step, side):
+        if step:
+            ring[step - 1, side].wait_recv()
+        if step < count - 1:
+            ring[step, side] = moves.go(shard(step, side), shard(step, side), near["up"])
+
+    def project(c, steps):
+        first, number = steps
+
+        @pl.loop(0, number * (cols // 256))
+        def _(i):
+            step = first + lax.div(i, cols // 256)
+            tile = lax.rem(i, cols // 256)
+            owner = lax.rem(z - step + count, count)
+            at = pl.ds(pl.multiple_of(owner * rows, rows), rows)
+            to = pl.ds(pl.multiple_of(tile * 256, 256), 256)
+            found = jnp.dot(group[at, :], weights[c, :, to], preferred_element_type=F32)
+            if c == 0:
+                cosine, sine = cos_ref[at, :], sin_ref[at, :]
+                one, two = found[:, :128], found[:, 128:]
+                qk_out[at, to] = jnp.concatenate(
+                    [one * cosine - two * sine, one * sine + two * cosine], axis=1
+                ).astype(BF)
+            elif c == 1:
+                v_out[at, to] = found.astype(BF)
+            else:
+                gate_out[at, to] = found.astype(BF)
+
+    def turn(step):
+        owner = lax.rem(z - step + count, count)
+
+        @pl.loop(0, width // 256)
+        def _(i):
+            at = pl.ds(pl.multiple_of(i * 256, 256), 256)
+            to = pl.ds(pl.multiple_of(owner * rows, rows), rows)
+            turned[at, to] = group[to, at].T
+
+    kept = []
+
+    def keep(c):
+        copy = pltpu.make_async_copy(
+            weights.at[c], weights_out.at[:, pl.ds(c * cols, cols)], keep_sem.at[c]
+        )
+        copy.start()
+        kept.append(copy)
+
+    pass_on(0, 0)
+    pass_on(0, 1)
+    chunks[0].second()
+    chunks[2].first()
+    pass_on(1, 0)
+    chunks[1].second()
+    outward.first()
+    pass_on(1, 1)
+    chunks[0].third()
+    chunks[0].done()
+    keep(0)
+    project(0, (0, 2))
+    pass_on(2, 0)
+    turn(0)
+    turn(1)
+    chunks[2].second()
+    pass_on(2, 1)
+    chunks[1].third()
+    chunks[1].done()
+    keep(1)
+    project(1, (0, 2))
+    outward.second()
+    project(0, (2, 1))
+    project(1, (2, 1))
+    turn(2)
+    chunks[2].third()
+    chunks[2].done()
+    keep(2)
+    pass_on(3, 0)
+    outward.third()
+    project(2, (0, 3))
+    pass_on(3, 1)
+    turn(3)
+    copy = pltpu.make_async_copy(turned, turned_out, keep_sem.at[3])
+    copy.start()
+    kept.append(copy)
+    project(0, (3, 1))
+    project(1, (3, 1))
+    project(2, (3, 1))
+    outward.done()
+    for copy in kept:
+        copy.wait()
+    moves.finish()
+
+
+def xor_places(tok):
+    places = []
+    for r in range(8):
+        place = tok
+        for bit in (1, 2, 4):
+            if r & bit:
+                place = flipped(place, bit)
+        places.append(place)
+    return places
+
+
+def enter(tokens, gain, cosine, sine, w_query, w_key, w_value, w_gate, w_out):
+    rows, width = tokens.shape
+    group_rows = rows * lax.axis_size("head")
+    cols = w_value.shape[1]
+    moves = 4 * 8 + 6
+    return pl.pallas_call(
+        enter_kernel,
+        out_shape=(
+            jax.ShapeDtypeStruct((width, group_rows), BF),
+            jax.ShapeDtypeStruct((width, 3 * cols), BF),
+            jax.ShapeDtypeStruct((w_out.shape[0], width), BF),
+            jax.ShapeDtypeStruct((group_rows, cols), BF),
+            jax.ShapeDtypeStruct((group_rows, cols), BF),
+            jax.ShapeDtypeStruct((group_rows, cols), BF),
+        ),
+        in_specs=[VMEM] * 4 + [ANY] * 5,
+        out_specs=[ANY] * 3 + [VMEM] * 3,
+        scratch_shapes=[
+            pltpu.VMEM((width, group_rows), BF),
+            pltpu.VMEM((group_rows, width), BF),
+            pltpu.VMEM((3, width, cols), BF),
+            pltpu.SemaphoreType.DMA((moves,)),
+            pltpu.SemaphoreType.DMA((moves,)),
+            pltpu.SemaphoreType.DMA((5,)),
+            pltpu.SemaphoreType.DMA((4,)),
+        ],
+        compiler_params=pltpu.CompilerParams(
+            collective_id=0, has_side_effects=True, vmem_limit_bytes=LIMIT
+        ),
+        cost_estimate=pl.CostEstimate(
+            flops=2 * group_rows * width * 3 * cols, bytes_accessed=40 << 20, transcendentals=0
+        ),
+    )(tokens, gain[None, :], cosine, sine, w_query, w_key, w_value, w_gate, w_out)
+
+
+class Scatter:
+    def __init__(self, moves, near, term, buffers, result):
+        self.moves, self.near, self.term, self.result = moves, near, term, result
+        self.odd_out, self.odd_in, self.far_out, self.far_in, self.near_out, self.near_in = buffers
+        self.half = self.far_out.shape[0] // 2
+
+    def odd(self, i):
+        self.odd_out[i] = self.term(2 * i + 1).astype(BF)
+        move = self.moves.go(self.odd_out.at[i], self.odd_in.at[i], self.near["core"])
+        if i == 3:
+            self.cores = {}
+        self.cores[i] = move
+
+    def folded(self, i):
+        self.cores[i].wait_recv()
+        return self.term(2 * i) + self.odd_in[i].astype(F32)
+
+    def far(self):
+        self.far_out[...] = self.folded(3).astype(BF)
+        self.fars = [
+            self.moves.go(
+                self.far_out.at[pl.ds(side * self.half, self.half), :],
+                self.far_in.at[side],
+                self.near[way],
+            )
+            for side, way in ((0, "x"), (1, "y"))
+        ]
+
+    def close(self):
+        half = self.half
+        self.nears = []
+        for i, side, way in ((1, 1, "x"), (2, 0, "y")):
+            value = self.folded(i)
+            self.fars[side].wait_recv()
+            helped = value[side * half : (side + 1) * half] + self.far_in[side].astype(F32)
+            other = value[(1 - side) * half : (2 - side) * half]
+            self.near_out[i - 1, pl.ds(side * half, half), :] = helped.astype(BF)
+            self.near_out[i - 1, pl.ds((1 - side) * half, half), :] = other.astype(BF)
+            self.nears.append(
+                self.moves.go(self.near_out.at[i - 1], self.near_in.at[i - 1], self.near[way])
+            )
+
+    def done(self):
+        value = self.folded(0)
+        for i in range(2):
+            self.nears[i].wait_recv()
+            value = value + self.near_in[i].astype(F32)
+        self.result(value)
+
+
+def leave_kernel(
+    grads_ref,
+    weights_ref,
+    turned_ref,
+    tok_ref,
+    resid_ref,
+    gain_ref,
+    sums_ref,
+    tokens_grad,
+    wq_out,
+    wk_out,
+    wv_out,
+    gains_out,
+    grads,
+    weights,
+    turned,
+    ring_out,
+    ring_in,
+    held,
+    odd_out,
+    odd_in,
+    far_out,
+    far_in,
+    near_out,
+    near_in,
+    gains,
+    gains_in,
+    gains_z,
+    send,
+    recv,
+    load_sem,
+):
+    near = peers()
+    tok = lax.axis_index("tok")
+    z = lax.axis_index("head")
+    count = lax.axis_size("head")
+    rows, width = tok_ref.shape
+    part = width // 8
+    side_rows = rows // 2
+    cols = wv_out.shape[1]
+    loads = [
+        pltpu.make_async_copy(grads_ref, grads, load_sem.at[0]),
+        pltpu.make_async_copy(weights_ref, weights, load_sem.at[1]),
+        pltpu.make_async_copy(turned_ref, turned, load_sem.at[2]),
+    ]
+    for load in loads:
+        load.start()
+    others = [
+        {"tok": tok, "head": lax.rem(z + step, count)} for step in range(1, count)
+    ]
+    greet(near["core"], near["x"], near["y"], *others)
+    moves = Moves(send, recv)
+
+    def ring_term(step):
+        owner = lax.rem(z + 2 * count - 1 - step, count)
+        at = pl.ds(pl.multiple_of(owner * rows, rows), rows)
+
+        @pl.loop(0, width // 256)
+        def _(i):
+            to = pl.ds(pl.multiple_of(i * 256, 256), 256)
+            held[:, to] = lax.dot_general(
+                grads[at, :], weights[to, :], (((1,), (1,)), ((), ())), preferred_element_type=F32
+            )
+
+    ring = {}
+
+    def ring_send(step, side):
+        at = pl.ds(side * side_rows, side_rows)
+        value = held[at, :]
+        if step:
+            ring[step - 1, side].wait_recv()
+            value = value + ring_in[step - 1, at, :].astype(F32)
+        ring_out[step, at, :] = value.astype(BF)
+        ring[step, side] = moves.go(
+            ring_out.at[step, at, :], ring_in.at[step, at, :], near["up"]
+        )
+
+    def chunk_term(c):
+        def term(r):
+            left = turned[pl.ds(r * part, part), :]
+            return jnp.concatenate(
+                [
+                    jnp.dot(
+                        left,
+                        grads[:, c * cols + j * 256 : c * cols + (j + 1) * 256],
+                        preferred_element_type=F32,
+                    )
+                    for j in range(cols // 256)
+                ],
+                axis=1,
+            )
+
+        return term
+
+    def qk_result(value):
+        wq_out[...] = value[:, : cols // 2]
+        wk_out[...] = value[:, cols // 2 :]
+
+    def v_result(value):
+        wv_out[...] = value
+
+    def buffers(c):
+        return (
+            odd_out.at[c], odd_in.at[c], far_out.at[c], far_in.at[c], near_out.at[c], near_in.at[c]
+        )
+
+    scatters = [
+        Scatter(moves, near, chunk_term(c), buffers(c), result)
+        for c, result in enumerate((qk_result, v_result))
+    ]
+
+    loads[0].wait()
+    loads[1].wait()
+    ring_term(0)
+    ring_send(0, 0)
+    ring_send(0, 1)
+    loads[2].wait()
+    for i in (3, 1, 2, 0):
+        scatters[0].odd(i)
+    ring_term(1)
+    ring_send(1, 0)
+    scatters[0].far()
+    for i in (3, 1):
+        scatters[1].odd(i)
+    ring_send(1, 1)
+    scatters[0].close()
+    ring_term(2)
+    for i in (2, 0):
+        scatters[1].odd(i)
+    ring_send(2, 0)
+    scatters[1].far()
+    ring_send(2, 1)
+    scatters[1].close()
+    scatters[0].done()
+    ring_term(3)
+    scatters[1].done()
+
+    gains[...] = sums_ref[...]
+    size = 32
+    for side in range(2):
+        ring[2, side].wait_recv()
+
+        def block(i, total):
+            at = pl.ds(pl.multiple_of(side * side_rows + i * size, size), size)
+            values = jnp.concatenate(
+                [
+                    tok_ref[at, pl.ds(pl.multiple_of(place * part, part), part)]
+                    for place in xor_places(tok)
+                ],
+                axis=1,
+            ).astype(F32)
+            mean = jnp.mean(values, axis=-1, keepdims=True)
+            centred = values - mean
+            inverse = lax.rsqrt(jnp.mean(centred * centred, axis=-1, keepdims=True) + EPS)
+            unit = centred * inverse
+            grad = held[at, :] + ring_in[2, at, :].astype(F32)
+            scaled = grad * gain_ref[...]
+            first = jnp.mean(scaled, axis=-1, keepdims=True)
+            second = jnp.mean(scaled * unit, axis=-1, keepdims=True)
+            found = resid_ref[at, :] + inverse * (scaled - first - unit * second)
+            for r, place in enumerate(xor_places(tok)):
+                tokens_grad[at, pl.ds(pl.multiple_of(place * part, part), part)] = found[
+                    :, r * part : (r + 1) * part
+                ]
+            return total + jnp.sum(grad * unit, axis=0, keepdims=True)
+
+        total = lax.fori_loop(
+            0, side_rows // size, block, jnp.zeros((1, width), F32)
+        )
+        for r, place in enumerate(xor_places(tok)):
+            at = pl.ds(pl.multiple_of(place * part, part), part)
+            gains[pl.ds(0, 1), at] += total[:, r * part : (r + 1) * part]
+
+    for i, way in enumerate(("core", "x", "y")):
+        move = moves.go(gains, gains_in.at[i], near[way])
+        move.wait_recv()
+        moves.sent(move)
+        gains[...] += gains_in[i]
+    last = [moves.go(gains, gains_z.at[i], others[i]) for i in range(count - 1)]
+    total = gains[...]
+    gains_out[...] = total
+    for i, move in enumerate(last):
+        move.wait_recv()
+        gains_out[pl.ds(0, 2), :] += gains_z[i, pl.ds(0, 2), :]
+    moves.finish()
+
+
+def depart(grads, weights, turned, tokens, resid_grad, gain, sums):
+    rows, width = tokens.shape
+    count = lax.axis_size("head")
+    cols = grads.shape[1] // 3
+    part = width // 8
+    moves = 6 + 2 * 8 + 3 + count - 1
+    return pl.pallas_call(
+        leave_kernel,
+        out_shape=(
+            jax.ShapeDtypeStruct((rows, width), F32),
+            jax.ShapeDtypeStruct((part, cols // 2), F32),
+            jax.ShapeDtypeStruct((part, cols // 2), F32),
+            jax.ShapeDtypeStruct((part, cols), F32),
+            jax.ShapeDtypeStruct(sums.shape, F32),
+        ),
+        in_specs=[ANY] * 3 + [VMEM] * 4,
+        out_specs=[VMEM] * 5,
+        scratch_shapes=[
+            pltpu.VMEM(grads.shape, BF),
+            pltpu.VMEM(weights.shape, BF),
+            pltpu.VMEM(turned.shape, BF),
+            pltpu.VMEM((3, rows, width), BF),
+            pltpu.VMEM((3, rows, width), BF),
+            pltpu.VMEM((rows, width), F32),
+            pltpu.VMEM((2, 4, part, cols), BF),
+            pltpu.VMEM((2, 4, part, cols), BF),
+            pltpu.VMEM((2, part, cols), BF),
+            pltpu.VMEM((2, 2, part // 2, cols), BF),
+            pltpu.VMEM((2, 2, part, cols), BF),
+            pltpu.VMEM((2, 2, part, cols), BF),
+            pltpu.VMEM(sums.shape, F32),
+            pltpu.VMEM((3,) + sums.shape, F32),
+            pltpu.VMEM((count - 1,) + sums.shape, F32),
+            pltpu.SemaphoreType.DMA((moves,)),
+            pltpu.SemaphoreType.DMA((moves,)),
+            pltpu.SemaphoreType.DMA((3,)),
+        ],
+        compiler_params=pltpu.CompilerParams(
+            collective_id=1, has_side_effects=True, vmem_limit_bytes=LIMIT
+        ),
+        cost_estimate=pl.CostEstimate(
+            flops=2 * grads.shape[0] * width * 5 * cols, bytes_accessed=40 << 20, transcendentals=0
+        ),
+    )(grads, weights, turned, tokens, resid_grad, gain[None, :], sums)
 
 
 def norm_forward(values, gain):
@@ -224,15 +830,8 @@
     gain1 = reorder(norm_gain)
     gain2 = reorder(ffn_gain)
     normed1, unit1, inverse1 = norm_forward(tokens_f, gain1)
-    group = head_gather(normed1.astype(BF))
-    qkvg_full = tok_gather(jnp.concatenate([w_query, w_key, w_value, w_gate], axis=1), 0)
     qk = w_query.shape[1]
     vg = w_value.shape[1]
-    query_full = qkvg_full[:, :qk]
-    key_full = qkvg_full[:, qk : 2 * qk]
-    value_full = qkvg_full[:, 2 * qk : 2 * qk + vg]
-    gate_full = qkvg_full[:, 2 * qk + vg :]
-    out_full = tok_gather(w_out, 1)
     up_two = jnp.concatenate([w_up, swap(w_up, "head", 2)], axis=1)
     down_two = jnp.concatenate([w_down, swap(w_down, "head", 2)], axis=0)
     up_full = tok_gather(up_two, 0)
@@ -250,10 +849,25 @@
     ranks = lax.dynamic_slice_in_dim(head_order, z * heads, heads)
     log_decay = jnp.log1p(-jnp.exp2(-(5.0 + ranks.astype(F32))))
 
-    query_proj = mm(group, query_full)
-    key_proj = mm(group, key_full)
-    value_proj = mm(group, value_full)
-    gate = mm(group, gate_full)
+    if paired():
+        turned, qkvg_full, out_full, qk_rows, v_rows, gate = enter(
+            tokens, gain1, cosine, sine, w_query, w_key, w_value, w_gate, w_out
+        )
+        gate = gate.astype(F32)
+    else:
+        group = head_gather(normed1.astype(BF))
+        qkvg_full = tok_gather(jnp.concatenate([w_query, w_key, w_value, w_gate], axis=1), 0)
+        out_full = tok_gather(w_out, 1)
+        projected = mm(group, qkvg_full)
+        qk_rows = jnp.concatenate(
+            [
+                rotate(projected[:, h * KEY : (h + 1) * KEY], cosine, sine).astype(BF)
+                for h in range(2 * heads)
+            ],
+            axis=1,
+        )
+        v_rows = projected[:, 2 * qk : 2 * qk + vg].astype(BF)
+        gate = projected[:, 2 * qk + vg :]
 
     def head_of(array, head, size):
         return array[:, head * size : (head + 1) * size]
@@ -263,9 +877,9 @@
 
     q, k, v, masks = [], [], [], []
     for h in range(heads):
-        q.append(rotate(head_of(query_proj, h, KEY), cosine, sine).astype(BF))
-        k.append(rotate(head_of(key_proj, h, KEY), cosine, sine).astype(BF))
-        v.append(head_of(value_proj, h, VAL).astype(BF))
+        q.append(head_of(qk_rows, h, KEY))
+        k.append(head_of(qk_rows, heads + h, KEY))
+        v.append(head_of(v_rows, h, VAL))
         masks.append(
             [
                 span_masks(
@@ -382,7 +996,12 @@
         ret_grad.append(back.astype(BF))
         group_gain_parts.append(gain_term)
     gate_grad = jnp.concatenate(gate_parts, axis=1)
-    w_gate_grad = tok_scatter([mm_tn(piece(group, r), gate_grad) for r in slots])
+    if paired():
+        w_gate_grad = tok_scatter(
+            [mm(turned[r * part : (r + 1) * part], gate_grad) for r in slots]
+        )
+    else:
+        w_gate_grad = tok_scatter([mm_tn(piece(group, r), gate_grad) for r in slots])
 
     pending_of, pending_terms = [], []
     for h in range(heads):
@@ -424,18 +1043,34 @@
         k_parts.append(unrotate(jnp.concatenate(kg, axis=0), cosine, sine).astype(BF))
         v_parts.append(jnp.concatenate(vg_, axis=0).astype(BF))
     all_grad = jnp.concatenate(q_parts + k_parts + v_parts + [gate_grad], axis=1)
-    row_grad = head_scatter(lambda i: mm_nt(rows_of(all_grad, i, rows), qkvg_full))
-    input_part, norm_gain_local = norm_backward(row_grad, unit1, inverse1, gain1)
-    tokens_grad = reorder(resid_grad + input_part)
-    qkv_grad = all_grad[:, : 2 * qk + vg]
-    w_qkv_grad = tok_scatter([mm_tn(piece(group, r), qkv_grad) for r in slots])
-    w_query_grad = w_qkv_grad[:, :qk]
-    w_key_grad = w_qkv_grad[:, qk : 2 * qk]
-    w_value_grad = w_qkv_grad[:, 2 * qk :]
-
-    group_gain_grad = sum_small(jnp.concatenate(group_gain_parts, axis=0), "tok")
-    ffn_sum = sum_small(sum_small(reorder(ffn_gain_local), "tok"), "head")
-    norm_sum = sum_small(sum_small(reorder(norm_gain_local), "tok"), "head")
+    group_terms = jnp.concatenate(group_gain_parts, axis=0)
+    ffn_terms = reorder(ffn_gain_local)
+    if paired():
+        sums = jnp.concatenate(
+            [
+                jnp.zeros((1, width), F32),
+                ffn_terms[None, :],
+                jnp.concatenate([group_terms, jnp.zeros((width - vg,), F32)])[None, :],
+                jnp.zeros((5, width), F32),
+            ],
+            axis=0,
+        )
+        tokens_grad, w_query_grad, w_key_grad, w_value_grad, sums = depart(
+            all_grad, qkvg_full, turned, tokens, resid_grad, gain1, sums
+        )
+        norm_sum, ffn_sum, group_gain_grad = sums[0], sums[1], sums[2, :vg]
+    else:
+        row_grad = head_scatter(lambda i: mm_nt(rows_of(all_grad, i, rows), qkvg_full))
+        input_part, norm_gain_local = norm_backward(row_grad, unit1, inverse1, gain1)
+        tokens_grad = reorder(resid_grad + input_part)
+        qkv_grad = all_grad[:, : 2 * qk + vg]
+        w_qkv_grad = tok_scatter([mm_tn(piece(group, r), qkv_grad) for r in slots])
+        w_query_grad = w_qkv_grad[:, :qk]
+        w_key_grad = w_qkv_grad[:, qk : 2 * qk]
+        w_value_grad = w_qkv_grad[:, 2 * qk :]
+        group_gain_grad = sum_small(group_terms, "tok")
+        ffn_sum = sum_small(sum_small(ffn_terms, "tok"), "head")
+        norm_sum = sum_small(sum_small(reorder(norm_gain_local), "tok"), "head")
     return (
         layer_out,
         tokens_grad,

time: 897 us -> 867 us (0.967)
  Pallas kernels: 0 us -> 204 us
  waiting for transfers between devices: 378 us -> 259 us
  matrix products: 225 us -> 158 us
  local copies, waits for them, and re-layouts: 123 us -> 84.3 us
  starting transfers between devices: 77.3 us -> 54.6 us
  other arithmetic: 65.3 us -> 78.2 us
    pallas_call x0 -> x2, Pallas kernels: none -> 204 us  [the longest x1 103 us: enter(): pl.pallas_call(enter_kernel, out_shape=(jax.ShapeDtypeStruct((width, grou...]
    ppermute x12 -> x6, waiting for transfers between devices: 143 us -> 80.9 us  [shift(): lax.ppermute(array, 'head', [(i, (i + 1) % count) for i in range(count)])]
    ppermute x93 -> x56, waiting for transfers between devices: 235 us -> 178 us  [swap(): return lax.ppermute(array, axis, [(i, i ^ bit) for i in range(count)])]
    dot_general x24 -> x20, matrix products: 86.1 us -> 47.6 us  [mm_nt(): lax.dot_general(left, right, (((1,), (1,)), ((), ())), preferred_element_...]
    unnamed x408 -> x311, local copies, waits for them, and re-layouts: 93.8 us -> 57.6 us
    dot_general x56 -> x40, matrix products: 80.3 us -> 57.4 us  [mm_tn(): lax.dot_general(left, right, (((0,), (0,)), ((), ())), preferred_element_...]
    ppermute x93 -> x56, starting transfers between devices: 60.8 us -> 46.7 us  [swap(): return lax.ppermute(array, axis, [(i, i ^ bit) for i in range(count)])]
    dot_general x27 -> x31, matrix products: 58.1 us -> 52.8 us  [mm(): return jnp.dot(left, right, preferred_element_type=F32)]
  transfers between devices with their start and end apart: 107 -> 64, of which waited for: 42 -> 23; matrix products, arithmetic and copies ran while one was open for 32% -> 25% of each run, Pallas kernels for 0% -> 12%
where the time goes in v2:
time: 867 us; the launch traced here: 859 us
  waiting for transfers between devices  259 us (30%)
  Pallas kernels  204 us (24%)
  matrix products  158 us (18%)
  local copies, waits for them, and re-layouts  84.3 us (10%)
  other arithmetic  78.2 us (9%)
  starting transfers between devices  54.6 us (6%)
  between operations  22.2 us (3%)
    ppermute x56, waiting for transfers between devices, swap(): return lax.ppermute(array, axis, [(i, i ^ bit) for i in range(count)])  178 us
    pallas_call x1, Pallas kernels, enter(): pl.pallas_call(enter_kernel, out_shape=(jax.ShapeDtypeStruct((width, grou...  103 us
    pallas_call x1, Pallas kernels, depart(): pl.pallas_call(leave_kernel, out_shape=(jax.ShapeDtypeStruct((rows, width...  100 us
    ppermute x6, waiting for transfers between devices, shift(): lax.ppermute(array, 'head', [(i, (i + 1) % count) for i in range(count)])  80.9 us
    unnamed x311, local copies, waits for them, and re-layouts  57.6 us
    dot_general x40, matrix products, mm_tn(): lax.dot_general(left, right, (((0,), (0,)), ((), ())), preferred_element_...  57.4 us
    dot_general x31, matrix products, mm(): return jnp.dot(left, right, preferred_element_type=F32)  52.8 us
    dot_general x20, matrix products, mm_nt(): lax.dot_general(left, right, (((1,), (1,)), ((), ())), preferred_element_...  47.6 us
  transfers between devices with their start and end apart: 64, of which 23 were waited for; matrix products, arithmetic and copies ran while one was open for 25% of the time, Pallas kernels for 12%

profile of v2, /device:TPU:0, one launch (start us, length us, event | category | flops | bytes accessed | tf_op | source)
XLA Modules:
  0.0 859.5 jit_solution(10377289734689596956)
XLA Ops:
  25.3 3.0 multiply_sine_fusion
  28.3 103.5 %shard_map.229 = (bf16[2048,1024]{1,0:T(8,128)(2,1)}, bf16[2048,3072]{1,0:T(8,128)(2,1)}, bf16[1024,2048]{1,0:T(8,128)(2,1)}, bf16[1024,1024]{1,0:T(8,128)(2,1)}...) custom-call(bf16[256,2048]{1,0:T(8,128)(2,1)} %tok_ref.3, f32[1,2048]{1,0:T(1,128)} %bitcast.91, ...), custom_call_target="tpu_custom_call" | custom-call | flops 12884901888 | bytes 41943040 | tf_op jit(solution)/shard_map/pallas_call | solution.py:425
  140.6 2.9 collective-permute-start.4
  160.1 15.1 %collective-permute-done.13 = bf16[1024,256]{1,0:T(8,128)(2,1)} collective-permute-done((bf16[1024,256]{1,0:T(8,128)(2,1)}, bf16[1024,256]{1,0:T(8,128)(2,1)}, u32[]{:S(2)}, u32[]{:S(2)}) %collective-permute-start.13) | collective-permute-done | bytes 524320 | tf_op jit(solution)/shard_map/ppermute | solution.py:33
  182.5 4.0 convert_element_type.526
  194.4 9.2 %collective-permute-done.15 = bf16[2048,256]{1,0:T(8,128)(2,1)} collective-permute-done((bf16[2048,256]{1,0:T(8,128)(2,1)}, bf16[2048,256]{1,0:T(8,128)(2,1)}, u32[]{:S(2)}, u32[]{:S(2)}) %collective-permute-start.15) | collective-permute-done | bytes 1048608 | tf_op jit(solution)/shard_map/ppermute | solution.py:33
  213.3 3.3 multiply_reduce_fusion.2
  238.5 2.8 collective-permute-done.19
  244.6 6.1 collective-permute-done.10
  251.3 6.4 collective-permute-done
  265.4 34.8 %collective-permute-done.1 = bf16[256,2048]{1,0:T(8,128)(2,1)S(1)} collective-permute-done((bf16[256,2048]{1,0:T(8,128)(2,1)S(1)}, bf16[256,2048]{1,0:T(8,128)(2,1)S(1)}, u32[]{:S(2)}, u32[]{:S(2)}) %collective-permute-start.1) | collective-permute-done | bytes 1048608 | tf_op jit(solution)/shard_map/ppermute | solution.py:38
  305.3 22.6 %collective-permute-done.2 = bf16[256,2048]{1,0:T(8,128)(2,1)S(1)} collective-permute-done((bf16[256,2048]{1,0:T(8,128)(2,1)S(1)}, bf16[256,2048]{1,0:T(8,128)(2,1)S(1)}, u32[]{:S(2)}, u32[]{:S(2)}) %collective-permute-start.2) | collective-permute-done | bytes 1048608 | tf_op jit(solution)/shard_map/ppermute | solution.py:38
  332.5 21.5 %collective-permute-done.3 = bf16[256,2048]{1,0:T(8,128)(2,1)S(1)} collective-permute-done((bf16[256,2048]{1,0:T(8,128)(2,1)S(1)}, bf16[256,2048]{1,0:T(8,128)(2,1)S(1)}, u32[]{:S(2)}, u32[]{:S(2)}) %collective-permute-start.3) | collective-permute-done | bytes 1048608 | tf_op jit(solution)/shard_map/ppermute | solution.py:33
  354.0 15.9 %fusion.2 = (bf16[512,2048]{1,0:T(8,128)(2,1)S(1)}, f32[512,2048]{1,0:T(8,128)}) fusion(bf16[2048,2048]{1,0:T(8,128)(2,1)S(1)} %constant_dynamic-update-slice_fusion.4, bf16[256,2048]{1,0:T(8,128)(2,1)S(1)} %collective-permute-done.3, bf16[256,2048]{1,0:T(8,128)(2,1)S(1)} %multiply_convert_fusion.2), kind=kOutput, calls=%fused_computation.38 | convolution fusion | flops 4367319040 | bytes 16777216 | tf_op jit(solution)/shard_map/dot_general | solution.py:20
  369.9 5.7 convolution_convert_fusion.18
  376.0 8.7 %fusion.8 = bf16[512,2048]{1,0:T(8,128)(2,1)S(1)} fusion(f32[512,2048]{1,0:T(8,128)} %get-tuple-element.117, bf16[2048,2048]{1,0:T(8,128)(2,1)} %constant_dynamic-update-slice_fusion.16, bf16[256,2048]{1,0:T(8,128)(2,1)S(1)} %collective-permute-done.23, bf16[256,2048]{1,0:T(8,128)(2,1)S(1)} %dynamic-slice_dynamic-update-slice_fusion), kind=kOutput, calls=%fused_computation.44 | convolution fusion | flops 4309647360 | bytes 16777216 | tf_op jit(solution)/shard_map/dot_general | solution.py:24
  384.7 6.7 convolution_convert_fusion.17
  406.2 5.8 fusion.39
  413.5 8.6 collective-permute-done.24
  423.1 7.0 multiply_reduce_fusion.6
  445.7 2.7 constant_dynamic-update-slice_fusion.53
  455.4 9.6 %collective-permute-done.50 = bf16[128,2048]{1,0:T(8,128)(2,1)S(1)} collective-permute-done((bf16[128,2048]{1,0:T(8,128)(2,1)S(1)}, bf16[128,2048]{1,0:T(8,128)(2,1)S(1)}, u32[]{:S(2)}, u32[]{:S(2)}) %collective-permute-start.50) | collective-permute-done | bytes 524320 | tf_op jit(solution)/shard_map/ppermute | solution.py:33
  467.9 9.8 %collective-permute-done.59 = bf16[1024,256]{1,0:T(8,128)(2,1)S(1)} collective-permute-done((bf16[1024,256]{1,0:T(8,128)(2,1)S(1)}, bf16[1024,256]{1,0:T(8,128)(2,1)S(1)}, u32[]{:S(2)}, u32[]{:S(2)}) %collective-permute-start.59) | collective-permute-done | bytes 524320 | tf_op jit(solution)/shard_map/ppermute | solution.py:33
  483.0 20.8 %collective-permute-done.51 = bf16[256,2048]{1,0:T(8,128)(2,1)S(1)} collective-permute-done((bf16[256,2048]{1,0:T(8,128)(2,1)S(1)}, bf16[256,2048]{1,0:T(8,128)(2,1)S(1)}, u32[]{:S(2)}, u32[]{:S(2)}) %collective-permute-start.51) | collective-permute-done | bytes 1048608 | tf_op jit(solution)/shard_map/ppermute | solution.py:33
  511.3 3.3 collective-permute-start.52
  514.7 17.2 %collective-permute-done.26 = bf16[256,2048]{1,0:T(8,128)(2,1)S(1)} collective-permute-done((bf16[256,2048]{1,0:T(8,128)(2,1)S(1)}, bf16[256,2048]{1,0:T(8,128)(2,1)S(1)}, u32[]{:S(2)}, u32[]{:S(2)}) %collective-permute-start.26) | collective-permute-done | bytes 1048608 | tf_op jit(solution)/shard_map/ppermute | solution.py:38
  531.8 5.5 collective-permute-start.27
  541.7 39.6 %collective-permute-done.52 = bf16[256,1024]{1,0:T(8,128)(2,1)S(1)} collective-permute-done((bf16[256,1024]{1,0:T(8,128)(2,1)S(1)}, bf16[256,1024]{1,0:T(8,128)(2,1)S(1)}, u32[]{:S(2)}, u32[]{:S(2)}) %collective-permute-start.52) | collective-permute-done | bytes 524320 | tf_op jit(solution)/shard_map/ppermute | solution.py:33
  582.4 10.0 %collective-permute-done.61 = bf16[1024,256]{1,0:T(8,128)(2,1)S(1)} collective-permute-done((bf16[1024,256]{1,0:T(8,128)(2,1)S(1)}, bf16[1024,256]{1,0:T(8,128)(2,1)S(1)}, u32[]{:S(2)}, u32[]{:S(2)}) %collective-permute-start.61) | collective-permute-done | bytes 524320 | tf_op jit(solution)/shard_map/ppermute | solution.py:33
  594.7 7.8 convolution_convert_fusion.19
  602.6 3.7 multiply_reduce_fusion.4
  612.6 2.8 convolution_convert_fusion.20
  631.8 3.1 fusion.252
  635.0 3.3 fusion.251
  646.0 3.2 fusion.250
  650.4 3.1 fusion.249
  657.3 2.7 collective-permute-start.42
  663.2 3.8 collective-permute-done.42
  670.7 10.2 %collective-permute-done.43 = bf16[1024,256]{1,0:T(8,128)(2,1)S(1)} collective-permute-done((bf16[1024,256]{1,0:T(8,128)(2,1)S(1)}, bf16[1024,256]{1,0:T(8,128)(2,1)S(1)}, u32[]{:S(2)}, u32[]{:S(2)}) %collective-permute-start.43) | collective-permute-done | bytes 524320 | tf_op jit(solution)/shard_map/ppermute | solution.py:33
  682.3 2.8 fusion.58
  685.1 3.4 multiply_reduce_fusion
  691.8 3.1 fusion.248
  694.9 3.1 fusion.247
  699.4 3.1 fusion.246
  702.5 3.1 fusion.245
  722.8 100.2 %shard_map.230 = (f32[256,2048]{1,0:T(8,128)}, f32[256,512]{1,0:T(8,128)}, f32[256,512]{1,0:T(8,128)}, f32[256,1024]{1,0:T(8,128)}, f32[8,2048]{1,0:T(8,128)}) custom-call(bf16[1024,3072]{1,0:T(8,128)(2,1)} %get-tuple-element.51.grads_ref, bf16[2048,3072]{1,0:T(8,128)(2,1)} %get-tuple-element.27.weights_ref, ...), custom_call_target="tpu_custom_call" | custom-call | flops 21474836480 | bytes 41943040 | tf_op jit(solution)/shard_map/pallas_call | solution.py:698
  835.0 2.6 collective-permute-done.31
  842.6 3.6 collective-permute-done.35
  (618 shorter events, 256.2 us)
Async XLA Ops:
  7.2 206.1 %all-gather.5.cloned.1.call-start = ((), (), s32[]{:S(2)}) async-start(), calls=%async_computation | async-start | bytes 4718592 | tf_op jit(solution)/shard_map/all_gather | solution.py:914
  140.2 544.9 %all-gather.7.cloned.1.call-start = ((), (), s32[]{:S(2)}) async-start(), calls=%async_computation.1 | async-start | bytes 4718592 | tf_op jit(solution)/shard_map/all_gather | solution.py:1017
  140.5 34.7 %collective-permute-start.13 = (bf16[1024,256]{1,0:T(8,128)(2,1)}, bf16[1024,256]{1,0:T(8,128)(2,1)}, u32[]{:S(2)}, u32[]{:S(2)}) collective-permute-start(bf16[1024,256]{1,0:T(8,128)(2,1)} %param.27), channel_id=1, source_target_pairs={{0,2},{1,3},{2,0},{3,1},{4,6},{5,7},{6,4},{7,5},{8,10},{9,11},{10,... | collective-permute-start | bytes 1572872 | tf_op jit(solution)/shard_map/ppermute | solution.py:33
  140.6 51.1 %collective-permute-start.4 = (bf16[256,1024]{1,0:T(8,128)(2,1)}, bf16[256,1024]{1,0:T(8,128)(2,1)}, u32[]{:S(2)}, u32[]{:S(2)}) collective-permute-start(bf16[256,1024]{1,0:T(8,128)(2,1)} %param.26), channel_id=1, source_target_pairs={{0,2},{1,3},{2,0},{3,1},{4,6},{5,7},{6,4},{7,5},{8,10},{9,11},{10,... | collective-permute-start | bytes 1572872 | tf_op jit(solution)/shard_map/ppermute | solution.py:33
  177.3 32.0 %collective-permute-start.14 = (bf16[2048,256]{1,0:T(8,128)(2,1)}, bf16[2048,256]{1,0:T(8,128)(2,1)}, u32[]{:S(2)}, u32[]{:S(2)}) collective-permute-start(bf16[2048,256]{1,0:T(8,128)(2,1)} %get-tuple-element.90), channel_id=1, source_target_pairs={{0,4},{4,0},{8,12},{12,8},{16,20},{20,16},{24,28},{28,24},{1,5},{5... | collective-permute-start | bytes 3145736 | tf_op jit(solution)/shard_map/ppermute | solution.py:33
  177.3 26.3 %collective-permute-start.15 = (bf16[2048,256]{1,0:T(8,128)(2,1)}, bf16[2048,256]{1,0:T(8,128)(2,1)}, u32[]{:S(2)}, u32[]{:S(2)}) collective-permute-start(bf16[2048,256]{1,0:T(8,128)(2,1)} %get-tuple-element.90), channel_id=1, source_target_pairs={{0,8},{4,12},{8,0},{12,4},{16,24},{20,28},{24,16},{28,20},{1,9},{5... | collective-permute-start | bytes 3145736 | tf_op jit(solution)/shard_map/ppermute | solution.py:33
  178.9 28.2 %collective-permute-start.17 = (bf16[2048,256]{1,0:T(8,128)(2,1)}, bf16[2048,256]{1,0:T(8,128)(2,1)}, u32[]{:S(2)}, u32[]{:S(2)}) collective-permute-start(bf16[2048,256]{1,0:T(8,128)(2,1)} %get-tuple-element.90), channel_id=1, source_target_pairs={{0,16},{4,20},{8,24},{12,28},{16,0},{20,4},{24,8},{28,12},{1,17},{... | collective-permute-start | bytes 3145736 | tf_op jit(solution)/shard_map/ppermute | solution.py:33
  193.8 42.7 %collective-permute-start.5 = (bf16[256,2048]{1,0:T(8,128)(2,1)}, bf16[256,2048]{1,0:T(8,128)(2,1)}, u32[]{:S(2)}, u32[]{:S(2)}) collective-permute-start(bf16[256,2048]{1,0:T(8,128)(2,1)} %get-tuple-element.86), channel_id=1, source_target_pairs={{0,4},{4,0},{8,12},{12,8},{16,20},{20,16},{24,28},{28,24},{1,5},{5... | collective-permute-start | bytes 3145736 | tf_op jit(solution)/shard_map/ppermute | solution.py:33
  193.9 35.7 %collective-permute-start.6 = (bf16[256,2048]{1,0:T(8,128)(2,1)}, bf16[256,2048]{1,0:T(8,128)(2,1)}, u32[]{:S(2)}, u32[]{:S(2)}) collective-permute-start(bf16[256,2048]{1,0:T(8,128)(2,1)} %get-tuple-element.86), channel_id=1, source_target_pairs={{0,8},{4,12},{8,0},{12,4},{16,24},{20,28},{24,16},{28,20},{1,9},{5... | collective-permute-start | bytes 3145736 | tf_op jit(solution)/shard_map/ppermute | solution.py:33
  203.6 30.2 %collective-permute-start.8 = (bf16[256,2048]{1,0:T(8,128)(2,1)}, bf16[256,2048]{1,0:T(8,128)(2,1)}, u32[]{:S(2)}, u32[]{:S(2)}) collective-permute-start(bf16[256,2048]{1,0:T(8,128)(2,1)} %get-tuple-element.86), channel_id=1, source_target_pairs={{0,16},{4,20},{8,24},{12,28},{16,0},{20,4},{24,8},{28,12},{1,17},{... | collective-permute-start | bytes 3145736 | tf_op jit(solution)/shard_map/ppermute | solution.py:33
  207.1 34.2 %collective-permute-start.19 = (bf16[1024,256]{1,0:T(8,128)(2,1)}, bf16[1024,256]{1,0:T(8,128)(2,1)}, u32[]{:S(2)}, u32[]{:S(2)}) collective-permute-start(bf16[1024,256]{1,0:T(8,128)(2,1)} %slice.531), channel_id=1, source_target_pairs={{0,16},{4,20},{8,24},{12,28},{16,0},{20,4},{24,8},{28,12},{1,17},{... | collective-permute-start | bytes 1572872 | tf_op jit(solution)/shard_map/ppermute | solution.py:33
  209.4 33.2 %collective-permute-start.20 = (bf16[1024,256]{1,0:T(8,128)(2,1)}, bf16[1024,256]{1,0:T(8,128)(2,1)}, u32[]{:S(2)}, u32[]{:S(2)}) collective-permute-start(bf16[1024,256]{1,0:T(8,128)(2,1)} %slice.532), channel_id=1, source_target_pairs={{0,8},{4,12},{8,0},{12,4},{16,24},{20,28},{24,16},{28,20},{1,9},{5... | collective-permute-start | bytes 1572872 | tf_op jit(solution)/shard_map/ppermute | solution.py:33
  229.5 28.2 %collective-permute-start = (bf16[256,2048]{1,0:T(8,128)(2,1)S(1)}, bf16[256,2048]{1,0:T(8,128)(2,1)S(1)}, u32[]{:S(2)}, u32[]{:S(2)}) collective-permute-start(bf16[256,2048]{1,0:T(8,128)(2,1)S(1)} %convolution_convert_fusion.16), channel_id=1, source_target_pairs={{0,1},{1,2},{2,3},{3,0},{4,5},{5,6},{6,7},{7,4},{8,9},{9,10},{10,1... | collective-permute-start | bytes 3145736 | tf_op jit(solution)/shard_map/ppermute | solution.py:38
  233.9 16.8 %collective-permute-start.10 = (bf16[128,2048]{1,0:T(8,128)(2,1)S(1)}, bf16[128,2048]{1,0:T(8,128)(2,1)S(1)}, u32[]{:S(2)}, u32[]{:S(2)}) collective-permute-start(bf16[128,2048]{1,0:T(8,128)(2,1)S(1)} %slice.528), channel_id=1, source_target_pairs={{0,16},{4,20},{8,24},{12,28},{16,0},{20,4},{24,8},{28,12},{1,17},{... | collective-permute-start | bytes 1572872 | tf_op jit(solution)/shard_map/ppermute | solution.py:33
  241.3 17.7 %collective-permute-start.16 = (bf16[2048,256]{1,0:T(8,128)(2,1)}, bf16[2048,256]{1,0:T(8,128)(2,1)S(1)}, u32[]{:S(2)}, u32[]{:S(2)}) collective-permute-start(bf16[2048,256]{1,0:T(8,128)(2,1)} %collective-permute-done.15), channel_id=1, source_target_pairs={{0,4},{4,0},{8,12},{12,8},{16,20},{20,16},{24,28},{28,24},{1,5},{5... | collective-permute-start | bytes 3145736 | tf_op jit(solution)/shard_map/ppermute | solution.py:33
  242.6 133.4 %collective-permute-start.23 = (bf16[256,2048]{1,0:T(8,128)(2,1)S(1)}, bf16[256,2048]{1,0:T(8,128)(2,1)S(1)}, u32[]{:S(2)}, u32[]{:S(2)}) collective-permute-start(bf16[256,2048]{1,0:T(8,128)(2,1)S(1)} %dynamic-slice_dynamic-update-slice_fusion), channel_id=1, source_target_pairs={{0,1},{1,0},{2,3},{3,2},{4,5},{5,4},{6,7},{7,6},{8,9},{9,8},{10,11... | collective-permute-start | bytes 3145736 | tf_op jit(solution)/shard_map/ppermute | solution.py:33
  250.7 49.7 %collective-permute-start.7 = (bf16[256,2048]{1,0:T(8,128)(2,1)}, bf16[256,2048]{1,0:T(8,128)(2,1)S(1)}, u32[]{:S(2)}, u32[]{:S(2)}) collective-permute-start(bf16[256,2048]{1,0:T(8,128)(2,1)} %collective-permute-done.6), channel_id=1, source_target_pairs={{0,4},{4,0},{8,12},{12,8},{16,20},{20,16},{24,28},{28,24},{1,5},{5... | collective-permute-start | bytes 3145736 | tf_op jit(solution)/shard_map/ppermute | solution.py:33
  257.7 46.2 %collective-permute-start.9 = (bf16[256,2048]{1,0:T(8,128)(2,1)}, bf16[256,2048]{1,0:T(8,128)(2,1)S(1)}, u32[]{:S(2)}, u32[]{:S(2)}) collective-permute-start(bf16[256,2048]{1,0:T(8,128)(2,1)} %collective-permute-done.8), channel_id=1, source_target_pairs={{0,4},{4,0},{8,12},{12,8},{16,20},{20,16},{24,28},{28,24},{1,5},{5... | collective-permute-start | bytes 3145736 | tf_op jit(solution)/shard_map/ppermute | solution.py:33
  259.0 41.1 %collective-permute-start.1 = (bf16[256,2048]{1,0:T(8,128)(2,1)S(1)}, bf16[256,2048]{1,0:T(8,128)(2,1)S(1)}, u32[]{:S(2)}, u32[]{:S(2)}) collective-permute-start(bf16[256,2048]{1,0:T(8,128)(2,1)S(1)} %add_convert_fusion.1), channel_id=1, source_target_pairs={{0,1},{1,2},{2,3},{3,0},{4,5},{5,6},{6,7},{7,4},{8,9},{9,10},{10,1... | collective-permute-start | bytes 3145736 | tf_op jit(solution)/shard_map/ppermute | solution.py:38
  262.5 68.8 %collective-permute-start.21 = (bf16[2048,256]{1,0:T(8,128)(2,1)S(1)}, bf16[2048,256]{1,0:T(8,128)(2,1)S(1)}, u32[]{:S(2)}, u32[]{:S(2)}) collective-permute-start(bf16[2048,256]{1,0:T(8,128)(2,1)S(1)} %pad_maximum_fusion.9), channel_id=1, source_target_pairs={{0,4},{4,0},{8,12},{12,8},{16,20},{20,16},{24,28},{28,24},{1,5},{5... | collective-permute-start | bytes 3145736 | tf_op jit(solution)/shard_map/ppermute | solution.py:33
  300.1 32.3 %collective-permute-start.12 = (bf16[256,2048]{1,0:T(8,128)(2,1)S(1)}, bf16[256,2048]{1,0:T(8,128)(2,1)S(1)}, u32[]{:S(2)}, u32[]{:S(2)}) collective-permute-start(bf16[256,2048]{1,0:T(8,128)(2,1)S(1)} %pad_maximum_fusion.8), channel_id=1, source_target_pairs={{0,4},{4,0},{8,12},{12,8},{16,20},{20,16},{24,28},{28,24},{1,5},{5... | collective-permute-start | bytes 3145736 | tf_op jit(solution)/shard_map/ppermute | solution.py:33
  300.4 27.4 %collective-permute-start.2 = (bf16[256,2048]{1,0:T(8,128)(2,1)S(1)}, bf16[256,2048]{1,0:T(8,128)(2,1)S(1)}, u32[]{:S(2)}, u32[]{:S(2)}) collective-permute-start(bf16[256,2048]{1,0:T(8,128)(2,1)S(1)} %add_convert_fusion), channel_id=1, source_target_pairs={{0,1},{1,2},{2,3},{3,0},{4,5},{5,6},{6,7},{7,4},{8,9},{9,10},{10,1... | collective-permute-start | bytes 3145736 | tf_op jit(solution)/shard_map/ppermute | solution.py:38
  329.2 24.9 %collective-permute-start.3 = (bf16[256,2048]{1,0:T(8,128)(2,1)S(1)}, bf16[256,2048]{1,0:T(8,128)(2,1)S(1)}, u32[]{:S(2)}, u32[]{:S(2)}) collective-permute-start(bf16[256,2048]{1,0:T(8,128)(2,1)S(1)} %multiply_convert_fusion.2), channel_id=1, source_target_pairs={{0,1},{1,0},{2,3},{3,2},{4,5},{5,4},{6,7},{7,6},{8,9},{9,8},{10,11... | collective-permute-start | bytes 3145736 | tf_op jit(solution)/shard_map/ppermute | solution.py:33
  375.6 30.1 %collective-permute-start.22 = (bf16[256,2048]{1,0:T(8,128)(2,1)S(1)}, bf16[256,2048]{1,0:T(8,128)(2,1)S(1)}, u32[]{:S(2)}, u32[]{:S(2)}) collective-permute-start(bf16[256,2048]{1,0:T(8,128)(2,1)S(1)} %convolution_convert_fusion.18), channel_id=1, source_target_pairs={{0,1},{1,0},{2,3},{3,2},{4,5},{5,4},{6,7},{7,6},{8,9},{9,8},{10,11... | collective-permute-start | bytes 3145736 | tf_op jit(solution)/shard_map/ppermute | solution.py:33
  391.4 30.6 %collective-permute-start.24 = (bf16[256,2048]{1,0:T(8,128)(2,1)}, bf16[256,2048]{1,0:T(8,128)(2,1)S(1)}, u32[]{:S(2)}, u32[]{:S(2)}) collective-permute-start(bf16[256,2048]{1,0:T(8,128)(2,1)} %convolution_convert_fusion.17), channel_id=1, source_target_pairs={{0,1},{1,0},{2,3},{3,2},{4,5},{5,4},{6,7},{7,6},{8,9},{9,8},{10,11... | collective-permute-start | bytes 3145736 | tf_op jit(solution)/shard_map/ppermute | solution.py:33
  393.9 43.7 %collective-permute-start.49 = (bf16[256,2048]{1,0:T(8,128)(2,1)S(1)}, bf16[256,2048]{1,0:T(8,128)(2,1)S(1)}, u32[]{:S(2)}, u32[]{:S(2)}) collective-permute-start(bf16[256,2048]{1,0:T(8,128)(2,1)S(1)} %convolution_convert_fusion.8), channel_id=1, source_target_pairs={{0,4},{4,0},{8,12},{12,8},{16,20},{20,16},{24,28},{28,24},{1,5},{5... | collective-permute-start | bytes 3145736 | tf_op jit(solution)/shard_map/ppermute | solution.py:33
  395.7 39.3 %collective-permute-start.46 = (bf16[256,2048]{1,0:T(8,128)(2,1)}, bf16[256,2048]{1,0:T(8,128)(2,1)}, u32[]{:S(2)}, u32[]{:S(2)}) collective-permute-start(bf16[256,2048]{1,0:T(8,128)(2,1)} %convolution_convert_fusion.10), channel_id=1, source_target_pairs={{0,4},{4,0},{8,12},{12,8},{16,20},{20,16},{24,28},{28,24},{1,5},{5... | collective-permute-start | bytes 3145736 | tf_op jit(solution)/shard_map/ppermute | solution.py:33
  397.9 50.6 %collective-permute-start.45 = (bf16[256,2048]{1,0:T(8,128)(2,1)}, bf16[256,2048]{1,0:T(8,128)(2,1)}, u32[]{:S(2)}, u32[]{:S(2)}) collective-permute-start(bf16[256,2048]{1,0:T(8,128)(2,1)} %convolution_convert_fusion.12), channel_id=1, source_target_pairs={{0,4},{4,0},{8,12},{12,8},{16,20},{20,16},{24,28},{28,24},{1,5},{5... | collective-permute-start | bytes 3145736 | tf_op jit(solution)/shard_map/ppermute | solution.py:33
  405.7 75.8 %collective-permute-start.44 = (bf16[256,2048]{1,0:T(8,128)(2,1)S(1)}, bf16[256,2048]{1,0:T(8,128)(2,1)S(1)}, u32[]{:S(2)}, u32[]{:S(2)}) collective-permute-start(bf16[256,2048]{1,0:T(8,128)(2,1)S(1)} %convolution_convert_fusion.14), channel_id=1, source_target_pairs={{0,4},{4,0},{8,12},{12,8},{16,20},{20,16},{24,28},{28,24},{1,5},{5... | collective-permute-start | bytes 3145736 | tf_op jit(solution)/shard_map/ppermute | solution.py:33
  423.0 17.6 %collective-permute-start.55 = (bf16[2048,256]{1,0:T(8,128)(2,1)}, bf16[2048,256]{1,0:T(8,128)(2,1)}, u32[]{:S(2)}, u32[]{:S(2)}) collective-permute-start(bf16[2048,256]{1,0:T(8,128)(2,1)} %convolution_convert_fusion.2), channel_id=1, source_target_pairs={{0,4},{4,0},{8,12},{12,8},{16,20},{20,16},{24,28},{28,24},{1,5},{5... | collective-permute-start | bytes 3145736 | tf_op jit(solution)/shard_map/ppermute | solution.py:33
  440.7 96.7 %collective-permute-start.53 = (bf16[2048,256]{1,0:T(8,128)(2,1)S(1)}, bf16[2048,256]{1,0:T(8,128)(2,1)S(1)}, u32[]{:S(2)}, u32[]{:S(2)}) collective-permute-start(bf16[2048,256]{1,0:T(8,128)(2,1)S(1)} %copy-done.118), channel_id=1, source_target_pairs={{0,4},{4,0},{8,12},{12,8},{16,20},{20,16},{24,28},{28,24},{1,5},{5... | collective-permute-start | bytes 3145736 | tf_op jit(solution)/shard_map/ppermute | solution.py:33
  448.6 34.4 %collective-permute-start.25 = (bf16[256,2048]{1,0:T(8,128)(2,1)S(1)}, bf16[256,2048]{1,0:T(8,128)(2,1)S(1)}, u32[]{:S(2)}, u32[]{:S(2)}) collective-permute-start(bf16[256,2048]{1,0:T(8,128)(2,1)S(1)} %get-tuple-element.58), channel_id=1, source_target_pairs={{0,1},{1,2},{2,3},{3,0},{4,5},{5,6},{6,7},{7,4},{8,9},{9,10},{10,1... | collective-permute-start | bytes 3145736 | tf_op jit(solution)/shard_map/ppermute | solution.py:38
  477.7 26.1 %collective-permute-start.51 = (bf16[256,2048]{1,0:T(8,128)(2,1)S(1)}, bf16[256,2048]{1,0:T(8,128)(2,1)S(1)}, u32[]{:S(2)}, u32[]{:S(2)}) collective-permute-start(bf16[256,2048]{1,0:T(8,128)(2,1)S(1)} %pad_maximum_fusion.11), channel_id=1, source_target_pairs={{0,16},{4,20},{8,24},{12,28},{16,0},{20,4},{24,8},{28,12},{1,17},{... | collective-permute-start | bytes 3145736 | tf_op jit(solution)/shard_map/ppermute | solution.py:33
  479.4 30.9 %collective-permute-start.48 = (bf16[256,2048]{1,0:T(8,128)(2,1)S(1)}, bf16[256,2048]{1,0:T(8,128)(2,1)S(1)}, u32[]{:S(2)}, u32[]{:S(2)}) collective-permute-start(bf16[256,2048]{1,0:T(8,128)(2,1)S(1)} %pad_maximum_fusion.10), channel_id=1, source_target_pairs={{0,8},{4,12},{8,0},{12,4},{16,24},{20,28},{24,16},{28,20},{1,9},{5... | collective-permute-start | bytes 3145736 | tf_op jit(solution)/shard_map/ppermute | solution.py:33
  481.5 55.8 %collective-permute-start.60 = (bf16[2048,256]{1,0:T(8,128)(2,1)S(1)}, bf16[2048,256]{1,0:T(8,128)(2,1)S(1)}, u32[]{:S(2)}, u32[]{:S(2)}) collective-permute-start(bf16[2048,256]{1,0:T(8,128)(2,1)S(1)} %pad_maximum_fusion.13), channel_id=1, source_target_pairs={{0,16},{4,20},{8,24},{12,28},{16,0},{20,4},{24,8},{28,12},{1,17},{... | collective-permute-start | bytes 3145736 | tf_op jit(solution)/shard_map/ppermute | solution.py:33
  483.0 54.3 %collective-permute-start.57 = (bf16[2048,256]{1,0:T(8,128)(2,1)S(1)}, bf16[2048,256]{1,0:T(8,128)(2,1)S(1)}, u32[]{:S(2)}, u32[]{:S(2)}) collective-permute-start(bf16[2048,256]{1,0:T(8,128)(2,1)S(1)} %pad_maximum_fusion.12), channel_id=1, source_target_pairs={{0,8},{4,12},{8,0},{12,4},{16,24},{20,28},{24,16},{28,20},{1,9},{5... | collective-permute-start | bytes 3145736 | tf_op jit(solution)/shard_map/ppermute | solution.py:33
  503.8 28.0 %collective-permute-start.26 = (bf16[256,2048]{1,0:T(8,128)(2,1)S(1)}, bf16[256,2048]{1,0:T(8,128)(2,1)S(1)}, u32[]{:S(2)}, u32[]{:S(2)}) collective-permute-start(bf16[256,2048]{1,0:T(8,128)(2,1)S(1)} %collective-permute-done.25), channel_id=1, source_target_pairs={{0,1},{1,2},{2,3},{3,0},{4,5},{5,6},{6,7},{7,4},{8,9},{9,10},{10,1... | collective-permute-start | bytes 3145736 | tf_op jit(solution)/shard_map/ppermute | solution.py:38
  511.3 69.9 %collective-permute-start.52 = (bf16[256,1024]{1,0:T(8,128)(2,1)S(1)}, bf16[256,1024]{1,0:T(8,128)(2,1)S(1)}, u32[]{:S(2)}, u32[]{:S(2)}) collective-permute-start(bf16[256,1024]{1,0:T(8,128)(2,1)S(1)} %slice.1073), channel_id=1, source_target_pairs={{0,2},{1,3},{2,0},{3,1},{4,6},{5,7},{6,4},{7,5},{8,10},{9,11},{10,... | collective-permute-start | bytes 1572872 | tf_op jit(solution)/shard_map/ppermute | solution.py:33
  531.8 61.7 %collective-permute-start.27 = (bf16[256,2048]{1,0:T(8,128)(2,1)S(1)}, bf16[256,2048]{1,0:T(8,128)(2,1)S(1)}, u32[]{:S(2)}, u32[]{:S(2)}) collective-permute-start(bf16[256,2048]{1,0:T(8,128)(2,1)S(1)} %collective-permute-done.26), channel_id=1, source_target_pairs={{0,1},{1,2},{2,3},{3,0},{4,5},{5,6},{6,7},{7,4},{8,9},{9,10},{10,1... | collective-permute-start | bytes 3145736 | tf_op jit(solution)/shard_map/ppermute | solution.py:38
  538.2 54.2 %collective-permute-start.61 = (bf16[1024,256]{1,0:T(8,128)(2,1)S(1)}, bf16[1024,256]{1,0:T(8,128)(2,1)S(1)}, u32[]{:S(2)}, u32[]{:S(2)}) collective-permute-start(bf16[1024,256]{1,0:T(8,128)(2,1)S(1)} %slice.1070), channel_id=1, source_target_pairs={{0,2},{1,3},{2,0},{3,1},{4,6},{5,7},{6,4},{7,5},{8,10},{9,11},{10,... | collective-permute-start | bytes 1572872 | tf_op jit(solution)/shard_map/ppermute | solution.py:33
  628.5 25.0 %collective-permute-start.41 = (bf16[1024,256]{1,0:T(8,128)(2,1)}, bf16[1024,256]{1,0:T(8,128)(2,1)S(1)}, u32[]{:S(2)}, u32[]{:S(2)}) collective-permute-start(bf16[1024,256]{1,0:T(8,128)(2,1)} %convolution_convert_fusion.20), channel_id=1, source_target_pairs={{0,4},{4,0},{8,12},{12,8},{16,20},{20,16},{24,28},{28,24},{1,5},{5... | collective-permute-start | bytes 1572872 | tf_op jit(solution)/shard_map/ppermute | solution.py:33
  628.6 26.8 %collective-permute-start.38 = (bf16[1024,256]{1,0:T(8,128)(2,1)}, bf16[1024,256]{1,0:T(8,128)(2,1)S(1)}, u32[]{:S(2)}, u32[]{:S(2)}) collective-permute-start(bf16[1024,256]{1,0:T(8,128)(2,1)} %convolution_convert_fusion.22), channel_id=1, source_target_pairs={{0,4},{4,0},{8,12},{12,8},{16,20},{20,16},{24,28},{28,24},{1,5},{5... | collective-permute-start | bytes 1572872 | tf_op jit(solution)/shard_map/ppermute | solution.py:33
  629.1 32.2 %collective-permute-start.37 = (bf16[1024,256]{1,0:T(8,128)(2,1)}, bf16[1024,256]{1,0:T(8,128)(2,1)S(1)}, u32[]{:S(2)}, u32[]{:S(2)}) collective-permute-start(bf16[1024,256]{1,0:T(8,128)(2,1)} %convolution_convert_fusion.24), channel_id=1, source_target_pairs={{0,4},{4,0},{8,12},{12,8},{16,20},{20,16},{24,28},{28,24},{1,5},{5... | collective-permute-start | bytes 1572872 | tf_op jit(solution)/shard_map/ppermute | solution.py:33
  629.2 41.5 %collective-permute-start.36 = (bf16[1024,256]{1,0:T(8,128)(2,1)}, bf16[1024,256]{1,0:T(8,128)(2,1)S(1)}, u32[]{:S(2)}, u32[]{:S(2)}) collective-permute-start(bf16[1024,256]{1,0:T(8,128)(2,1)} %convolution_convert_fusion.26), channel_id=1, source_target_pairs={{0,4},{4,0},{8,12},{12,8},{16,20},{20,16},{24,28},{28,24},{1,5},{5... | collective-permute-start | bytes 1572872 | tf_op jit(solution)/shard_map/ppermute | solution.py:33
  721.8 101.2 %collective-permute-start.33 = (bf16[256,1024]{1,0:T(8,128)(2,1)}, bf16[256,1024]{1,0:T(8,128)(2,1)}, u32[]{:S(2)}, u32[]{:S(2)}) collective-permute-start(bf16[256,1024]{1,0:T(8,128)(2,1)} %convolution_convert_fusion.28), channel_id=1, source_target_pairs={{0,4},{4,0},{8,12},{12,8},{16,20},{20,16},{24,28},{28,24},{1,5},{5... | collective-permute-start | bytes 1572872 | tf_op jit(solution)/shard_map/ppermute | solution.py:33
  721.8 103.2 %collective-permute-start.30 = (bf16[256,1024]{1,0:T(8,128)(2,1)S(1)}, bf16[256,1024]{1,0:T(8,128)(2,1)}, u32[]{:S(2)}, u32[]{:S(2)}) collective-permute-start(bf16[256,1024]{1,0:T(8,128)(2,1)S(1)} %convolution_convert_fusion.30), channel_id=1, source_target_pairs={{0,4},{4,0},{8,12},{12,8},{16,20},{20,16},{24,28},{28,24},{1,5},{5... | collective-permute-start | bytes 1572872 | tf_op jit(solution)/shard_map/ppermute | solution.py:33
  722.3 107.7 %collective-permute-start.29 = (bf16[256,1024]{1,0:T(8,128)(2,1)}, bf16[256,1024]{1,0:T(8,128)(2,1)}, u32[]{:S(2)}, u32[]{:S(2)}) collective-permute-start(bf16[256,1024]{1,0:T(8,128)(2,1)} %convolution_convert_fusion.32), channel_id=1, source_target_pairs={{0,4},{4,0},{8,12},{12,8},{16,20},{20,16},{24,28},{28,24},{1,5},{5... | collective-permute-start | bytes 1572872 | tf_op jit(solution)/shard_map/ppermute | solution.py:33
  722.3 120.2 %collective-permute-start.28 = (bf16[256,1024]{1,0:T(8,128)(2,1)}, bf16[256,1024]{1,0:T(8,128)(2,1)S(1)}, u32[]{:S(2)}, u32[]{:S(2)}) collective-permute-start(bf16[256,1024]{1,0:T(8,128)(2,1)} %convolution_convert_fusion.34), channel_id=1, source_target_pairs={{0,4},{4,0},{8,12},{12,8},{16,20},{20,16},{24,28},{28,24},{1,5},{5... | collective-permute-start | bytes 1572872 | tf_op jit(solution)/shard_map/ppermute | solution.py:33
  (141 other events, 3048.0 us)
Sparse Core Ops, SparseCore 0:
  140.3 34.8 all-gather.4
  627.1 36.4 all-gather.6

commit v3 on v2

--- a/solution.py
+++ b/solution.py
@@ -154,6 +154,15 @@
         "pair": {"tok": tok, "head": flipped(z, 1)},
         "cross": {"tok": tok, "head": flipped(z, 2)},
     }
+
+
+def everyone():
+    near = peers()
+    tok = lax.axis_index("tok")
+    z = lax.axis_index("head")
+    count = lax.axis_size("head")
+    others = [{"tok": tok, "head": lax.rem(z + step, count)} for step in range(1, count)]
+    return [near["core"], near["x"], near["y"], *others]
 
 
 def greet(*devices):
@@ -453,24 +462,31 @@
 
 
 class Scatter:
-    def __init__(self, moves, near, term, buffers, result):
+    def __init__(self, moves, near, term, buffers, result, before=None, ready=None):
         self.moves, self.near, self.term, self.result = moves, near, term, result
         self.odd_out, self.odd_in, self.far_out, self.far_in, self.near_out, self.near_in = buffers
         self.half = self.far_out.shape[0] // 2
+        self.before, self.ready, self.frees = before, ready, None
+        self.cores = {}
 
     def odd(self, i):
+        if self.before is not None:
+            if not self.cores:
+                pl.semaphore_wait(self.ready, 1)
+            self.moves.sent(self.before.cores[i])
         self.odd_out[i] = self.term(2 * i + 1).astype(BF)
-        move = self.moves.go(self.odd_out.at[i], self.odd_in.at[i], self.near["core"])
-        if i == 3:
-            self.cores = {}
-        self.cores[i] = move
+        self.cores[i] = self.moves.go(self.odd_out.at[i], self.odd_in.at[i], self.near["core"])
 
     def folded(self, i):
         self.cores[i].wait_recv()
         return self.term(2 * i) + self.odd_in[i].astype(F32)
 
     def far(self):
-        self.far_out[...] = self.folded(3).astype(BF)
+        value = self.folded(3).astype(BF)
+        if self.before is not None:
+            for move in self.before.fars:
+                self.moves.sent(move)
+        self.far_out[...] = value
         self.fars = [
             self.moves.go(
                 self.far_out.at[pl.ds(side * self.half, self.half), :],
@@ -488,18 +504,23 @@
             self.fars[side].wait_recv()
             helped = value[side * half : (side + 1) * half] + self.far_in[side].astype(F32)
             other = value[(1 - side) * half : (2 - side) * half]
+            if self.before is not None:
+                self.moves.sent(self.before.nears[i - 1])
             self.near_out[i - 1, pl.ds(side * half, half), :] = helped.astype(BF)
             self.near_out[i - 1, pl.ds((1 - side) * half, half), :] = other.astype(BF)
             self.nears.append(
                 self.moves.go(self.near_out.at[i - 1], self.near_in.at[i - 1], self.near[way])
             )
+        self.result[...] = self.folded(0)
+        if self.frees is not None:
+            pl.semaphore_signal(
+                self.frees, inc=1, device_id=self.near["core"], device_id_type=MESH
+            )
 
     def done(self):
-        value = self.folded(0)
         for i in range(2):
             self.nears[i].wait_recv()
-            value = value + self.near_in[i].astype(F32)
-        self.result(value)
+        self.result[...] += self.near_in[0].astype(F32) + self.near_in[1].astype(F32)
 
 
 def leave_kernel(
@@ -509,11 +530,12 @@
     tok_ref,
     resid_ref,
     gain_ref,
-    sums_ref,
+    ffn_ref,
+    group_ref,
     tokens_grad,
-    wq_out,
-    wk_out,
+    wqk_out,
     wv_out,
+    wg_out,
     gains_out,
     grads,
     weights,
@@ -533,6 +555,7 @@
     send,
     recv,
     load_sem,
+    free_sem,
 ):
     near = peers()
     tok = lax.axis_index("tok")
@@ -596,22 +619,20 @@
 
         return term
 
-    def qk_result(value):
-        wq_out[...] = value[:, : cols // 2]
-        wk_out[...] = value[:, cols // 2 :]
-
-    def v_result(value):
-        wv_out[...] = value
-
     def buffers(c):
+        s = c % 2
         return (
-            odd_out.at[c], odd_in.at[c], far_out.at[c], far_in.at[c], near_out.at[c], near_in.at[c]
+            odd_out.at[s], odd_in.at[s], far_out.at[s], far_in.at[c], near_out.at[s], near_in.at[c]
         )
 
     scatters = [
         Scatter(moves, near, chunk_term(c), buffers(c), result)
-        for c, result in enumerate((qk_result, v_result))
+        for c, result in enumerate((wqk_out, wv_out))
     ]
+    scatters.append(
+        Scatter(moves, near, chunk_term(2), buffers(2), wg_out, scatters[0], free_sem)
+    )
+    scatters[0].frees = free_sem
 
     loads[0].wait()
     loads[1].wait()
@@ -628,18 +649,32 @@
         scatters[1].odd(i)
     ring_send(1, 1)
     scatters[0].close()
-    ring_term(2)
     for i in (2, 0):
         scatters[1].odd(i)
+    ring_term(2)
     ring_send(2, 0)
     scatters[1].far()
+    for i in (3, 1):
+        scatters[2].odd(i)
     ring_send(2, 1)
     scatters[1].close()
+    for i in (2, 0):
+        scatters[2].odd(i)
     scatters[0].done()
+    scatters[2].far()
     ring_term(3)
     scatters[1].done()
-
-    gains[...] = sums_ref[...]
+    scatters[2].close()
+    scatters[2].done()
+
+    gains[...] = jnp.zeros_like(gains)
+    gains[pl.ds(2, 1), pl.ds(0, group_ref.shape[1])] = group_ref[pl.ds(0, 1), :]
+    for r, place in enumerate(xor_places(tok)):
+        at = pl.ds(pl.multiple_of(place * part, part), part)
+        gains[pl.ds(1, 1), at] = (
+            ffn_ref[pl.ds(0, 1), r * part : (r + 1) * part]
+            + ffn_ref[pl.ds(1, 1), r * part : (r + 1) * part]
+        )
     size = 32
     for side in range(2):
         ring[2, side].wait_recv()
@@ -689,22 +724,23 @@
     moves.finish()
 
 
-def depart(grads, weights, turned, tokens, resid_grad, gain, sums):
+def depart(grads, weights, turned, tokens, resid_grad, gain, ffn_terms, group_terms):
     rows, width = tokens.shape
     count = lax.axis_size("head")
     cols = grads.shape[1] // 3
     part = width // 8
-    moves = 6 + 2 * 8 + 3 + count - 1
+    moves = 6 + 3 * 8 + 3 + count - 1
+    sums = (8, width)
     return pl.pallas_call(
         leave_kernel,
         out_shape=(
             jax.ShapeDtypeStruct((rows, width), F32),
-            jax.ShapeDtypeStruct((part, cols // 2), F32),
-            jax.ShapeDtypeStruct((part, cols // 2), F32),
             jax.ShapeDtypeStruct((part, cols), F32),
-            jax.ShapeDtypeStruct(sums.shape, F32),
+            jax.ShapeDtypeStruct((part, cols), F32),
+            jax.ShapeDtypeStruct((part, cols), F32),
+            jax.ShapeDtypeStruct(sums, F32),
         ),
-        in_specs=[ANY] * 3 + [VMEM] * 4,
+        in_specs=[ANY] * 3 + [VMEM] * 5,
         out_specs=[VMEM] * 5,
         scratch_shapes=[
             pltpu.VMEM(grads.shape, BF),
@@ -716,15 +752,16 @@
             pltpu.VMEM((2, 4, part, cols), BF),
             pltpu.VMEM((2, 4, part, cols), BF),
             pltpu.VMEM((2, part, cols), BF),
-            pltpu.VMEM((2, 2, part // 2, cols), BF),
+            pltpu.VMEM((3, 2, part // 2, cols), BF),
             pltpu.VMEM((2, 2, part, cols), BF),
-            pltpu.VMEM((2, 2, part, cols), BF),
-            pltpu.VMEM(sums.shape, F32),
-            pltpu.VMEM((3,) + sums.shape, F32),
-            pltpu.VMEM((count - 1,) + sums.shape, F32),
+            pltpu.VMEM((3, 2, part, cols), BF),
+            pltpu.VMEM(sums, F32),
+            pltpu.VMEM((3,) + sums, F32),
+            pltpu.VMEM((count - 1,) + sums, F32),
             pltpu.SemaphoreType.DMA((moves,)),
             pltpu.SemaphoreType.DMA((moves,)),
             pltpu.SemaphoreType.DMA((3,)),
+            pltpu.SemaphoreType.REGULAR,
         ],
         compiler_params=pltpu.CompilerParams(
             collective_id=1, has_side_effects=True, vmem_limit_bytes=LIMIT
@@ -732,7 +769,922 @@
         cost_estimate=pl.CostEstimate(
             flops=2 * grads.shape[0] * width * 5 * cols, bytes_accessed=40 << 20, transcendentals=0
         ),
-    )(grads, weights, turned, tokens, resid_grad, gain[None, :], sums)
+    )(
+        grads, weights, turned, tokens, resid_grad, gain[None, :], ffn_terms, group_terms
+    )
+
+
+def dot_nt(left, right):
+    return lax.dot_general(left, right, (((1,), (1,)), ((), ())), preferred_element_type=F32)
+
+
+def dot_tn(left, right):
+    return lax.dot_general(left, right, (((0,), (0,)), ((), ())), preferred_element_type=F32)
+
+
+def dot_nn(left, right):
+    return jnp.dot(left, right, preferred_element_type=F32)
+
+
+def tile_decay(docs_col, docs_row, log_decay, first, tile, top):
+    size = tile + top
+    shape = (top, size)
+    lag = (
+        lax.broadcasted_iota(jnp.int32, shape, 0)
+        + tile
+        - lax.broadcasted_iota(jnp.int32, shape, 1)
+    )
+    same = docs_col[pl.ds(first + tile, top), :] == docs_row[:, pl.ds(first, size)]
+    power = jnp.exp(jnp.maximum(lag, 0).astype(F32) * log_decay)
+    return jnp.where(same & (lag >= 0), power, 0.0)
+
+
+def retain_kernel(
+    decay_ref,
+    across_ref,
+    fold_ref,
+    docs_col,
+    docs_row,
+    scale_ref,
+    gain_ref,
+    qk_ref,
+    v_ref,
+    gate_ref,
+    tok_ref,
+    wo_ref,
+    cot_ref,
+    wu_ref,
+    wd_ref,
+    resid_out,
+    unit_out,
+    inverse_out,
+    states_out,
+    cot_pair,
+    mixed_turned,
+    up_full,
+    down_full,
+    mixed_out,
+    out_weights,
+    retained,
+    terms,
+    folded,
+    gathered,
+    held,
+    ring_out,
+    ring_in,
+    cot_rows,
+    send,
+    recv,
+    own_sem,
+):
+    near = peers()
+    tok = lax.axis_index("tok")
+    z = lax.axis_index("head")
+    count = lax.axis_size("head")
+    rows, width = tok_ref.shape
+    group_rows = rows * count
+    part = width // 8
+    heads = v_ref.shape[1] // VAL
+    blocks = group_rows // SPAN
+    side_rows = rows // 2
+    slice_ = wu_ref.shape[1]
+    own = [
+        pltpu.make_async_copy(
+            wu_ref, up_full.at[pl.ds(0, part), pl.ds(0, slice_)], own_sem.at[0]
+        ),
+        pltpu.make_async_copy(
+            wd_ref, down_full.at[pl.ds(0, slice_), pl.ds(0, part)], own_sem.at[1]
+        ),
+        pltpu.make_async_copy(wo_ref, out_weights, own_sem.at[2]),
+    ]
+    for copy in own:
+        copy.start()
+    greet(*everyone())
+    moves = Moves(send, recv)
+    far_up = moves.go(
+        wu_ref, up_full.at[pl.ds(0, part), pl.ds(slice_, slice_)], near["cross"]
+    )
+    far_down = moves.go(
+        wd_ref, down_full.at[pl.ds(slice_, slice_), pl.ds(0, part)], near["cross"]
+    )
+
+    def block_rows(b):
+        return pl.ds(pl.multiple_of(b * SPAN, SPAN), SPAN)
+
+    def q_cols(h):
+        return pl.ds(h * KEY, KEY)
+
+    def k_cols(h):
+        return pl.ds((heads + h) * KEY, KEY)
+
+    def v_cols(h):
+        return pl.ds(h * VAL, VAL)
+
+    for h in range(heads):
+        total = jnp.zeros((KEY, VAL), F32)
+        for b in range(blocks):
+            weighed = v_ref[block_rows(b), v_cols(h)].astype(F32) * scale_ref[
+                block_rows(b), heads + h : heads + h + 1
+            ]
+            term = dot_tn(qk_ref[block_rows(b), k_cols(h)], weighed.astype(BF))
+            terms[b, pl.ds(h * KEY, KEY), :] = term
+            total = across_ref[h, b] * total + term
+        gathered[0, pl.ds(h * KEY, KEY), :] = total.astype(BF)
+
+    def state_view(r, side=None):
+        if side is None:
+            return gathered.at[r]
+        size = gathered.shape[1] // 2
+        return gathered.at[r, pl.ds(side * size, size), :]
+
+    def up_view(s):
+        def view(r, side=None):
+            if side is None:
+                return up_full.at[pl.ds(r * part, part), pl.ds(s * slice_, slice_)]
+            size = part // 2
+            return up_full.at[
+                pl.ds(r * part + side * size, size), pl.ds(s * slice_, slice_)
+            ]
+
+        return view
+
+    def down_view(s):
+        def view(r, side=None):
+            if side is None:
+                return down_full.at[pl.ds(s * slice_, slice_), pl.ds(r * part, part)]
+            size = slice_ // 2
+            return down_full.at[
+                pl.ds(s * slice_ + side * size, size), pl.ds(r * part, part)
+            ]
+
+        return view
+
+    states = Gather(moves, near, state_view)
+    wide = [
+        Gather(moves, near, view) for view in (up_view(0), down_view(0), up_view(1), down_view(1))
+    ]
+    states.first()
+    own[0].wait()
+    own[1].wait()
+    wide[0].first()
+    cot_move = moves.go(cot_ref, cot_rows, near["pair"])
+
+    def intra(h):
+        @pl.loop(0, blocks)
+        def _(b):
+            first = pl.multiple_of(b * SPAN, SPAN)
+            for tile in range(0, SPAN, 128):
+                at = pl.ds(first + tile, 128)
+                seen = pl.ds(first, tile + 128)
+                scores = dot_nt(qk_ref[at, q_cols(h)], qk_ref[seen, k_cols(h)])
+                mask = tile_decay(docs_col, docs_row, decay_ref[h], first, tile, 128)
+                probs = (scores * mask).astype(BF)
+                retained[at, v_cols(h)] = dot_nn(probs, v_ref[seen, v_cols(h)])
+
+    def finish_head(h):
+        first = jnp.zeros((KEY, VAL), F32)
+        for r in range(8):
+            first = first + fold_ref[h, r] * gathered[r, pl.ds(h * KEY, KEY), :].astype(F32)
+        for b in range(blocks):
+            folded[b] = first.astype(BF)
+            states_out[pl.ds((h * blocks + b) * KEY, KEY), :] = first.astype(BF)
+            first = across_ref[h, b] * first + terms[b, pl.ds(h * KEY, KEY), :]
+
+        @pl.loop(0, group_rows // 128)
+        def _(i):
+            at = pl.ds(pl.multiple_of(i * 128, 128), 128)
+            b = lax.div(i, SPAN // 128)
+            cross = dot_nn(qk_ref[at, q_cols(h)], folded[b])
+            values = retained[at, v_cols(h)] + scale_ref[at, h : h + 1] * cross
+            mean = jnp.mean(values, axis=-1, keepdims=True)
+            centred = values - mean
+            inverse = lax.rsqrt(jnp.mean(centred * centred, axis=-1, keepdims=True) + EPS)
+            unit = centred * inverse
+            gate = gate_ref[at, v_cols(h)].astype(F32)
+            swish = gate / (1.0 + jnp.exp(-gate))
+            unit_out[at, v_cols(h)] = unit.astype(BF)
+            inverse_out[at, h : h + 1] = inverse
+            mixed = (swish * unit * gain_ref[:, h * VAL : (h + 1) * VAL]).astype(BF)
+            mixed_out[at, v_cols(h)] = mixed
+            mixed_turned[v_cols(h), at] = mixed.T
+
+    intra(0)
+    states.second()
+    wide[1].first()
+    for h in range(1, heads):
+        intra(h)
+    states.third()
+    wide[0].second()
+    states.done()
+    for h in range(heads):
+        finish_head(h)
+
+    def ring_term(step):
+        owner = lax.rem(z + 2 * count - 1 - step, count)
+        at = pl.ds(pl.multiple_of(owner * rows, rows), rows)
+
+        @pl.loop(0, width // 256)
+        def _(i):
+            to = pl.ds(pl.multiple_of(i * 256, 256), 256)
+            held[:, to] = dot_nn(mixed_out[at, :], out_weights[:, to])
+
+    ring = {}
+
+    def ring_send(step, side):
+        at = pl.ds(side * side_rows, side_rows)
+        value = held[at, :]
+        if step:
+            ring[step - 1, side].wait_recv()
+            value = value + ring_in[step - 1, at, :].astype(F32)
+        ring_out[step, at, :] = value.astype(BF)
+        ring[step, side] = moves.go(
+            ring_out.at[step, at, :], ring_in.at[step, at, :], near["up"]
+        )
+
+    own[2].wait()
+    ring_term(0)
+    ring_send(0, 0)
+    ring_send(0, 1)
+    wide[1].second()
+    far_up.wait_recv()
+    wide[2].first()
+    wide[0].third()
+    ring_term(1)
+    ring_send(1, 0)
+    far_down.wait_recv()
+    wide[3].first()
+    wide[1].third()
+    ring_send(1, 1)
+    ring_term(2)
+    wide[2].second()
+    ring_send(2, 0)
+    wide[3].second()
+    ring_send(2, 1)
+    ring_term(3)
+    wide[2].third()
+    wide[3].third()
+    size = 32
+    for side in range(2):
+        ring[2, side].wait_recv()
+
+        @pl.loop(0, side_rows // size)
+        def _(i):
+            at = pl.ds(pl.multiple_of(side * side_rows + i * size, size), size)
+            values = jnp.concatenate(
+                [
+                    tok_ref[at, pl.ds(pl.multiple_of(place * part, part), part)]
+                    for place in xor_places(tok)
+                ],
+                axis=1,
+            ).astype(F32)
+            resid_out[at, :] = values + held[at, :] + ring_in[2, at, :].astype(F32)
+
+    cot_move.wait_recv()
+    for ref, first in ((cot_ref, 0), (cot_rows, rows)):
+        for r, place in enumerate(xor_places(tok)):
+            cot_pair[pl.ds(first, rows), pl.ds(r * part, part)] = ref[
+                :, pl.ds(pl.multiple_of(place * part, part), part)
+            ]
+    for gather in wide:
+        gather.done()
+    moves.finish()
+
+
+SMEM = pl.BlockSpec(memory_space=pltpu.SMEM)
+
+
+def retain(
+    decay, across, fold, docs, scales, gain, qk, v, gate, tokens, out_full, cotangent, w_up, w_down
+):
+    rows, width = tokens.shape
+    count = lax.axis_size("head")
+    group_rows = rows * count
+    heads = v.shape[1] // VAL
+    blocks = group_rows // SPAN
+    wide = 2 * w_up.shape[1]
+    moves = 3 + 5 * 8 + 6
+    struct = jax.ShapeDtypeStruct
+    return pl.pallas_call(
+        retain_kernel,
+        out_shape=(
+            struct((rows, width), F32),
+            struct(v.shape, BF),
+            struct((group_rows, heads), F32),
+            struct((heads * blocks * KEY, VAL), BF),
+            struct((2 * rows, width), BF),
+            struct((heads * VAL, group_rows), BF),
+            struct((width, wide), BF),
+            struct((wide, width), BF),
+        ),
+        in_specs=[SMEM] * 3 + [VMEM] * 8 + [ANY, VMEM] + [ANY] * 2,
+        out_specs=[VMEM] * 6 + [ANY] * 2,
+        scratch_shapes=[
+            pltpu.VMEM(v.shape, BF),
+            pltpu.VMEM(out_full.shape, BF),
+            pltpu.VMEM((group_rows, heads * VAL), F32),
+            pltpu.VMEM((blocks, heads * KEY, VAL), F32),
+            pltpu.VMEM((blocks, KEY, VAL), BF),
+            pltpu.VMEM((8, heads * KEY, VAL), BF),
+            pltpu.VMEM((rows, width), F32),
+            pltpu.VMEM((3, rows, width), BF),
+            pltpu.VMEM((3, rows, width), BF),
+            pltpu.VMEM((rows, width), BF),
+            pltpu.SemaphoreType.DMA((moves,)),
+            pltpu.SemaphoreType.DMA((moves,)),
+            pltpu.SemaphoreType.DMA((3,)),
+        ],
+        compiler_params=pltpu.CompilerParams(
+            collective_id=2, has_side_effects=True, vmem_limit_bytes=LIMIT
+        ),
+        cost_estimate=pl.CostEstimate(
+            flops=12 << 30, bytes_accessed=40 << 20, transcendentals=0
+        ),
+    )(
+        decay, across, fold, docs[:, None], docs[None, :], scales, gain[None, :], qk, v, gate,
+        tokens, out_full, cotangent, w_up, w_down,
+    )
+
+
+def feed_kernel(
+    resid_ref,
+    gain_ref,
+    cot_ref,
+    up_ref,
+    down_ref,
+    layer_out,
+    far_out,
+    resid_grad,
+    gain_out,
+    up_own,
+    up_far,
+    down_own,
+    down_far,
+    branch,
+    up,
+    down,
+    lifted,
+    cot,
+    hidden,
+    turned,
+    pre,
+    back_out,
+    back_in,
+    staged,
+    odd_out_d,
+    odd_in_d,
+    odd_out_u,
+    odd_in_u,
+    far_out_d,
+    far_in_d,
+    far_out_u,
+    far_in_u,
+    near_out_d,
+    near_in_d,
+    near_out_u,
+    near_in_u,
+    send,
+    recv,
+    load_sem,
+    free_sem,
+):
+    near = peers()
+    z = lax.axis_index("head")
+    count = lax.axis_size("head")
+    rows, width = resid_ref.shape
+    part = width // 8
+    side_rows = rows // 2
+    wide = up.shape[1]
+    slice_ = wide // 2
+    loads = [
+        pltpu.make_async_copy(cot_ref, cot, load_sem.at[0]),
+        pltpu.make_async_copy(up_ref, up, load_sem.at[1]),
+        pltpu.make_async_copy(down_ref, down, load_sem.at[2]),
+    ]
+    for load in loads:
+        load.start()
+    greet(*everyone())
+    moves = Moves(send, recv)
+    size = 32
+
+    pairs = []
+    for side in range(2):
+
+        @pl.loop(0, side_rows // size)
+        def _(i):
+            at = pl.ds(pl.multiple_of(side * side_rows + i * size, size), size)
+            values = resid_ref[at, :]
+            mean = jnp.mean(values, axis=-1, keepdims=True)
+            centred = values - mean
+            inverse = lax.rsqrt(jnp.mean(centred * centred, axis=-1, keepdims=True) + EPS)
+            lifted[at, :] = (centred * inverse * gain_ref[...]).astype(BF)
+
+        pairs.append(
+            moves.go(
+                lifted.at[pl.ds(side * side_rows, side_rows), :],
+                lifted.at[pl.ds(rows + side * side_rows, side_rows), :],
+                near["pair"],
+            )
+        )
+
+    def feed(first, number):
+        @pl.loop(0, wide // 256)
+        def _(i):
+            to = pl.ds(pl.multiple_of(i * 256, 256), 256)
+            at = pl.ds(first, number)
+            hidden_pre = dot_nn(lifted[at, :], up[:, to])
+            hidden_grad = dot_nt(cot[at, :], down[to, :])
+            phi = 0.5 * (1.0 + lax.erf(hidden_pre * SQRT_HALF))
+            made = (hidden_pre * phi).astype(BF)
+            hidden[at, to] = made
+            turned[to, at] = made.T
+            slope = phi + hidden_pre * jnp.exp(-0.5 * hidden_pre * hidden_pre) * INV_ROOT_TWO_PI
+            pre[at, to] = (hidden_grad * slope).astype(BF)
+
+    for load in loads:
+        load.wait()
+    feed(0, rows)
+    backs = []
+    for side in range(2):
+        pairs[side].wait_recv()
+        feed(rows + side * side_rows, side_rows)
+
+        @pl.loop(0, width // 256)
+        def _(i):
+            to = pl.ds(pl.multiple_of(i * 256, 256), 256)
+            found = dot_nt(pre[pl.ds(rows + side * side_rows, side_rows), :], up[to, :])
+            back_out[pl.ds(side * side_rows, side_rows), to] = found.astype(BF)
+
+        at = pl.ds(side * side_rows, side_rows)
+        backs.append(moves.go(back_out.at[at, :], back_in.at[at, :], near["pair"]))
+
+    @pl.loop(0, width // 256)
+    def _(i):
+        to = pl.ds(pl.multiple_of(i * 256, 256), 256)
+        resid_grad[:, to] = dot_nt(pre[pl.ds(0, rows), :], up[to, :])
+
+    def down_term(s):
+        def term(r):
+            return dot_nn(turned[pl.ds(s * slice_, slice_), :], cot[:, r * part : (r + 1) * part])
+
+        return term
+
+    def up_term(s):
+        def term(r):
+            return dot_tn(
+                lifted[:, r * part : (r + 1) * part], pre[:, s * slice_ : (s + 1) * slice_]
+            )
+
+        return term
+
+    down_sets = [
+        (odd_out_d, odd_in_d, far_out_d, far_in_d.at[s], near_out_d, near_in_d.at[s])
+        for s in range(2)
+    ]
+    up_sets = [
+        (odd_out_u, odd_in_u, far_out_u, far_in_u.at[s], near_out_u, near_in_u.at[s])
+        for s in range(2)
+    ]
+    sums = [
+        Scatter(moves, near, down_term(0), down_sets[0], down_own),
+        Scatter(moves, near, up_term(0), up_sets[0], up_own),
+    ]
+    sums += [
+        Scatter(moves, near, down_term(1), down_sets[1], down_far, sums[0], free_sem.at[0]),
+        Scatter(moves, near, up_term(1), up_sets[1], up_far, sums[1], free_sem.at[1]),
+    ]
+    sums[0].frees = free_sem.at[0]
+    sums[1].frees = free_sem.at[1]
+
+    ring = {}
+
+    def shard(step, side):
+        owner = lax.rem(z - step + count, count)
+        first = pl.multiple_of(owner * rows + side * side_rows, side_rows)
+        return branch.at[pl.ds(first, side_rows), :]
+
+    def pass_on(step, side):
+        if step:
+            ring[step - 1, side].wait_recv()
+        if step < count - 1:
+            here = staged.at[pl.ds(side * side_rows, side_rows), :] if step == 0 else shard(step, side)
+            ring[step, side] = moves.go(here, shard(step, side), near["up"])
+
+    def norm_back(side):
+        backs[side].wait_recv()
+
+        def block(i, total):
+            at = pl.ds(pl.multiple_of(side * side_rows + i * size, size), size)
+            values = resid_ref[at, :]
+            mean = jnp.mean(values, axis=-1, keepdims=True)
+            centred = values - mean
+            inverse = lax.rsqrt(jnp.mean(centred * centred, axis=-1, keepdims=True) + EPS)
+            unit = centred * inverse
+            grad = resid_grad[at, :] + back_in[at, :].astype(F32)
+            scaled = grad * gain_ref[...]
+            first = jnp.mean(scaled, axis=-1, keepdims=True)
+            second = jnp.mean(scaled * unit, axis=-1, keepdims=True)
+            found = cot[at, :].astype(F32) + inverse * (scaled - first - unit * second)
+            resid_grad[at, :] = found
+            staged[at, :] = found.astype(BF)
+            return total + jnp.sum(grad * unit, axis=0, keepdims=True)
+
+        total = lax.fori_loop(0, side_rows // size, block, jnp.zeros((1, width), F32))
+        gain_out[pl.ds(side, 1), :] = total
+
+    norm_back(0)
+    pass_on(0, 0)
+    for i in (3, 1):
+        sums[0].odd(i)
+    norm_back(1)
+    pass_on(0, 1)
+    mine = pltpu.make_async_copy(
+        staged, branch.at[pl.ds(pl.multiple_of(z * rows, rows), rows), :], load_sem.at[3]
+    )
+    mine.start()
+    for i in (2, 0):
+        sums[0].odd(i)
+    pass_on(1, 0)
+    sums[0].far()
+    for i in (3, 1):
+        sums[1].odd(i)
+
+    @pl.loop(0, width // 256)
+    def _(i):
+        to = pl.ds(pl.multiple_of(i * 256, 256), 256)
+        layer_out[:, to] = resid_ref[:, to] + dot_nn(hidden[pl.ds(0, rows), :], down[:, to])
+
+    pass_on(1, 1)
+    for i in (2, 0):
+        sums[1].odd(i)
+    sums[0].close()
+    sums[1].far()
+    pass_on(2, 0)
+    for i in (3, 1):
+        sums[2].odd(i)
+
+    @pl.loop(0, width // 256)
+    def _(i):
+        to = pl.ds(pl.multiple_of(i * 256, 256), 256)
+        far_out[:, to] = dot_nn(hidden[pl.ds(rows, rows), :], down[:, to]).astype(BF)
+
+    sums[1].close()
+    for i in (2, 0):
+        sums[2].odd(i)
+    pass_on(2, 1)
+    sums[2].far()
+    for i in (3, 1, 2, 0):
+        sums[3].odd(i)
+    sums[0].done()
+    sums[3].far()
+    sums[2].close()
+    sums[1].done()
+    sums[3].close()
+    pass_on(3, 0)
+    sums[2].done()
+    sums[3].done()
+    pass_on(3, 1)
+    mine.wait()
+    moves.finish()
+
+
+def feed_forward(resid, gain, cot_pair, up_full, down_full):
+    rows, width = resid.shape
+    count = lax.axis_size("head")
+    part = width // 8
+    wide = up_full.shape[1]
+    slice_ = wide // 2
+    moves = 4 + 4 * 8 + 6
+    struct = jax.ShapeDtypeStruct
+    down_piece = (slice_, part)
+    up_piece = (part, slice_)
+
+    def sets(piece):
+        half = (piece[0] // 2, piece[1])
+        return [
+            pltpu.VMEM(piece, BF),
+            pltpu.VMEM((2, 2) + half, BF),
+        ]
+
+    def nears(piece):
+        return [pltpu.VMEM((2,) + piece, BF), pltpu.VMEM((2, 2) + piece, BF)]
+
+    def odds(piece):
+        return [pltpu.VMEM((4,) + piece, BF)] * 2
+
+    return pl.pallas_call(
+        feed_kernel,
+        out_shape=(
+            struct((rows, width), F32),
+            struct((rows, width), BF),
+            struct((rows, width), F32),
+            struct((8, width), F32),
+            struct(up_piece, F32),
+            struct(up_piece, F32),
+            struct(down_piece, F32),
+            struct(down_piece, F32),
+            struct((count * rows, width), BF),
+        ),
+        in_specs=[VMEM] * 2 + [ANY] * 3,
+        out_specs=[VMEM] * 8 + [ANY],
+        scratch_shapes=[
+            pltpu.VMEM((width, wide), BF),
+            pltpu.VMEM((wide, width), BF),
+            pltpu.VMEM((2 * rows, width), BF),
+            pltpu.VMEM((2 * rows, width), BF),
+            pltpu.VMEM((2 * rows, wide), BF),
+            pltpu.VMEM((wide, 2 * rows), BF),
+            pltpu.VMEM((2 * rows, wide), BF),
+            pltpu.VMEM((rows, width), BF),
+            pltpu.VMEM((rows, width), BF),
+            pltpu.VMEM((rows, width), BF),
+            *odds(down_piece),
+            *odds(up_piece),
+            *sets(down_piece),
+            *sets(up_piece),
+            *nears(down_piece),
+            *nears(up_piece),
+            pltpu.SemaphoreType.DMA((moves,)),
+            pltpu.SemaphoreType.DMA((moves,)),
+            pltpu.SemaphoreType.DMA((4,)),
+            pltpu.SemaphoreType.REGULAR((2,)),
+        ],
+        compiler_params=pltpu.CompilerParams(
+            collective_id=3, has_side_effects=True, vmem_limit_bytes=LIMIT
+        ),
+        cost_estimate=pl.CostEstimate(
+            flops=26 << 30, bytes_accessed=40 << 20, transcendentals=0
+        ),
+    )(resid, gain[None, :], cot_pair, up_full, down_full)
+
+
+def recall_kernel(
+    decay_ref,
+    across_ref,
+    fold_ref,
+    docs_col,
+    docs_row,
+    scale_ref,
+    gain_ref,
+    qk_ref,
+    v_ref,
+    gate_ref,
+    unit_ref,
+    inverse_ref,
+    states_ref,
+    cos_ref,
+    sin_ref,
+    turned_ref,
+    branch_ref,
+    wo_ref,
+    far_ref,
+    up_ref,
+    down_ref,
+    grads,
+    wo_grad,
+    gains,
+    far_in,
+    up_in,
+    down_in,
+    branch,
+    out_weights,
+    back,
+    terms,
+    gathered,
+    folded,
+    dqk,
+    dv,
+    odd_out,
+    odd_in,
+    out_far,
+    in_far,
+    out_near,
+    in_near,
+    send,
+    recv,
+    load_sem,
+):
+    near = peers()
+    group_rows, cols = v_ref.shape
+    heads = cols // VAL
+    blocks = group_rows // SPAN
+    width = branch.shape[1]
+    part = width // 8
+    loads = [
+        pltpu.make_async_copy(branch_ref, branch, load_sem.at[0]),
+        pltpu.make_async_copy(wo_ref, out_weights, load_sem.at[1]),
+    ]
+    for load in loads:
+        load.start()
+    greet(*everyone())
+    moves = Moves(send, recv)
+    swaps = [
+        moves.go(far_ref, far_in, near["pair"]),
+        moves.go(up_ref, up_in, near["cross"]),
+        moves.go(down_ref, down_in, near["cross"]),
+    ]
+
+    def block_rows(b):
+        return pl.ds(pl.multiple_of(b * SPAN, SPAN), SPAN)
+
+    def q_cols(h):
+        return pl.ds(h * KEY, KEY)
+
+    def k_cols(h):
+        return pl.ds((heads + h) * KEY, KEY)
+
+    def v_cols(h):
+        return pl.ds(h * VAL, VAL)
+
+    for load in loads:
+        load.wait()
+
+    def tile_back(i, totals):
+        at = pl.ds(pl.multiple_of(i * 128, 128), 128)
+        sums = []
+        for h in range(heads):
+            grad = dot_nt(branch[at, :], out_weights[v_cols(h), :]).astype(BF).astype(F32)
+            gate = gate_ref[at, v_cols(h)].astype(F32)
+            sigma = 1.0 / (1.0 + jnp.exp(-gate))
+            swish = gate * sigma
+            unit = unit_ref[at, v_cols(h)].astype(F32)
+            gain = gain_ref[:, h * VAL : (h + 1) * VAL]
+            grads[at, pl.ds(2 * heads * KEY + cols + h * VAL, VAL)] = (
+                grad * unit * gain * (sigma + swish * (1.0 - sigma))
+            ).astype(BF)
+            inner = grad * swish
+            scaled = inner * gain
+            first = jnp.mean(scaled, axis=-1, keepdims=True)
+            second = jnp.mean(scaled * unit, axis=-1, keepdims=True)
+            back[at, v_cols(h)] = (
+                inverse_ref[at, h : h + 1] * (scaled - first - unit * second)
+            ).astype(BF)
+            sums.append(totals[h] + jnp.sum(inner * unit, axis=0, keepdims=True))
+        return tuple(sums)
+
+    totals = lax.fori_loop(
+        0, group_rows // 128, tile_back, tuple(jnp.zeros((1, VAL), F32) for _ in range(heads))
+    )
+    gains[...] = jnp.zeros_like(gains)
+    for h in range(heads):
+        gains[pl.ds(0, 1), v_cols(h)] = totals[h]
+
+    for h in range(heads):
+        total = jnp.zeros((KEY, VAL), F32)
+        for b in reversed(range(blocks)):
+            weighed = back[block_rows(b), v_cols(h)].astype(F32) * scale_ref[
+                block_rows(b), h : h + 1
+            ]
+            term = dot_tn(qk_ref[block_rows(b), q_cols(h)], weighed.astype(BF))
+            terms[b, pl.ds(h * KEY, KEY), :] = term
+            total = across_ref[h, b] * total + term
+        gathered[0, pl.ds(h * KEY, KEY), :] = total.astype(BF)
+
+    def state_view(r, side=None):
+        if side is None:
+            return gathered.at[r]
+        size = gathered.shape[1] // 2
+        return gathered.at[r, pl.ds(side * size, size), :]
+
+    states = Gather(moves, near, state_view)
+    states.first()
+
+    def out_term(r):
+        return dot_nn(turned_ref[...], branch[:, r * part : (r + 1) * part])
+
+    outward = Scatter(
+        moves, near, out_term, (odd_out, odd_in, out_far, in_far, out_near, in_near), wo_grad
+    )
+
+    def intra(h):
+        @pl.loop(0, blocks)
+        def _(b):
+            first = pl.multiple_of(b * SPAN, SPAN)
+            for tile in range(SPAN - 128, -1, -128):
+                at = pl.ds(first + tile, 128)
+                seen = pl.ds(first, tile + 128)
+                mask = tile_decay(docs_col, docs_row, decay_ref[h], first, tile, 128)
+                query = qk_ref[at, q_cols(h)]
+                key = qk_ref[seen, k_cols(h)]
+                ret = back[at, v_cols(h)]
+                probs = (dot_nt(query, key) * mask).astype(BF)
+                score = (dot_nt(ret, v_ref[seen, v_cols(h)]) * mask).astype(BF)
+                dqk[at, q_cols(h)] = dot_nn(score, key)
+                to_keys = dot_tn(score, query)
+                to_values = dot_tn(probs, ret)
+                if tile == SPAN - 128:
+                    dqk[seen, k_cols(h)] = to_keys
+                    dv[seen, v_cols(h)] = to_values
+                else:
+                    dqk[seen, k_cols(h)] += to_keys
+                    dv[seen, v_cols(h)] += to_values
+
+    def finish_head(h):
+        later = jnp.zeros((KEY, VAL), F32)
+        for r in range(8):
+            later = later + fold_ref[h, r] * gathered[r, pl.ds(h * KEY, KEY), :].astype(F32)
+        for b in reversed(range(blocks)):
+            folded[b] = later.astype(BF)
+            later = across_ref[h, b] * later + terms[b, pl.ds(h * KEY, KEY), :]
+
+        @pl.loop(0, group_rows // 128)
+        def _(i):
+            at = pl.ds(pl.multiple_of(i * 128, 128), 128)
+            b = lax.div(i, SPAN // 128)
+            reach = scale_ref[at, h : h + 1]
+            leave = scale_ref[at, heads + h : heads + h + 1]
+            state = states_ref[pl.ds(pl.multiple_of((h * blocks + b) * KEY, KEY), KEY), :]
+            cosine, sine = cos_ref[at, :], sin_ref[at, :]
+            for found, to in (
+                (
+                    dqk[at, q_cols(h)] + reach * dot_nt(back[at, v_cols(h)], state),
+                    q_cols(h),
+                ),
+                (
+                    dqk[at, k_cols(h)] + leave * dot_nt(v_ref[at, v_cols(h)], folded[b]),
+                    k_cols(h),
+                ),
+            ):
+                one, two = found[:, : KEY // 2], found[:, KEY // 2 :]
+                grads[at, to] = jnp.concatenate(
+                    [one * cosine + two * sine, two * cosine - one * sine], axis=1
+                ).astype(BF)
+            found = dv[at, v_cols(h)] + leave * dot_nn(qk_ref[at, k_cols(h)], folded[b])
+            grads[at, pl.ds(2 * heads * KEY + h * VAL, VAL)] = found.astype(BF)
+
+    for i in (3, 1):
+        outward.odd(i)
+    intra(0)
+    states.second()
+    for i in (2, 0):
+        outward.odd(i)
+    for h in range(1, heads):
+        intra(h)
+    states.third()
+    outward.far()
+    states.done()
+    finish_head(0)
+    outward.close()
+    for h in range(1, heads):
+        finish_head(h)
+    outward.done()
+    for swap_ in swaps:
+        swap_.wait_recv()
+    moves.finish()
+
+
+def recall(
+    decay, across, fold, docs, scales, gain, qk, v, gate, unit, inverse, states, cosine, sine,
+    mixed_turned, branch, out_full, far_out, up_far, down_far,
+):
+    group_rows, cols = v.shape
+    heads = cols // VAL
+    blocks = group_rows // SPAN
+    width = branch.shape[1]
+    part = width // 8
+    piece = (cols, part)
+    moves = 3 + 8 + 8
+    struct = jax.ShapeDtypeStruct
+    return pl.pallas_call(
+        recall_kernel,
+        out_shape=(
+            struct((group_rows, 3 * cols), BF),
+            struct(piece, F32),
+            struct((8, cols), F32),
+            struct(far_out.shape, BF),
+            struct(up_far.shape, BF),
+            struct(down_far.shape, BF),
+        ),
+        in_specs=[SMEM] * 3 + [VMEM] * 13 + [ANY] * 5,
+        out_specs=[VMEM] * 3 + [ANY] * 3,
+        scratch_shapes=[
+            pltpu.VMEM(branch.shape, BF),
+            pltpu.VMEM(out_full.shape, BF),
+            pltpu.VMEM(v.shape, BF),
+            pltpu.VMEM((blocks, heads * KEY, VAL), F32),
+            pltpu.VMEM((8, heads * KEY, VAL), BF),
+            pltpu.VMEM((blocks, KEY, VAL), BF),
+            pltpu.VMEM((group_rows, 2 * heads * KEY), F32),
+            pltpu.VMEM((group_rows, cols), F32),
+            pltpu.VMEM((4,) + piece, BF),
+            pltpu.VMEM((4,) + piece, BF),
+            pltpu.VMEM(piece, BF),
+            pltpu.VMEM((2, cols // 2, part), BF),
+            pltpu.VMEM((2,) + piece, BF),
+            pltpu.VMEM((2,) + piece, BF),
+            pltpu.SemaphoreType.DMA((moves,)),
+            pltpu.SemaphoreType.DMA((moves,)),
+            pltpu.SemaphoreType.DMA((2,)),
+        ],
+        compiler_params=pltpu.CompilerParams(
+            collective_id=4, has_side_effects=True, vmem_limit_bytes=LIMIT
+        ),
+        cost_estimate=pl.CostEstimate(
+            flops=20 << 30, bytes_accessed=40 << 20, transcendentals=0
+        ),
+    )(
+        decay, across, fold, docs[:, None], docs[None, :], scales, gain[None, :], qk, v, gate, unit,
+        inverse, states, cosine, sine, mixed_turned, branch, out_full, far_out, up_far, down_far,
+    )
 
 
 def norm_forward(values, gain):
@@ -798,7 +1750,7 @@
     )
 
 
-def local(
+def plain(
     tokens,
     cotangent,
     doc_lengths,
@@ -849,25 +1801,19 @@
     ranks = lax.dynamic_slice_in_dim(head_order, z * heads, heads)
     log_decay = jnp.log1p(-jnp.exp2(-(5.0 + ranks.astype(F32))))
 
-    if paired():
-        turned, qkvg_full, out_full, qk_rows, v_rows, gate = enter(
-            tokens, gain1, cosine, sine, w_query, w_key, w_value, w_gate, w_out
-        )
-        gate = gate.astype(F32)
-    else:
-        group = head_gather(normed1.astype(BF))
-        qkvg_full = tok_gather(jnp.concatenate([w_query, w_key, w_value, w_gate], axis=1), 0)
-        out_full = tok_gather(w_out, 1)
-        projected = mm(group, qkvg_full)
-        qk_rows = jnp.concatenate(
-            [
-                rotate(projected[:, h * KEY : (h + 1) * KEY], cosine, sine).astype(BF)
-                for h in range(2 * heads)
-            ],
-            axis=1,
-        )
-        v_rows = projected[:, 2 * qk : 2 * qk + vg].astype(BF)
-        gate = projected[:, 2 * qk + vg :]
+    group = head_gather(normed1.astype(BF))
+    qkvg_full = tok_gather(jnp.concatenate([w_query, w_key, w_value, w_gate], axis=1), 0)
+    out_full = tok_gather(w_out, 1)
+    projected = mm(group, qkvg_full)
+    qk_rows = jnp.concatenate(
+        [
+            rotate(projected[:, h * KEY : (h + 1) * KEY], cosine, sine).astype(BF)
+            for h in range(2 * heads)
+        ],
+        axis=1,
+    )
+    v_rows = projected[:, 2 * qk : 2 * qk + vg].astype(BF)
+    gate = projected[:, 2 * qk + vg :]
 
     def head_of(array, head, size):
         return array[:, head * size : (head + 1) * size]
@@ -996,12 +1942,7 @@
         ret_grad.append(back.astype(BF))
         group_gain_parts.append(gain_term)
     gate_grad = jnp.concatenate(gate_parts, axis=1)
-    if paired():
-        w_gate_grad = tok_scatter(
-            [mm(turned[r * part : (r + 1) * part], gate_grad) for r in slots]
-        )
-    else:
-        w_gate_grad = tok_scatter([mm_tn(piece(group, r), gate_grad) for r in slots])
+    w_gate_grad = tok_scatter([mm_tn(piece(group, r), gate_grad) for r in slots])
 
     pending_of, pending_terms = [], []
     for h in range(heads):
@@ -1045,32 +1986,17 @@
     all_grad = jnp.concatenate(q_parts + k_parts + v_parts + [gate_grad], axis=1)
     group_terms = jnp.concatenate(group_gain_parts, axis=0)
     ffn_terms = reorder(ffn_gain_local)
-    if paired():
-        sums = jnp.concatenate(
-            [
-                jnp.zeros((1, width), F32),
-                ffn_terms[None, :],
-                jnp.concatenate([group_terms, jnp.zeros((width - vg,), F32)])[None, :],
-                jnp.zeros((5, width), F32),
-            ],
-            axis=0,
-        )
-        tokens_grad, w_query_grad, w_key_grad, w_value_grad, sums = depart(
-            all_grad, qkvg_full, turned, tokens, resid_grad, gain1, sums
-        )
-        norm_sum, ffn_sum, group_gain_grad = sums[0], sums[1], sums[2, :vg]
-    else:
-        row_grad = head_scatter(lambda i: mm_nt(rows_of(all_grad, i, rows), qkvg_full))
-        input_part, norm_gain_local = norm_backward(row_grad, unit1, inverse1, gain1)
-        tokens_grad = reorder(resid_grad + input_part)
-        qkv_grad = all_grad[:, : 2 * qk + vg]
-        w_qkv_grad = tok_scatter([mm_tn(piece(group, r), qkv_grad) for r in slots])
-        w_query_grad = w_qkv_grad[:, :qk]
-        w_key_grad = w_qkv_grad[:, qk : 2 * qk]
-        w_value_grad = w_qkv_grad[:, 2 * qk :]
-        group_gain_grad = sum_small(group_terms, "tok")
-        ffn_sum = sum_small(sum_small(ffn_terms, "tok"), "head")
-        norm_sum = sum_small(sum_small(reorder(norm_gain_local), "tok"), "head")
+    row_grad = head_scatter(lambda i: mm_nt(rows_of(all_grad, i, rows), qkvg_full))
+    input_part, norm_gain_local = norm_backward(row_grad, unit1, inverse1, gain1)
+    tokens_grad = reorder(resid_grad + input_part)
+    qkv_grad = all_grad[:, : 2 * qk + vg]
+    w_qkv_grad = tok_scatter([mm_tn(piece(group, r), qkv_grad) for r in slots])
+    w_query_grad = w_qkv_grad[:, :qk]
+    w_key_grad = w_qkv_grad[:, qk : 2 * qk]
+    w_value_grad = w_qkv_grad[:, 2 * qk :]
+    group_gain_grad = sum_small(group_terms, "tok")
+    ffn_sum = sum_small(sum_small(ffn_terms, "tok"), "head")
+    norm_sum = sum_small(sum_small(reorder(norm_gain_local), "tok"), "head")
     return (
         layer_out,
         tokens_grad,
@@ -1085,6 +2011,117 @@
         w_up_grad,
         w_down_grad,
     )
+
+
+def fused(
+    tokens,
+    cotangent,
+    doc_lengths,
+    head_order,
+    norm_gain,
+    w_query,
+    w_key,
+    w_value,
+    w_gate,
+    group_gain,
+    w_out,
+    ffn_gain,
+    w_up,
+    w_down,
+):
+    heads = w_query.shape[1] // KEY
+    head_count = lax.axis_size("head")
+    tok_count = lax.axis_size("tok")
+    z = lax.axis_index("head")
+    tok = lax.axis_index("tok")
+    rows = tokens.shape[0]
+    group_rows = rows * head_count
+    qk = w_query.shape[1]
+    vg = w_value.shape[1]
+
+    gain1 = reorder(norm_gain)
+    gain2 = reorder(ffn_gain)
+
+    ends = jnp.cumsum(doc_lengths)
+    starts = ends - doc_lengths
+    first_row = tok * group_rows
+    row_ids = first_row + jnp.arange(group_rows, dtype=jnp.int32)
+    doc_ids = doc_index(row_ids, starts)
+    cosine, sine = angles(doc_position(row_ids, starts), KEY // 2)
+    ranks = lax.dynamic_slice_in_dim(head_order, z * heads, heads)
+    log_decay = jnp.log1p(-jnp.exp2(-(5.0 + ranks.astype(F32))))
+    place = row_ids % SPAN
+    block_first = row_ids - place
+    before = doc_index(block_first - 1, starts)
+    last = doc_index(block_first + SPAN - 1, starts)
+    reach = jnp.where(
+        (doc_ids == before)[:, None], jnp.exp((place + 1).astype(F32)[:, None] * log_decay), 0.0
+    )
+    leave = jnp.where(
+        (doc_ids == last)[:, None],
+        jnp.exp((SPAN - 1 - place).astype(F32)[:, None] * log_decay),
+        0.0,
+    )
+    scales = jnp.concatenate([reach, leave], axis=1)
+    across = jnp.where(
+        (before[::SPAN] == last[::SPAN])[None, :], jnp.exp(SPAN * log_decay)[:, None], 0.0
+    )
+    order = jnp.arange(tok_count, dtype=jnp.int32) ^ tok
+
+    def weigh(lag, same):
+        return jnp.where(
+            ((lag >= 0) & same)[None, :],
+            jnp.exp(jnp.maximum(lag, 0).astype(F32) * group_rows * log_decay[:, None]),
+            0.0,
+        )
+
+    fold = weigh(
+        tok - 1 - order, doc_index((order + 1) * group_rows - 1, starts) == before[0]
+    )
+    fold_back = weigh(
+        order - 1 - tok, doc_index(order * group_rows - 1, starts) == doc_ids[-1]
+    )
+
+    turned, qkvg_full, out_full, qk_rows, v_rows, gate = enter(
+        tokens, gain1, cosine, sine, w_query, w_key, w_value, w_gate, w_out
+    )
+    resid, unit_g, inverse_g, states, cot_pair, mixed_turned, up_full, down_full = retain(
+        log_decay, across, fold, doc_ids, scales, group_gain, qk_rows, v_rows, gate, tokens,
+        out_full, cotangent, w_up, w_down,
+    )
+    (
+        layer_own, far_out, resid_grad, ffn_gain_parts, up_own, up_far, down_own, down_far, branch
+    ) = feed_forward(resid, gain2, cot_pair, up_full, down_full)
+    all_grad, w_out_grad, group_terms, far_in, up_in, down_in = recall(
+        log_decay, across, fold_back, doc_ids, scales, group_gain, qk_rows, v_rows, gate, unit_g,
+        inverse_g, states, cosine, sine, mixed_turned, branch, out_full, far_out,
+        up_far.astype(BF), down_far.astype(BF),
+    )
+    layer_out = reorder((layer_own + far_in.astype(F32)).astype(BF))
+    w_up_grad = up_own + up_in.astype(F32)
+    w_down_grad = down_own + down_in.astype(F32)
+    tokens_grad, w_qk_grad, w_value_grad, w_gate_grad, sums = depart(
+        all_grad, qkvg_full, turned, tokens, resid_grad, gain1, ffn_gain_parts, group_terms
+    )
+    w_query_grad, w_key_grad = w_qk_grad[:, :qk], w_qk_grad[:, qk:]
+    return (
+        layer_out,
+        tokens_grad,
+        sums[0],
+        w_query_grad,
+        w_key_grad,
+        w_value_grad,
+        w_gate_grad,
+        sums[2, :vg],
+        w_out_grad,
+        sums[1],
+        w_up_grad,
+        w_down_grad,
+    )
+
+
+def local(*arrays):
+    return fused(*arrays) if paired() else plain(*arrays)
 
 
 def solution(mesh):

time: 867 us -> 623 us (0.72)
  Pallas kernels: 204 us -> 571 us
  waiting for transfers between devices: 259 us -> 0 us
  matrix products: 158 us -> 0 us
  other arithmetic: 78.2 us -> 14.9 us
  local copies, waits for them, and re-layouts: 84.3 us -> 25.6 us
  starting transfers between devices: 54.6 us -> 0 us
  between operations: 22.2 us -> 1.41 us
    pallas_call x0 -> x3, Pallas kernels: none -> 358 us  [the longest x1 147 us: retain(): pl.pallas_call(retain_kernel, out_shape=(struct((rows, width), F32), stru...]
    ppermute x62 -> x0, waiting for transfers between devices: 259 us -> none  [the longest x56 178 us: swap(): return lax.ppermute(array, axis, [(i, i ^ bit) for i in range(count)])]
    dot_general x91 -> x0, matrix products: 158 us -> none  [the longest x40 57.4 us: mm_tn(): lax.dot_general(left, right, (((0,), (0,)), ((), ())), preferred_element_...]
    ppermute x62 -> x0, starting transfers between devices: 54.3 us -> none  [the longest x56 46.7 us: swap(): return lax.ppermute(array, axis, [(i, i ^ bit) for i in range(count)])]
    unnamed x311 -> x56, local copies, waits for them, and re-layouts: 57.6 us -> 16.7 us
    unnamed x15 -> x2, other arithmetic: 30.1 us -> 0.01 us
    reduce_sum x9 -> x0, other arithmetic: 12.6 us -> none  [the longest x1 3.67 us: norm_backward(): jnp.sum(grad_out * unit, axis=0)]
    pallas_call x1, Pallas kernels: 100 us -> 109 us  [depart(): pl.pallas_call(leave_kernel, out_shape=(jax.ShapeDtypeStruct((rows, width...]
  transfers between devices with their start and end apart: 64 -> 0, of which waited for: 23 -> 0; matrix products, arithmetic and copies ran while one was open for 25% -> 0% of each run, Pallas kernels for 12% -> 0%
where the time goes in v3:
time: 623 us; the launch traced here: 613 us
  Pallas kernels  571 us (92%)
  local copies, waits for them, and re-layouts  25.6 us (4%)
  other arithmetic  14.9 us (2%)
    pallas_call x1, Pallas kernels, retain(): pl.pallas_call(retain_kernel, out_shape=(struct((rows, width), F32), stru...  147 us
    pallas_call x1, Pallas kernels, feed_forward(): pl.pallas_call(feed_kernel, out_shape=(struct((rows, width), F32), struct...  145 us
    pallas_call x1, Pallas kernels, depart(): pl.pallas_call(leave_kernel, out_shape=(jax.ShapeDtypeStruct((rows, width...  109 us
    pallas_call x1, Pallas kernels, enter(): pl.pallas_call(enter_kernel, out_shape=(jax.ShapeDtypeStruct((width, grou...  103 us
    pallas_call x1, Pallas kernels, recall(): pl.pallas_call(recall_kernel, out_shape=(struct((group_rows, 3 * cols), B...  67 us
    unnamed x56, local copies, waits for them, and re-layouts  16.7 us

profile of v3, /device:TPU:0, one launch (start us, length us, event | category | flops | bytes accessed | tf_op | source)
XLA Modules:
  0.0 613.0 jit_solution(8653556881307275913)
XLA Ops:
  0.7 0.8 reduce-window.9
  1.5 0.7 bitcast_subtract_fusion
  2.3 0.7 multiply_exponential_fusion.1
  3.1 0.1 fusion.1
  3.3 0.6 slice.30
  3.9 0.5 slice.29
  4.5 1.3 compare_and_fusion
  5.8 0.1 slice.28
  5.9 0.6 broadcast_select_fusion.across_ref
  6.5 0.6 exponential_select_fusion.2
  7.2 0.8 constant_dynamic-update-slice_fusion
  8.0 0.8 constant_dynamic-update-slice_fusion.14
  8.7 0.8 constant_dynamic-update-slice_fusion.12
  9.5 0.8 constant_dynamic-update-slice_fusion.10
  10.3 0.8 constant_dynamic-update-slice_fusion.8
  11.0 0.8 constant_dynamic-update-slice_fusion.6
  11.8 0.8 constant_dynamic-update-slice_fusion.4
  12.6 0.8 constant_dynamic-update-slice_fusion.2
  13.3 0.8 constant_dynamic-update-slice_fusion.15
  14.1 0.8 constant_dynamic-update-slice_fusion.13
  14.9 0.8 constant_dynamic-update-slice_fusion.11
  15.6 0.8 constant_dynamic-update-slice_fusion.9
  16.4 0.8 constant_dynamic-update-slice_fusion.7
  17.2 0.8 constant_dynamic-update-slice_fusion.5
  17.9 0.8 constant_dynamic-update-slice_fusion.3
  18.8 1.0 copy.33.scale_ref
  19.8 1.0 copy.32.docs_col
  20.9 3.0 multiply_sine_fusion
  23.9 103.5 %shard_map.229 = (bf16[2048,1024]{1,0:T(8,128)(2,1)}, bf16[2048,3072]{1,0:T(8,128)(2,1)}, bf16[1024,2048]{1,0:T(8,128)(2,1)}, bf16[1024,1024]{1,0:T(8,128)(2,1)}...) custom-call(bf16[256,2048]{1,0:T(8,128)(2,1)} %tok_ref.5, f32[1,2048]{1,0:T(1,128)} %bitcast.19, ...), custom_call_target="tpu_custom_call" | custom-call | flops 12884901888 | bytes 41943040 | tf_op jit(solution)/shard_map/pallas_call | solution.py:434
  127.4 146.8 %shard_map.230 = (f32[256,2048]{1,0:T(8,128)}, bf16[1024,1024]{1,0:T(8,128)(2,1)}, f32[1024,2]{1,0:T(8,128)}, bf16[1024,512]{1,0:T(8,128)(2,1)}, bf16[512,2048]{...) custom-call(f32[2]{0:T(128)} %copy-done.13, ...), custom_call_target="tpu_custom_call" | custom-call | flops 12884901888 | bytes 41943040 | tf_op jit(solution)/shard_map/pallas_call | solution.py:1067
  274.2 144.7 %shard_map.231 = (f32[256,2048]{1,0:T(8,128)}, bf16[256,2048]{1,0:T(8,128)(2,1)}, f32[256,2048]{1,0:T(8,128)}, f32[8,2048]{1,0:T(8,128)}, f32[256,1024]{1,0:T(8,...) custom-call(f32[256,2048]{1,0:T(8,128)} %get-tuple-element.50.resid_ref, ...), custom_call_target="tpu_custom_call" | custom-call | flops 27917287424 | bytes 41943040 | tf_op jit(solution)/shard_map/pallas_call | solution.py:1374
  418.9 2.2 convert_element_type.82.up_ref
  421.1 0.8 convert_element_type.83.down_ref
  421.9 67.0 %shard_map.232 = (bf16[1024,3072]{1,0:T(8,128)(2,1)}, f32[1024,256]{1,0:T(8,128)}, f32[8,1024]{1,0:T(8,128)}, bf16[256,2048]{1,0:T(8,128)(2,1)}, bf16[256,1024]{1,0:T(8,128)(2,1)}, /*index=5*/bf16[1024,256]{1,0:T(8,128)(2,1)}) custom-call(f32[2]{0:T(128)} %copy-done.13, f32[2,2]{1,0:T(2,128)} %broadcast_select_fusion.across_ref, ...), custom_call_target="tpu_custom_call" | custom-call | flops 21474836480 | bytes 41943040 | tf_op jit(solution)/shard_map/pallas_call | solution.py:1647
  488.9 2.2 convert_add_fusion
  491.2 1.1 convert_add_fusion.1
  492.3 109.2 %shard_map.233 = (f32[256,2048]{1,0:T(8,128)}, f32[256,1024]{1,0:T(8,128)}, f32[256,1024]{1,0:T(8,128)}, f32[256,1024]{1,0:T(8,128)}, f32[8,2048]{1,0:T(8,128)}) custom-call(bf16[1024,3072]{1,0:T(8,128)(2,1)} %get-tuple-element.64.grads_ref, bf16[2048,3072]{1,0:T(8,128)(2,1)} %get-tuple-element.65.weights_ref, ...), custom_call_target="tpu_custom_call" | custom-call | flops 21474836480 | bytes 41943040 | tf_op jit(solution)/shard_map/pallas_call | solution.py:734
  601.5 0.3 add_convert_fusion
  601.8 1.4 slice.34
  603.3 1.5 fusion.13
  605.1 1.0 fusion.12
  606.1 1.0 copy-done.1
  607.2 1.3 copy.63
  608.5 0.6 copy-done.5
  609.1 1.0 copy.64
  610.1 0.6 copy-done.4
  610.7 1.0 copy.65
  611.7 1.0 copy.66
  (57 shorter events, 0.7 us)
Async XLA Ops:
  3.0 124.3 %copy-start.13 = (f32[2]{0:T(128)}, f32[2]{0:T(128)S(1)}, u32[]{:S(2)}) copy-start(f32[2]{0:T(128)S(1)} %get-tuple-element.87.decay_ref) | copy-start | bytes 28
  3.3 124.1 %copy-start.11 = (s32[1024]{0:T(1024)}, s32[1024]{0:T(1024)S(1)}, u32[]{:S(2)}) copy-start(s32[1024]{0:T(1024)S(1)} %broadcast_add_fusion) | copy-start | bytes 12292
  13.3 10.5 %copy-start.14 = (f32[2048]{0:T(1024)}, f32[2048]{0:T(1024)S(1)}, u32[]{:S(2)}) copy-start(f32[2048]{0:T(1024)S(1)} %constant_dynamic-update-slice_fusion.2) | copy-start | bytes 24580
  18.7 108.7 %copy-start.15 = (f32[2048]{0:T(1024)}, f32[2048]{0:T(1024)S(1)}, u32[]{:S(2)}) copy-start(f32[2048]{0:T(1024)S(1)} %constant_dynamic-update-slice_fusion.3) | copy-start | bytes 24580
  418.9 2.2 copy-start.2
  421.9 67.0 %copy-start.8 = (f32[1024,256]{1,0:T(8,128)S(1)}, f32[1024,256]{1,0:T(8,128)}, u32[]{:S(2)}) copy-start(f32[1024,256]{1,0:T(8,128)} %get-tuple-element.78) | copy-start | bytes 3145732
  488.9 2.3 copy-start.7
  488.9 2.3 copy-start.10
  492.3 109.2 %copy-start = (f32[256,2048]{1,0:T(8,128)S(1)}, f32[256,2048]{1,0:T(8,128)}, u32[]{:S(2)}) copy-start(f32[256,2048]{1,0:T(8,128)} %get-tuple-element.54) | copy-start | bytes 6291460
  492.3 109.3 %copy-start.9 = (bf16[256,2048]{1,0:T(8,128)(2,1)S(1)}, bf16[256,2048]{1,0:T(8,128)(2,1)}, u32[]{:S(2)}) copy-start(bf16[256,2048]{1,0:T(8,128)(2,1)} %get-tuple-element.63) | copy-start | bytes 3145732
  601.8 3.3 copy-start.6
  604.8 2.3 copy-start.1
  605.1 3.4 copy-start.12
  607.1 2.0 copy-start.5
  609.1 1.6 copy-start.4
  609.1 2.6 copy-start.3

commit v4 on v3

--- a/solution.py
+++ b/solution.py
@@ -134,6 +134,7 @@
 MESH = pl.DeviceIdType.MESH
 ANY = pl.BlockSpec(memory_space=pl.ANY)
 VMEM = pl.BlockSpec(memory_space=pltpu.VMEM)
+SMEM = pl.BlockSpec(memory_space=pltpu.SMEM)
 LIMIT = 60 * 1024 * 1024
 
 
@@ -172,6 +173,85 @@
     pl.semaphore_wait(barrier, len(devices))
 
 
+def doc_starts(lengths):
+    starts, total = [], 0
+    for d in range(lengths.shape[0]):
+        starts.append(total)
+        total = total + lengths[d]
+    return starts
+
+
+def doc_at(row, starts):
+    return sum((start <= row).astype(jnp.int32) for start in starts) - 1
+
+
+def doc_first(row, starts):
+    first = jnp.zeros_like(row)
+    for start in starts:
+        first = jnp.maximum(first, jnp.where(start <= row, start, 0))
+    return first
+
+
+def decays(order, heads):
+    z = lax.axis_index("head")
+    found = []
+    for h in range(heads):
+        rank = jnp.full((1, 1), order[z * heads + h], jnp.int32).astype(F32)
+        found.append(jnp.log1p(-jnp.exp2(-(5.0 + rank))))
+    return found
+
+
+def block_scales(lengths, log_decay, group_rows, scale, docs):
+    heads = len(log_decay)
+    starts = doc_starts(lengths)
+    first_row = lax.axis_index("tok") * group_rows
+    across = [[] for _ in range(heads)]
+    for b in range(group_rows // SPAN):
+        at = pl.ds(b * SPAN, SPAN)
+        low = first_row + b * SPAN
+        place = lax.broadcasted_iota(jnp.int32, (SPAN, 1), 0)
+        doc = doc_at(low + place, starts)
+        docs[at, :] = doc
+        before = doc_at(low - 1, starts)
+        last = doc_at(low + SPAN - 1, starts)
+        where = place.astype(F32)
+        for h in range(heads):
+            scale[at, h : h + 1] = jnp.where(
+                doc == before, jnp.exp((where + 1.0) * log_decay[h]), 0.0
+            )
+            scale[at, heads + h : heads + h + 1] = jnp.where(
+                doc == last, jnp.exp((SPAN - 1.0 - where) * log_decay[h]), 0.0
+            )
+            across[h].append(jnp.where(last == before, jnp.exp(SPAN * log_decay[h]), 0.0))
+    return across
+
+
+def row_docs(lengths, group_rows):
+    starts = doc_starts(lengths)
+    first_row = lax.axis_index("tok") * group_rows
+    return doc_at(first_row + lax.broadcasted_iota(jnp.int32, (8, group_rows), 1), starts)
+
+
+def group_weights(lengths, log_decay, group_rows, backward):
+    starts = doc_starts(lengths)
+    tok = lax.axis_index("tok")
+    first_row = tok * group_rows
+    found = [[] for _ in log_decay]
+    for other in xor_places(tok):
+        if backward:
+            lag = other - 1 - tok
+            same = doc_at(other * group_rows - 1, starts) == doc_at(
+                first_row + group_rows - 1, starts
+            )
+        else:
+            lag = tok - 1 - other
+            same = doc_at((other + 1) * group_rows - 1, starts) == doc_at(first_row - 1, starts)
+        amount = (jnp.maximum(lag, 0) * group_rows).astype(F32)
+        for h, rate in enumerate(log_decay):
+            found[h].append(jnp.where((lag >= 0) & same, jnp.exp(amount * rate), 0.0))
+    return found
+
+
 class Moves:
     def __init__(self, send, recv):
         self.send, self.recv, self.made, self.over = send, recv, [], []
@@ -233,8 +313,7 @@
 def enter_kernel(
     tok_ref,
     gain_ref,
-    cos_ref,
-    sin_ref,
+    lengths_ref,
     wq_ref,
     wk_ref,
     wv_ref,
@@ -246,9 +325,13 @@
     qk_out,
     v_out,
     gate_out,
+    cos_ref,
+    sin_ref,
     turned,
     group,
     weights,
+    own_out,
+    gain,
     send,
     recv,
     own_sem,
@@ -270,7 +353,7 @@
         ),
         pltpu.make_async_copy(wv_ref, weights.at[1, pl.ds(0, part), :], own_sem.at[2]),
         pltpu.make_async_copy(wg_ref, weights.at[2, pl.ds(0, part), :], own_sem.at[3]),
-        pltpu.make_async_copy(wo_ref, out_full.at[:, pl.ds(0, part)], own_sem.at[4]),
+        pltpu.make_async_copy(wo_ref, own_out, own_sem.at[4]),
     ]
     for copy in own:
         copy.start()
@@ -286,6 +369,8 @@
         return view
 
     def out_view(r, side=None):
+        if r == 0:
+            return own_out
         if side is None:
             return out_full.at[:, pl.ds(r * part, part)]
         size = out_full.shape[0] // 2
@@ -300,10 +385,13 @@
     chunks[1].first()
     own[3].wait()
     own[4].wait()
-
-    @pl.loop(0, rows // 32)
+    kept = [pltpu.make_async_copy(own_out, out_full.at[:, pl.ds(0, part)], keep_sem.at[4])]
+    kept[0].start()
+    gain[...] = arranged(gain_ref, tok)
+
+    @pl.loop(0, rows // 16)
     def _(i):
-        at = pl.ds(pl.multiple_of(i * 32, 32), 32)
+        at = pl.ds(pl.multiple_of(i * 16, 16), 16)
         values = jnp.concatenate(
             [
                 tok_ref[at, pl.ds(pl.multiple_of(place * part, part), part)]
@@ -314,8 +402,8 @@
         mean = jnp.mean(values, axis=-1, keepdims=True)
         centred = values - mean
         inverse = lax.rsqrt(jnp.mean(centred * centred, axis=-1, keepdims=True) + EPS)
-        lifted = (centred * inverse * gain_ref[...]).astype(BF)
-        group[pl.ds(pl.multiple_of(z * rows + i * 32, 32), 32), :] = lifted
+        lifted = (centred * inverse * gain[...]).astype(BF)
+        group[pl.ds(pl.multiple_of(z * rows + i * 16, 16), 16), :] = lifted
 
     def shard(step, side):
         owner = lax.rem(z - step + count, count)
@@ -361,8 +449,6 @@
             to = pl.ds(pl.multiple_of(owner * rows, rows), rows)
             turned[at, to] = group[to, at].T
 
-    kept = []
-
     def keep(c):
         copy = pltpu.make_async_copy(
             weights.at[c], weights_out.at[:, pl.ds(c * cols, cols)], keep_sem.at[c]
@@ -372,6 +458,19 @@
 
     pass_on(0, 0)
     pass_on(0, 1)
+    group_rows = rows * count
+    starts = doc_starts(lengths_ref)
+    index = lax.broadcasted_iota(jnp.int32, (1, KEY // 2), 1).astype(F32)
+    freq = jnp.exp(-jnp.log(10000.0) * index / (KEY // 2))
+
+    @pl.loop(0, group_rows // 64)
+    def _(i):
+        at = pl.ds(pl.multiple_of(i * 64, 64), 64)
+        row = tok * group_rows + i * 64 + lax.broadcasted_iota(jnp.int32, (64, KEY // 2), 0)
+        turn = (row - doc_first(row, starts)).astype(F32) * freq
+        cos_ref[at, :] = jnp.cos(turn)
+        sin_ref[at, :] = jnp.sin(turn)
+
     chunks[0].second()
     chunks[2].first()
     pass_on(1, 0)
@@ -415,6 +514,14 @@
     moves.finish()
 
 
+def arranged(ref, tok):
+    part = ref.shape[-1] // 8
+    return jnp.concatenate(
+        [ref[:, pl.ds(pl.multiple_of(place * part, part), part)] for place in xor_places(tok)],
+        axis=1,
+    )
+
+
 def xor_places(tok):
     places = []
     for r in range(8):
@@ -426,7 +533,7 @@
     return places
 
 
-def enter(tokens, gain, cosine, sine, w_query, w_key, w_value, w_gate, w_out):
+def enter(tokens, gain, doc_lengths, w_query, w_key, w_value, w_gate, w_out):
     rows, width = tokens.shape
     group_rows = rows * lax.axis_size("head")
     cols = w_value.shape[1]
@@ -440,17 +547,21 @@
             jax.ShapeDtypeStruct((group_rows, cols), BF),
             jax.ShapeDtypeStruct((group_rows, cols), BF),
             jax.ShapeDtypeStruct((group_rows, cols), BF),
+            jax.ShapeDtypeStruct((group_rows, KEY // 2), F32),
+            jax.ShapeDtypeStruct((group_rows, KEY // 2), F32),
         ),
-        in_specs=[VMEM] * 4 + [ANY] * 5,
-        out_specs=[ANY] * 3 + [VMEM] * 3,
+        in_specs=[VMEM] * 2 + [SMEM] + [ANY] * 5,
+        out_specs=[ANY] * 3 + [VMEM] * 5,
         scratch_shapes=[
             pltpu.VMEM((width, group_rows), BF),
             pltpu.VMEM((group_rows, width), BF),
             pltpu.VMEM((3, width, cols), BF),
+            pltpu.VMEM(w_out.shape, BF),
+            pltpu.VMEM((1, width), F32),
             pltpu.SemaphoreType.DMA((moves,)),
             pltpu.SemaphoreType.DMA((moves,)),
             pltpu.SemaphoreType.DMA((5,)),
-            pltpu.SemaphoreType.DMA((4,)),
+            pltpu.SemaphoreType.DMA((5,)),
         ],
         compiler_params=pltpu.CompilerParams(
             collective_id=0, has_side_effects=True, vmem_limit_bytes=LIMIT
@@ -458,7 +569,7 @@
         cost_estimate=pl.CostEstimate(
             flops=2 * group_rows * width * 3 * cols, bytes_accessed=40 << 20, transcendentals=0
         ),
-    )(tokens, gain[None, :], cosine, sine, w_query, w_key, w_value, w_gate, w_out)
+    )(tokens, gain[None, :], doc_lengths, w_query, w_key, w_value, w_gate, w_out)
 
 
 class Scatter:
@@ -523,6 +634,18 @@
         self.result[...] += self.near_in[0].astype(F32) + self.near_in[1].astype(F32)
 
 
+class Beside:
+    def __init__(self, left, right):
+        self.refs, self.size = (left, right), left.shape[1]
+
+    def __getitem__(self, index):
+        return jnp.concatenate([ref[...] for ref in self.refs], axis=1)
+
+    def __setitem__(self, index, value):
+        for i, ref in enumerate(self.refs):
+            ref[...] = value[:, i * self.size : (i + 1) * self.size]
+
+
 def leave_kernel(
     grads_ref,
     weights_ref,
@@ -533,7 +656,8 @@
     ffn_ref,
     group_ref,
     tokens_grad,
-    wqk_out,
+    wq_out,
+    wk_out,
     wv_out,
     wg_out,
     gains_out,
@@ -552,6 +676,7 @@
     gains,
     gains_in,
     gains_z,
+    gain,
     send,
     recv,
     load_sem,
@@ -563,13 +688,30 @@
     count = lax.axis_size("head")
     rows, width = tok_ref.shape
     part = width // 8
-    side_rows = rows // 2
+    gain[...] = arranged(gain_ref, tok)
     cols = wv_out.shape[1]
-    loads = [
-        pltpu.make_async_copy(grads_ref, grads, load_sem.at[0]),
-        pltpu.make_async_copy(weights_ref, weights, load_sem.at[1]),
-        pltpu.make_async_copy(turned_ref, turned, load_sem.at[2]),
+    strip = width // 4
+
+    def owned(step):
+        owner = lax.rem(z + 2 * count - 1 - step, count)
+        return pl.ds(pl.multiple_of(owner * rows, rows), rows)
+
+    grad_loads = [
+        pltpu.make_async_copy(
+            grads_ref.at[owned(step), :], grads.at[owned(step), :], load_sem.at[step]
+        )
+        for step in range(count)
     ]
+    strip_loads = [
+        pltpu.make_async_copy(
+            weights_ref.at[pl.ds(n * strip, strip), :],
+            weights.at[pl.ds(n * strip, strip), :],
+            load_sem.at[count + n],
+        )
+        for n in range(4)
+    ]
+    turned_load = pltpu.make_async_copy(turned_ref, turned, load_sem.at[count + 4])
+    loads = [grad_loads[0], *strip_loads, *grad_loads[1:], turned_load]
     for load in loads:
         load.start()
     others = [
@@ -578,28 +720,24 @@
     greet(near["core"], near["x"], near["y"], *others)
     moves = Moves(send, recv)
 
-    def ring_term(step):
-        owner = lax.rem(z + 2 * count - 1 - step, count)
-        at = pl.ds(pl.multiple_of(owner * rows, rows), rows)
-
-        @pl.loop(0, width // 256)
+    def ring_term(step, side):
+        @pl.loop(side * (width // 512), (side + 1) * (width // 512))
         def _(i):
             to = pl.ds(pl.multiple_of(i * 256, 256), 256)
-            held[:, to] = lax.dot_general(
-                grads[at, :], weights[to, :], (((1,), (1,)), ((), ())), preferred_element_type=F32
-            )
+            held[:, to] = dot_nt(grads[owned(step), :], weights[to, :])
 
     ring = {}
+    half = width // 2
 
     def ring_send(step, side):
-        at = pl.ds(side * side_rows, side_rows)
-        value = held[at, :]
+        at = pl.ds(side * half, half)
+        value = held[:, at]
         if step:
             ring[step - 1, side].wait_recv()
-            value = value + ring_in[step - 1, at, :].astype(F32)
-        ring_out[step, at, :] = value.astype(BF)
+            value = value + ring_in[step - 1, :, at].astype(F32)
+        ring_out[step, :, at] = value.astype(BF)
         ring[step, side] = moves.go(
-            ring_out.at[step, at, :], ring_in.at[step, at, :], near["up"]
+            ring_out.at[step, :, at], ring_in.at[step, :, at], near["up"]
         )
 
     def chunk_term(c):
@@ -627,31 +765,36 @@
 
     scatters = [
         Scatter(moves, near, chunk_term(c), buffers(c), result)
-        for c, result in enumerate((wqk_out, wv_out))
+        for c, result in enumerate((Beside(wq_out, wk_out), wv_out))
     ]
     scatters.append(
         Scatter(moves, near, chunk_term(2), buffers(2), wg_out, scatters[0], free_sem)
     )
     scatters[0].frees = free_sem
 
-    loads[0].wait()
-    loads[1].wait()
-    ring_term(0)
-    ring_send(0, 0)
-    ring_send(0, 1)
-    loads[2].wait()
+    grad_loads[0].wait()
+    for side in range(2):
+        strip_loads[2 * side].wait()
+        strip_loads[2 * side + 1].wait()
+        ring_term(0, side)
+        ring_send(0, side)
+    for load in grad_loads[1:]:
+        load.wait()
+    turned_load.wait()
+    ring_term(1, 0)
+    ring_term(1, 1)
     for i in (3, 1, 2, 0):
         scatters[0].odd(i)
-    ring_term(1)
     ring_send(1, 0)
     scatters[0].far()
     for i in (3, 1):
         scatters[1].odd(i)
     ring_send(1, 1)
-    scatters[0].close()
     for i in (2, 0):
         scatters[1].odd(i)
-    ring_term(2)
+    ring_term(2, 0)
+    scatters[0].close()
+    ring_term(2, 1)
     ring_send(2, 0)
     scatters[1].far()
     for i in (3, 1):
@@ -662,7 +805,8 @@
         scatters[2].odd(i)
     scatters[0].done()
     scatters[2].far()
-    ring_term(3)
+    ring_term(3, 0)
+    ring_term(3, 1)
     scatters[1].done()
     scatters[2].close()
     scatters[2].done()
@@ -675,40 +819,32 @@
             ffn_ref[pl.ds(0, 1), r * part : (r + 1) * part]
             + ffn_ref[pl.ds(1, 1), r * part : (r + 1) * part]
         )
-    size = 32
+    size = 16
     for side in range(2):
         ring[2, side].wait_recv()
 
-        def block(i, total):
-            at = pl.ds(pl.multiple_of(side * side_rows + i * size, size), size)
-            values = jnp.concatenate(
-                [
-                    tok_ref[at, pl.ds(pl.multiple_of(place * part, part), part)]
-                    for place in xor_places(tok)
-                ],
-                axis=1,
-            ).astype(F32)
-            mean = jnp.mean(values, axis=-1, keepdims=True)
-            centred = values - mean
-            inverse = lax.rsqrt(jnp.mean(centred * centred, axis=-1, keepdims=True) + EPS)
-            unit = centred * inverse
-            grad = held[at, :] + ring_in[2, at, :].astype(F32)
-            scaled = grad * gain_ref[...]
-            first = jnp.mean(scaled, axis=-1, keepdims=True)
-            second = jnp.mean(scaled * unit, axis=-1, keepdims=True)
-            found = resid_ref[at, :] + inverse * (scaled - first - unit * second)
-            for r, place in enumerate(xor_places(tok)):
-                tokens_grad[at, pl.ds(pl.multiple_of(place * part, part), part)] = found[
-                    :, r * part : (r + 1) * part
-                ]
-            return total + jnp.sum(grad * unit, axis=0, keepdims=True)
-
-        total = lax.fori_loop(
-            0, side_rows // size, block, jnp.zeros((1, width), F32)
-        )
+    def block(i, total):
+        at = pl.ds(pl.multiple_of(i * size, size), size)
+        values = arranged(tok_ref.at[at, :], tok).astype(F32)
+        mean = jnp.mean(values, axis=-1, keepdims=True)
+        centred = values - mean
+        inverse = lax.rsqrt(jnp.mean(centred * centred, axis=-1, keepdims=True) + EPS)
+        unit = centred * inverse
+        grad = held[at, :] + ring_in[2, at, :].astype(F32)
+        scaled = grad * gain[...]
+        first = jnp.mean(scaled, axis=-1, keepdims=True)
+        second = jnp.mean(scaled * unit, axis=-1, keepdims=True)
+        found = resid_ref[at, :] + inverse * (scaled - first - unit * second)
         for r, place in enumerate(xor_places(tok)):
-            at = pl.ds(pl.multiple_of(place * part, part), part)
-            gains[pl.ds(0, 1), at] += total[:, r * part : (r + 1) * part]
+            tokens_grad[at, pl.ds(pl.multiple_of(place * part, part), part)] = found[
+                :, r * part : (r + 1) * part
+            ]
+        return total + jnp.sum(grad * unit, axis=0, keepdims=True)
+
+    total = lax.fori_loop(0, rows // size, block, jnp.zeros((1, width), F32))
+    for r, place in enumerate(xor_places(tok)):
+        at = pl.ds(pl.multiple_of(place * part, part), part)
+        gains[pl.ds(0, 1), at] = total[:, r * part : (r + 1) * part]
 
     for i, way in enumerate(("core", "x", "y")):
         move = moves.go(gains, gains_in.at[i], near[way])
@@ -735,13 +871,14 @@
         leave_kernel,
         out_shape=(
             jax.ShapeDtypeStruct((rows, width), F32),
-            jax.ShapeDtypeStruct((part, cols), F32),
+            jax.ShapeDtypeStruct((part, cols // 2), F32),
+            jax.ShapeDtypeStruct((part, cols // 2), F32),
             jax.ShapeDtypeStruct((part, cols), F32),
             jax.ShapeDtypeStruct((part, cols), F32),
             jax.ShapeDtypeStruct(sums, F32),
         ),
         in_specs=[ANY] * 3 + [VMEM] * 5,
-        out_specs=[VMEM] * 5,
+        out_specs=[VMEM] * 6,
         scratch_shapes=[
             pltpu.VMEM(grads.shape, BF),
             pltpu.VMEM(weights.shape, BF),
@@ -758,9 +895,10 @@
             pltpu.VMEM(sums, F32),
             pltpu.VMEM((3,) + sums, F32),
             pltpu.VMEM((count - 1,) + sums, F32),
+            pltpu.VMEM((1, width), F32),
             pltpu.SemaphoreType.DMA((moves,)),
             pltpu.SemaphoreType.DMA((moves,)),
-            pltpu.SemaphoreType.DMA((3,)),
+            pltpu.SemaphoreType.DMA((count + 5,)),
             pltpu.SemaphoreType.REGULAR,
         ],
         compiler_params=pltpu.CompilerParams(
@@ -794,18 +932,14 @@
         + tile
         - lax.broadcasted_iota(jnp.int32, shape, 1)
     )
-    same = docs_col[pl.ds(first + tile, top), :] == docs_row[:, pl.ds(first, size)]
+    same = docs_col[pl.ds(first + tile, top), :] == docs_row[pl.ds(0, 1), pl.ds(first, size)]
     power = jnp.exp(jnp.maximum(lag, 0).astype(F32) * log_decay)
     return jnp.where(same & (lag >= 0), power, 0.0)
 
 
 def retain_kernel(
-    decay_ref,
-    across_ref,
-    fold_ref,
-    docs_col,
-    docs_row,
-    scale_ref,
+    lengths_ref,
+    order_ref,
     gain_ref,
     qk_ref,
     v_ref,
@@ -833,6 +967,9 @@
     ring_out,
     ring_in,
     cot_rows,
+    docs_col,
+    docs_row,
+    scale_ref,
     send,
     recv,
     own_sem,
@@ -871,6 +1008,11 @@
     def block_rows(b):
         return pl.ds(pl.multiple_of(b * SPAN, SPAN), SPAN)
 
+    rate = decays(order_ref, heads)
+    across = block_scales(lengths_ref, rate, group_rows, scale_ref, docs_col)
+    docs_row[...] = row_docs(lengths_ref, group_rows)
+    fold = group_weights(lengths_ref, rate, group_rows, False)
+
     def q_cols(h):
         return pl.ds(h * KEY, KEY)
 
@@ -888,7 +1030,7 @@
             ]
             term = dot_tn(qk_ref[block_rows(b), k_cols(h)], weighed.astype(BF))
             terms[b, pl.ds(h * KEY, KEY), :] = term
-            total = across_ref[h, b] * total + term
+            total = across[h][b] * total + term
         gathered[0, pl.ds(h * KEY, KEY), :] = total.astype(BF)
 
     def state_view(r, side=None):
@@ -899,6 +1041,8 @@
 
     def up_view(s):
         def view(r, side=None):
+            if r == 0 and s == 0:
+                return wu_ref
             if side is None:
                 return up_full.at[pl.ds(r * part, part), pl.ds(s * slice_, slice_)]
             size = part // 2
@@ -910,6 +1054,8 @@
 
     def down_view(s):
         def view(r, side=None):
+            if r == 0 and s == 0:
+                return wd_ref
             if side is None:
                 return down_full.at[pl.ds(s * slice_, slice_), pl.ds(r * part, part)]
             size = slice_ // 2
@@ -924,8 +1070,6 @@
         Gather(moves, near, view) for view in (up_view(0), down_view(0), up_view(1), down_view(1))
     ]
     states.first()
-    own[0].wait()
-    own[1].wait()
     wide[0].first()
     cot_move = moves.go(cot_ref, cot_rows, near["pair"])
 
@@ -937,18 +1081,18 @@
                 at = pl.ds(first + tile, 128)
                 seen = pl.ds(first, tile + 128)
                 scores = dot_nt(qk_ref[at, q_cols(h)], qk_ref[seen, k_cols(h)])
-                mask = tile_decay(docs_col, docs_row, decay_ref[h], first, tile, 128)
+                mask = tile_decay(docs_col, docs_row, rate[h], first, tile, 128)
                 probs = (scores * mask).astype(BF)
                 retained[at, v_cols(h)] = dot_nn(probs, v_ref[seen, v_cols(h)])
 
     def finish_head(h):
         first = jnp.zeros((KEY, VAL), F32)
         for r in range(8):
-            first = first + fold_ref[h, r] * gathered[r, pl.ds(h * KEY, KEY), :].astype(F32)
+            first = first + fold[h][r] * gathered[r, pl.ds(h * KEY, KEY), :].astype(F32)
         for b in range(blocks):
             folded[b] = first.astype(BF)
             states_out[pl.ds((h * blocks + b) * KEY, KEY), :] = first.astype(BF)
-            first = across_ref[h, b] * first + terms[b, pl.ds(h * KEY, KEY), :]
+            first = across[h][b] * first + terms[b, pl.ds(h * KEY, KEY), :]
 
         @pl.loop(0, group_rows // 128)
         def _(i):
@@ -1047,14 +1191,13 @@
             ]
     for gather in wide:
         gather.done()
+    own[0].wait()
+    own[1].wait()
     moves.finish()
 
 
-SMEM = pl.BlockSpec(memory_space=pltpu.SMEM)
-
-
 def retain(
-    decay, across, fold, docs, scales, gain, qk, v, gate, tokens, out_full, cotangent, w_up, w_down
+    doc_lengths, head_order, gain, qk, v, gate, tokens, out_full, cotangent, w_up, w_down
 ):
     rows, width = tokens.shape
     count = lax.axis_size("head")
@@ -1076,7 +1219,7 @@
             struct((width, wide), BF),
             struct((wide, width), BF),
         ),
-        in_specs=[SMEM] * 3 + [VMEM] * 8 + [ANY, VMEM] + [ANY] * 2,
+        in_specs=[SMEM] * 2 + [VMEM] * 5 + [ANY] + [VMEM] * 3,
         out_specs=[VMEM] * 6 + [ANY] * 2,
         scratch_shapes=[
             pltpu.VMEM(v.shape, BF),
@@ -1089,6 +1232,9 @@
             pltpu.VMEM((3, rows, width), BF),
             pltpu.VMEM((3, rows, width), BF),
             pltpu.VMEM((rows, width), BF),
+            pltpu.VMEM((group_rows, 1), jnp.int32),
+            pltpu.VMEM((8, group_rows), jnp.int32),
+            pltpu.VMEM((group_rows, 2 * heads), F32),
             pltpu.SemaphoreType.DMA((moves,)),
             pltpu.SemaphoreType.DMA((moves,)),
             pltpu.SemaphoreType.DMA((3,)),
@@ -1100,8 +1246,8 @@
             flops=12 << 30, bytes_accessed=40 << 20, transcendentals=0
         ),
     )(
-        decay, across, fold, docs[:, None], docs[None, :], scales, gain[None, :], qk, v, gate,
-        tokens, out_full, cotangent, w_up, w_down,
+        doc_lengths, head_order, gain[None, :], qk, v, gate, tokens, out_full, cotangent, w_up,
+        w_down,
     )
 
 
@@ -1129,7 +1275,6 @@
     pre,
     back_out,
     back_in,
-    staged,
     odd_out_d,
     odd_in_d,
     odd_out_u,
@@ -1142,12 +1287,16 @@
     near_in_d,
     near_out_u,
     near_in_u,
+    up_sum,
+    down_sum,
+    gain,
     send,
     recv,
     load_sem,
     free_sem,
 ):
     near = peers()
+    gain[...] = arranged(gain_ref, lax.axis_index("tok"))
     z = lax.axis_index("head")
     count = lax.axis_size("head")
     rows, width = resid_ref.shape
@@ -1164,7 +1313,7 @@
         load.start()
     greet(*everyone())
     moves = Moves(send, recv)
-    size = 32
+    size = 16
 
     pairs = []
     for side in range(2):
@@ -1176,7 +1325,7 @@
             mean = jnp.mean(values, axis=-1, keepdims=True)
             centred = values - mean
             inverse = lax.rsqrt(jnp.mean(centred * centred, axis=-1, keepdims=True) + EPS)
-            lifted[at, :] = (centred * inverse * gain_ref[...]).astype(BF)
+            lifted[at, :] = (centred * inverse * gain[...]).astype(BF)
 
         pairs.append(
             moves.go(
@@ -1205,6 +1354,13 @@
     feed(0, rows)
     backs = []
     for side in range(2):
+        if side:
+
+            @pl.loop(0, width // 256)
+            def _(i):
+                to = pl.ds(pl.multiple_of(i * 256, 256), 256)
+                resid_grad[:, to] = dot_nt(pre[pl.ds(0, rows), :], up[to, :])
+
         pairs[side].wait_recv()
         feed(rows + side * side_rows, side_rows)
 
@@ -1216,11 +1372,6 @@
 
         at = pl.ds(side * side_rows, side_rows)
         backs.append(moves.go(back_out.at[at, :], back_in.at[at, :], near["pair"]))
-
-    @pl.loop(0, width // 256)
-    def _(i):
-        to = pl.ds(pl.multiple_of(i * 256, 256), 256)
-        resid_grad[:, to] = dot_nt(pre[pl.ds(0, rows), :], up[to, :])
 
     def down_term(s):
         def term(r):
@@ -1249,8 +1400,8 @@
         Scatter(moves, near, up_term(0), up_sets[0], up_own),
     ]
     sums += [
-        Scatter(moves, near, down_term(1), down_sets[1], down_far, sums[0], free_sem.at[0]),
-        Scatter(moves, near, up_term(1), up_sets[1], up_far, sums[1], free_sem.at[1]),
+        Scatter(moves, near, down_term(1), down_sets[1], down_sum, sums[0], free_sem.at[0]),
+        Scatter(moves, near, up_term(1), up_sets[1], up_sum, sums[1], free_sem.at[1]),
     ]
     sums[0].frees = free_sem.at[0]
     sums[1].frees = free_sem.at[1]
@@ -1266,7 +1417,7 @@
         if step:
             ring[step - 1, side].wait_recv()
         if step < count - 1:
-            here = staged.at[pl.ds(side * side_rows, side_rows), :] if step == 0 else shard(step, side)
+            here = back_in.at[pl.ds(side * side_rows, side_rows), :] if step == 0 else shard(step, side)
             ring[step, side] = moves.go(here, shard(step, side), near["up"])
 
     def norm_back(side):
@@ -1280,12 +1431,12 @@
             inverse = lax.rsqrt(jnp.mean(centred * centred, axis=-1, keepdims=True) + EPS)
             unit = centred * inverse
             grad = resid_grad[at, :] + back_in[at, :].astype(F32)
-            scaled = grad * gain_ref[...]
+            scaled = grad * gain[...]
             first = jnp.mean(scaled, axis=-1, keepdims=True)
             second = jnp.mean(scaled * unit, axis=-1, keepdims=True)
             found = cot[at, :].astype(F32) + inverse * (scaled - first - unit * second)
             resid_grad[at, :] = found
-            staged[at, :] = found.astype(BF)
+            back_in[at, :] = found.astype(BF)
             return total + jnp.sum(grad * unit, axis=0, keepdims=True)
 
         total = lax.fori_loop(0, side_rows // size, block, jnp.zeros((1, width), F32))
@@ -1293,55 +1444,53 @@
 
     norm_back(0)
     pass_on(0, 0)
+    for i in (3, 1, 2, 0):
+        sums[0].odd(i)
     for i in (3, 1):
-        sums[0].odd(i)
+        sums[1].odd(i)
     norm_back(1)
     pass_on(0, 1)
     mine = pltpu.make_async_copy(
-        staged, branch.at[pl.ds(pl.multiple_of(z * rows, rows), rows), :], load_sem.at[3]
+        back_in, branch.at[pl.ds(pl.multiple_of(z * rows, rows), rows), :], load_sem.at[3]
     )
     mine.start()
+    sums[0].far()
     for i in (2, 0):
-        sums[0].odd(i)
+        sums[1].odd(i)
     pass_on(1, 0)
-    sums[0].far()
-    for i in (3, 1):
-        sums[1].odd(i)
+    sums[1].far()
+    sums[0].close()
+    pass_on(1, 1)
+    for i in (3, 1, 2, 0):
+        sums[2].odd(i)
+    sums[1].close()
+    sums[2].far()
+    pass_on(2, 0)
 
     @pl.loop(0, width // 256)
     def _(i):
         to = pl.ds(pl.multiple_of(i * 256, 256), 256)
         layer_out[:, to] = resid_ref[:, to] + dot_nn(hidden[pl.ds(0, rows), :], down[:, to])
 
-    pass_on(1, 1)
-    for i in (2, 0):
-        sums[1].odd(i)
-    sums[0].close()
-    sums[1].far()
-    pass_on(2, 0)
-    for i in (3, 1):
-        sums[2].odd(i)
+    for i in (3, 1, 2, 0):
+        sums[3].odd(i)
+    pass_on(2, 1)
+    sums[2].close()
+    sums[3].far()
+    sums[0].done()
+    sums[1].done()
 
     @pl.loop(0, width // 256)
     def _(i):
         to = pl.ds(pl.multiple_of(i * 256, 256), 256)
         far_out[:, to] = dot_nn(hidden[pl.ds(rows, rows), :], down[:, to]).astype(BF)
 
-    sums[1].close()
-    for i in (2, 0):
-        sums[2].odd(i)
-    pass_on(2, 1)
-    sums[2].far()
-    for i in (3, 1, 2, 0):
-        sums[3].odd(i)
-    sums[0].done()
-    sums[3].far()
-    sums[2].close()
-    sums[1].done()
     sums[3].close()
     pass_on(3, 0)
     sums[2].done()
+    down_far[...] = down_sum[...].astype(BF)
     sums[3].done()
+    up_far[...] = up_sum[...].astype(BF)
     pass_on(3, 1)
     mine.wait()
     moves.finish()
@@ -1379,9 +1528,9 @@
             struct((rows, width), F32),
             struct((8, width), F32),
             struct(up_piece, F32),
-            struct(up_piece, F32),
+            struct(up_piece, BF),
             struct(down_piece, F32),
-            struct(down_piece, F32),
+            struct(down_piece, BF),
             struct((count * rows, width), BF),
         ),
         in_specs=[VMEM] * 2 + [ANY] * 3,
@@ -1396,13 +1545,15 @@
             pltpu.VMEM((2 * rows, wide), BF),
             pltpu.VMEM((rows, width), BF),
             pltpu.VMEM((rows, width), BF),
-            pltpu.VMEM((rows, width), BF),
             *odds(down_piece),
             *odds(up_piece),
             *sets(down_piece),
             *sets(up_piece),
             *nears(down_piece),
             *nears(up_piece),
+            pltpu.VMEM(up_piece, F32),
+            pltpu.VMEM(down_piece, F32),
+            pltpu.VMEM((1, width), F32),
             pltpu.SemaphoreType.DMA((moves,)),
             pltpu.SemaphoreType.DMA((moves,)),
             pltpu.SemaphoreType.DMA((4,)),
@@ -1418,35 +1569,47 @@
 
 
 def recall_kernel(
-    decay_ref,
-    across_ref,
-    fold_ref,
+    lengths_ref,
+    order_ref,
+    gain_ref,
+    wo_hbm,
+    branch_hbm,
+    gate_hbm,
+    unit_hbm,
+    inverse_hbm,
+    qk_hbm,
+    v_hbm,
+    turned_hbm,
+    states_hbm,
+    cos_hbm,
+    sin_hbm,
+    own_hbm,
+    far_ref,
+    up_ref,
+    down_ref,
+    wo_grad,
+    gains,
+    layer_out,
+    grads_out,
+    up_in,
+    down_in,
+    out_weights,
+    branch,
+    gate_ref,
+    unit_ref,
+    inverse_ref,
+    qk_ref,
+    v_ref,
+    turned_ref,
+    states_ref,
+    cos_ref,
+    sin_ref,
+    own_ref,
+    far_in,
+    grads,
     docs_col,
     docs_row,
     scale_ref,
-    gain_ref,
-    qk_ref,
-    v_ref,
-    gate_ref,
-    unit_ref,
-    inverse_ref,
-    states_ref,
-    cos_ref,
-    sin_ref,
-    turned_ref,
-    branch_ref,
-    wo_ref,
-    far_ref,
-    up_ref,
-    down_ref,
-    grads,
-    wo_grad,
-    gains,
-    far_in,
-    up_in,
-    down_in,
-    branch,
-    out_weights,
     back,
     terms,
     gathered,
@@ -1462,16 +1625,33 @@
     send,
     recv,
     load_sem,
+    keep_sem,
 ):
     near = peers()
+    tok = lax.axis_index("tok")
     group_rows, cols = v_ref.shape
     heads = cols // VAL
     blocks = group_rows // SPAN
     width = branch.shape[1]
     part = width // 8
     loads = [
-        pltpu.make_async_copy(branch_ref, branch, load_sem.at[0]),
-        pltpu.make_async_copy(wo_ref, out_weights, load_sem.at[1]),
+        pltpu.make_async_copy(source, target, load_sem.at[n])
+        for n, (source, target) in enumerate(
+            (
+                (wo_hbm, out_weights),
+                (branch_hbm, branch),
+                (gate_hbm, gate_ref),
+                (unit_hbm, unit_ref),
+                (inverse_hbm, inverse_ref),
+                (qk_hbm, qk_ref),
+                (v_hbm, v_ref),
+                (turned_hbm, turned_ref),
+                (states_hbm, states_ref),
+                (cos_hbm, cos_ref),
+                (sin_hbm, sin_ref),
+                (own_hbm, own_ref),
+            )
+        )
     ]
     for load in loads:
         load.start()
@@ -1495,7 +1675,11 @@
     def v_cols(h):
         return pl.ds(h * VAL, VAL)
 
-    for load in loads:
+    rate = decays(order_ref, heads)
+    across = block_scales(lengths_ref, rate, group_rows, scale_ref, docs_col)
+    docs_row[...] = row_docs(lengths_ref, group_rows)
+    fold = group_weights(lengths_ref, rate, group_rows, True)
+    for load in loads[:5]:
         load.wait()
 
     def tile_back(i, totals):
@@ -1527,6 +1711,20 @@
     gains[...] = jnp.zeros_like(gains)
     for h in range(heads):
         gains[pl.ds(0, 1), v_cols(h)] = totals[h]
+    first_gate = 2 * heads * KEY + cols
+    kept = [
+        pltpu.make_async_copy(
+            grads.at[:, pl.ds(first_gate, cols)],
+            grads_out.at[:, pl.ds(first_gate, cols)],
+            keep_sem.at[0],
+        ),
+        pltpu.make_async_copy(
+            grads.at[:, pl.ds(0, first_gate)], grads_out.at[:, pl.ds(0, first_gate)], keep_sem.at[1]
+        ),
+    ]
+    kept[0].start()
+    for load in loads[5:]:
+        load.wait()
 
     for h in range(heads):
         total = jnp.zeros((KEY, VAL), F32)
@@ -1536,7 +1734,7 @@
             ]
             term = dot_tn(qk_ref[block_rows(b), q_cols(h)], weighed.astype(BF))
             terms[b, pl.ds(h * KEY, KEY), :] = term
-            total = across_ref[h, b] * total + term
+            total = across[h][b] * total + term
         gathered[0, pl.ds(h * KEY, KEY), :] = total.astype(BF)
 
     def state_view(r, side=None):
@@ -1562,7 +1760,7 @@
             for tile in range(SPAN - 128, -1, -128):
                 at = pl.ds(first + tile, 128)
                 seen = pl.ds(first, tile + 128)
-                mask = tile_decay(docs_col, docs_row, decay_ref[h], first, tile, 128)
+                mask = tile_decay(docs_col, docs_row, rate[h], first, tile, 128)
                 query = qk_ref[at, q_cols(h)]
                 key = qk_ref[seen, k_cols(h)]
                 ret = back[at, v_cols(h)]
@@ -1581,10 +1779,10 @@
     def finish_head(h):
         later = jnp.zeros((KEY, VAL), F32)
         for r in range(8):
-            later = later + fold_ref[h, r] * gathered[r, pl.ds(h * KEY, KEY), :].astype(F32)
+            later = later + fold[h][r] * gathered[r, pl.ds(h * KEY, KEY), :].astype(F32)
         for b in reversed(range(blocks)):
             folded[b] = later.astype(BF)
-            later = across_ref[h, b] * later + terms[b, pl.ds(h * KEY, KEY), :]
+            later = across[h][b] * later + terms[b, pl.ds(h * KEY, KEY), :]
 
         @pl.loop(0, group_rows // 128)
         def _(i):
@@ -1626,15 +1824,24 @@
     outward.close()
     for h in range(1, heads):
         finish_head(h)
+    kept[1].start()
+    swaps[0].wait_recv()
+    for r, place in enumerate(xor_places(tok)):
+        at = pl.ds(r * part, part)
+        layer_out[:, pl.ds(pl.multiple_of(place * part, part), part)] = (
+            own_ref[:, at] + far_in[:, at].astype(F32)
+        ).astype(BF)
     outward.done()
-    for swap_ in swaps:
+    for swap_ in swaps[1:]:
         swap_.wait_recv()
+    for copy in kept:
+        copy.wait()
     moves.finish()
 
 
 def recall(
-    decay, across, fold, docs, scales, gain, qk, v, gate, unit, inverse, states, cosine, sine,
-    mixed_turned, branch, out_full, far_out, up_far, down_far,
+    doc_lengths, head_order, gain, qk, v, gate, unit, inverse, states, cosine, sine, mixed_turned,
+    branch, out_full, layer_own, far_out, up_far, down_far,
 ):
     group_rows, cols = v.shape
     heads = cols // VAL
@@ -1644,21 +1851,28 @@
     piece = (cols, part)
     moves = 3 + 8 + 8
     struct = jax.ShapeDtypeStruct
+    loaded = (
+        out_full, branch, gate, unit, inverse, qk, v, mixed_turned, states, cosine, sine, layer_own
+    )
     return pl.pallas_call(
         recall_kernel,
         out_shape=(
-            struct((group_rows, 3 * cols), BF),
             struct(piece, F32),
             struct((8, cols), F32),
             struct(far_out.shape, BF),
+            struct((group_rows, 3 * cols), BF),
             struct(up_far.shape, BF),
             struct(down_far.shape, BF),
         ),
-        in_specs=[SMEM] * 3 + [VMEM] * 13 + [ANY] * 5,
+        in_specs=[SMEM] * 2 + [VMEM] + [ANY] * 15,
         out_specs=[VMEM] * 3 + [ANY] * 3,
         scratch_shapes=[
-            pltpu.VMEM(branch.shape, BF),
-            pltpu.VMEM(out_full.shape, BF),
+            *[pltpu.VMEM(array.shape, array.dtype) for array in loaded],
+            pltpu.VMEM(far_out.shape, BF),
+            pltpu.VMEM((group_rows, 3 * cols), BF),
+            pltpu.VMEM((group_rows, 1), jnp.int32),
+            pltpu.VMEM((8, group_rows), jnp.int32),
+            pltpu.VMEM((group_rows, 2 * heads), F32),
             pltpu.VMEM(v.shape, BF),
             pltpu.VMEM((blocks, heads * KEY, VAL), F32),
             pltpu.VMEM((8, heads * KEY, VAL), BF),
@@ -1673,6 +1887,7 @@
             pltpu.VMEM((2,) + piece, BF),
             pltpu.SemaphoreType.DMA((moves,)),
             pltpu.SemaphoreType.DMA((moves,)),
+            pltpu.SemaphoreType.DMA((len(loaded),)),
             pltpu.SemaphoreType.DMA((2,)),
         ],
         compiler_params=pltpu.CompilerParams(
@@ -1681,10 +1896,7 @@
         cost_estimate=pl.CostEstimate(
             flops=20 << 30, bytes_accessed=40 << 20, transcendentals=0
         ),
-    )(
-        decay, across, fold, docs[:, None], docs[None, :], scales, gain[None, :], qk, v, gate, unit,
-        inverse, states, cosine, sine, mixed_turned, branch, out_full, far_out, up_far, down_far,
-    )
+    )(doc_lengths, head_order, gain[None, :], *loaded, far_out, up_far, down_far)
 
 
 def norm_forward(values, gain):
@@ -2029,81 +2241,25 @@
     w_up,
     w_down,
 ):
-    heads = w_query.shape[1] // KEY
-    head_count = lax.axis_size("head")
-    tok_count = lax.axis_size("tok")
-    z = lax.axis_index("head")
-    tok = lax.axis_index("tok")
-    rows = tokens.shape[0]
-    group_rows = rows * head_count
-    qk = w_query.shape[1]
-    vg = w_value.shape[1]
-
-    gain1 = reorder(norm_gain)
-    gain2 = reorder(ffn_gain)
-
-    ends = jnp.cumsum(doc_lengths)
-    starts = ends - doc_lengths
-    first_row = tok * group_rows
-    row_ids = first_row + jnp.arange(group_rows, dtype=jnp.int32)
-    doc_ids = doc_index(row_ids, starts)
-    cosine, sine = angles(doc_position(row_ids, starts), KEY // 2)
-    ranks = lax.dynamic_slice_in_dim(head_order, z * heads, heads)
-    log_decay = jnp.log1p(-jnp.exp2(-(5.0 + ranks.astype(F32))))
-    place = row_ids % SPAN
-    block_first = row_ids - place
-    before = doc_index(block_first - 1, starts)
-    last = doc_index(block_first + SPAN - 1, starts)
-    reach = jnp.where(
-        (doc_ids == before)[:, None], jnp.exp((place + 1).astype(F32)[:, None] * log_decay), 0.0
-    )
-    leave = jnp.where(
-        (doc_ids == last)[:, None],
-        jnp.exp((SPAN - 1 - place).astype(F32)[:, None] * log_decay),
-        0.0,
-    )
-    scales = jnp.concatenate([reach, leave], axis=1)
-    across = jnp.where(
-        (before[::SPAN] == last[::SPAN])[None, :], jnp.exp(SPAN * log_decay)[:, None], 0.0
-    )
-    order = jnp.arange(tok_count, dtype=jnp.int32) ^ tok
-
-    def weigh(lag, same):
-        return jnp.where(
-            ((lag >= 0) & same)[None, :],
-            jnp.exp(jnp.maximum(lag, 0).astype(F32) * group_rows * log_decay[:, None]),
-            0.0,
-        )
-
-    fold = weigh(
-        tok - 1 - order, doc_index((order + 1) * group_rows - 1, starts) == before[0]
-    )
-    fold_back = weigh(
-        order - 1 - tok, doc_index(order * group_rows - 1, starts) == doc_ids[-1]
-    )
-
-    turned, qkvg_full, out_full, qk_rows, v_rows, gate = enter(
-        tokens, gain1, cosine, sine, w_query, w_key, w_value, w_gate, w_out
+    turned, qkvg_full, out_full, qk_rows, v_rows, gate, cosine, sine = enter(
+        tokens, norm_gain, doc_lengths, w_query, w_key, w_value, w_gate, w_out
     )
     resid, unit_g, inverse_g, states, cot_pair, mixed_turned, up_full, down_full = retain(
-        log_decay, across, fold, doc_ids, scales, group_gain, qk_rows, v_rows, gate, tokens,
-        out_full, cotangent, w_up, w_down,
+        doc_lengths, head_order, group_gain, qk_rows, v_rows, gate, tokens, out_full, cotangent,
+        w_up, w_down,
     )
     (
-        layer_own, far_out, resid_grad, ffn_gain_parts, up_own, up_far, down_own, down_far, branch
-    ) = feed_forward(resid, gain2, cot_pair, up_full, down_full)
-    all_grad, w_out_grad, group_terms, far_in, up_in, down_in = recall(
-        log_decay, across, fold_back, doc_ids, scales, group_gain, qk_rows, v_rows, gate, unit_g,
-        inverse_g, states, cosine, sine, mixed_turned, branch, out_full, far_out,
-        up_far.astype(BF), down_far.astype(BF),
-    )
-    layer_out = reorder((layer_own + far_in.astype(F32)).astype(BF))
+        layer_own, far_out, resid_grad, ffn_terms, up_own, up_far, down_own, down_far, branch
+    ) = feed_forward(resid, ffn_gain, cot_pair, up_full, down_full)
+    w_out_grad, group_terms, layer_out, all_grad, up_in, down_in = recall(
+        doc_lengths, head_order, group_gain, qk_rows, v_rows, gate, unit_g, inverse_g, states,
+        cosine, sine, mixed_turned, branch, out_full, layer_own, far_out, up_far, down_far,
+    )
     w_up_grad = up_own + up_in.astype(F32)
     w_down_grad = down_own + down_in.astype(F32)
-    tokens_grad, w_qk_grad, w_value_grad, w_gate_grad, sums = depart(
-        all_grad, qkvg_full, turned, tokens, resid_grad, gain1, ffn_gain_parts, group_terms
-    )
-    w_query_grad, w_key_grad = w_qk_grad[:, :qk], w_qk_grad[:, qk:]
+    tokens_grad, w_query_grad, w_key_grad, w_value_grad, w_gate_grad, sums = depart(
+        all_grad, qkvg_full, turned, tokens, resid_grad, norm_gain, ffn_terms, group_terms
+    )
     return (
         layer_out,
         tokens_grad,
@@ -2112,7 +2268,7 @@
         w_key_grad,
         w_value_grad,
         w_gate_grad,
-        sums[2, :vg],
+        sums[2, : group_gain.shape[0]],
         w_out_grad,
         sums[1],
         w_up_grad,

time: 623 us -> 544 us (0.87)
  Pallas kernels: 571 us -> 521 us
  local copies, waits for them, and re-layouts: 25.6 us -> 9.9 us
  other arithmetic: 14.9 us -> 3.33 us
    pallas_call x1, Pallas kernels: 147 us -> 124 us  [retain(): pl.pallas_call(retain_kernel, out_shape=(struct((rows, width), F32), stru...]
    pallas_call x1, Pallas kernels: 103 us -> 91.5 us  [enter(): pl.pallas_call(enter_kernel, out_shape=(jax.ShapeDtypeStruct((width, grou...]
    unnamed x56 -> x27, local copies, waits for them, and re-layouts: 16.7 us -> 6.87 us
where the time goes in v4:
time: 544 us; the launch traced here: 535 us
  Pallas kernels  521 us (96%)
  local copies, waits for them, and re-layouts  9.9 us (2%)
    pallas_call x1, Pallas kernels, feed_forward(): pl.pallas_call(feed_kernel, out_shape=(struct((rows, width), F32), struct...  139 us
    pallas_call x1, Pallas kernels, retain(): pl.pallas_call(retain_kernel, out_shape=(struct((rows, width), F32), stru...  124 us
    pallas_call x1, Pallas kernels, depart(): pl.pallas_call(leave_kernel, out_shape=(jax.ShapeDtypeStruct((rows, width...  104 us
    pallas_call x1, Pallas kernels, enter(): pl.pallas_call(enter_kernel, out_shape=(jax.ShapeDtypeStruct((width, grou...  91.5 us
    pallas_call x1, Pallas kernels, recall(): pl.pallas_call(recall_kernel, out_shape=(struct(piece, F32), struct((8, c...  62.3 us

profile of v4, /device:TPU:0, one launch (start us, length us, event | category | flops | bytes accessed | tf_op | source)
XLA Modules:
  0.0 535.0 jit_solution(11106246842342449511)
XLA Ops:
  0.6 91.5 %shard_map.229 = (bf16[2048,1024]{1,0:T(8,128)(2,1)}, bf16[2048,3072]{1,0:T(8,128)(2,1)}, bf16[1024,2048]{1,0:T(8,128)(2,1)}, bf16[1024,1024]{1,0:T(8,128)(2,1)}...) custom-call(bf16[256,2048]{1,0:T(8,128)(2,1)} %tok_ref.5, ...), custom_call_target="tpu_custom_call" | custom-call | flops 12884901888 | bytes 41943040 | tf_op jit(solution)/shard_map/pallas_call | solution.py:541
  92.2 123.5 %shard_map.230 = (f32[256,2048]{1,0:T(8,128)}, bf16[1024,1024]{1,0:T(8,128)(2,1)}, f32[1024,2]{1,0:T(8,128)}, bf16[1024,512]{1,0:T(8,128)(2,1)}, bf16[512,2048]{...) custom-call(s32[4]{0:T(128)} %lengths_ref.5, s32[8]{0:T(128)} %order_ref.3, ...), custom_call_target="tpu_custom_call" | custom-call | flops 12884901888 | bytes 41943040 | tf_op jit(solution)/shard_map/pallas_call | solution.py:1210
  215.7 139.3 %shard_map.231 = (f32[256,2048]{1,0:T(8,128)}, bf16[256,2048]{1,0:T(8,128)(2,1)}, f32[256,2048]{1,0:T(8,128)}, f32[8,2048]{1,0:T(8,128)}, f32[256,1024]{1,0:T(8,...) custom-call(f32[256,2048]{1,0:T(8,128)} %get-tuple-element.53.resid_, ...), custom_call_target="tpu_custom_call" | custom-call | flops 27917287424 | bytes 41943040 | tf_op jit(solution)/shard_map/pallas_call | solution.py:1523
  355.0 0.0 copy-start.4
  355.0 62.3 %shard_map.232 = (f32[1024,256]{1,0:T(8,128)}, f32[8,1024]{1,0:T(8,128)}, bf16[256,2048]{1,0:T(8,128)(2,1)}, bf16[1024,3072]{1,0:T(8,128)(2,1)}, bf16[256,1024]{1,0:T(8,128)(2,1)}, /*index=5*/bf16[1024,256]{1,0:T(8,128)(2,1)}) custom-call(s32[4]{0:T(128)} %lengths_ref.5, s32[8]{0:T(128)} %order_ref.3, f32[1,1024]{1,0:T(1,128)} %bitcast.13, ...), custom_call_target="tpu_custom_call" | custom-call | flops 21474836480 | bytes 41943040 | tf_op jit(solution)/shard_map/pallas_call | solution.py:1857
  417.3 0.0 copy-start.3
  417.3 0.0 copy-start.7
  417.3 0.0 copy-done.4
  417.4 2.2 convert_add_fusion
  419.6 0.0 copy-done.3
  419.6 0.0 copy-done.7
  419.6 1.1 convert_add_fusion.1
  420.7 0.0 copy-start.2
  420.7 103.9 %shard_map.233 = (f32[256,2048]{1,0:T(8,128)}, f32[256,512]{1,0:T(8,128)}, f32[256,512]{1,0:T(8,128)}, f32[256,1024]{1,0:T(8,128)}, f32[256,1024]{1,0:T(8,128)}, /*index=5*/f32[8,2048]{1,0:T(8,128)}) custom-call(bf16[1024,3072]{1,0:T(8,128)(2,1)} %get-tuple-element.69.grads_ref, bf16[2048,3072]{1,0:T(8,128)(2,1)} %get-tuple-element.70.weights_ref, ...), custom_call_target="tpu_custom_call" | custom-call | flops 21474836480 | bytes 41943040 | tf_op jit(solution)/shard_map/pallas_call | solution.py:870
  524.6 0.0 copy-start
  524.7 1.5 slice.10
  526.2 1.5 fusion
  527.7 0.0 copy-done.2
  527.7 1.0 copy.33
  528.7 0.0 copy-done
  528.7 0.0 copy-start.9
  528.7 0.0 copy-start.8
  528.7 1.3 copy.34
  530.0 0.1 copy-done.9
  530.0 0.0 copy-start.6
  530.0 0.0 copy-start.5
  530.0 0.8 copy.35
  530.8 0.0 copy-done.8
  530.8 0.8 copy.36
  531.6 0.0 copy-done.6
  531.6 0.0 copy-start.1
  531.6 1.0 copy.37
  532.6 0.0 copy-done.5
  532.6 1.0 copy.38
  533.6 0.0 copy-done.1
  533.6 1.0 copy.39
Async XLA Ops:
  355.0 62.3 %copy-start.4 = (f32[1024,256]{1,0:T(8,128)S(1)}, f32[1024,256]{1,0:T(8,128)}, u32[]{:S(2)}) copy-start(f32[1024,256]{1,0:T(8,128)} %get-tuple-element.84) | copy-start | bytes 3145732
  417.3 2.3 copy-start.3
  417.3 2.3 copy-start.7
  420.7 107.0 %copy-start.2 = (bf16[256,2048]{1,0:T(8,128)(2,1)S(1)}, bf16[256,2048]{1,0:T(8,128)(2,1)}, u32[]{:S(2)}) copy-start(bf16[256,2048]{1,0:T(8,128)(2,1)} %get-tuple-element.100) | copy-start | bytes 3145732
  524.6 4.0 copy-start
  528.7 1.4 copy-start.9
  528.7 2.2 copy-start.8
  530.0 1.6 copy-start.6
  530.0 2.6 copy-start.5
  531.6 1.9 copy-start.1

commit v5 on v4

--- a/solution.py
+++ b/solution.py
@@ -250,6 +250,15 @@
         for h, rate in enumerate(log_decay):
             found[h].append(jnp.where((lag >= 0) & same, jnp.exp(amount * rate), 0.0))
     return found
+
+
+def state_view(gathered, h):
+    def view(r, side=None):
+        if side is None:
+            return gathered.at[r, pl.ds(h * KEY, KEY), :]
+        return gathered.at[r, pl.ds(h * KEY + side * (KEY // 2), KEY // 2), :]
+
+    return view
 
 
 class Moves:
@@ -357,7 +366,7 @@
     ]
     for copy in own:
         copy.start()
-    greet(near["core"], near["x"], near["y"], near["up"], near["down"])
+    greet(*everyone())
     moves = Moves(send, recv)
 
     def chunk_view(c):
@@ -646,6 +655,24 @@
             ref[...] = value[:, i * self.size : (i + 1) * self.size]
 
 
+class AllSum:
+    def __init__(self, moves, vector, slots, others):
+        self.moves, self.vector, self.slots, self.others = moves, vector, slots, others
+
+    def start(self):
+        self.made = [
+            self.moves.go(self.vector, self.slots.at[n], device)
+            for n, device in enumerate(self.others)
+        ]
+
+    def total(self):
+        total = self.vector[...]
+        for n, move in enumerate(self.made):
+            move.wait_recv()
+            total = total + self.slots[n]
+        return total
+
+
 def leave_kernel(
     grads_ref,
     weights_ref,
@@ -660,7 +687,9 @@
     wk_out,
     wv_out,
     wg_out,
-    gains_out,
+    norm_out,
+    ffn_out,
+    group_out,
     grads,
     weights,
     turned,
@@ -673,9 +702,16 @@
     far_in,
     near_out,
     near_in,
-    gains,
-    gains_in,
-    gains_z,
+    norm_vec,
+    norm_vec2,
+    norm_slots_z,
+    norm_slots,
+    ffn_vec,
+    ffn_vec2,
+    ffn_slots_z,
+    ffn_slots,
+    group_vec,
+    group_slots,
     gain,
     send,
     recv,
@@ -714,10 +750,9 @@
     loads = [grad_loads[0], *strip_loads, *grad_loads[1:], turned_load]
     for load in loads:
         load.start()
-    others = [
-        {"tok": tok, "head": lax.rem(z + step, count)} for step in range(1, count)
-    ]
-    greet(near["core"], near["x"], near["y"], *others)
+    z_others = [{"tok": tok, "head": lax.rem(z + step, count)} for step in range(1, count)]
+    tok_others = [{"tok": place, "head": z} for place in xor_places(tok)[1:]]
+    greet(*z_others, *tok_others)
     moves = Moves(send, recv)
 
     def ring_term(step, side):
@@ -772,6 +807,19 @@
     )
     scatters[0].frees = free_sem
 
+    ffn_vec[...] = jnp.zeros_like(ffn_vec)
+    group_vec[...] = jnp.zeros_like(group_vec)
+    for r, place in enumerate(xor_places(tok)):
+        ffn_vec[pl.ds(place, 1), :] = (
+            ffn_ref[pl.ds(0, 1), r * part : (r + 1) * part]
+            + ffn_ref[pl.ds(1, 1), r * part : (r + 1) * part]
+        )
+    for n in range(cols // part):
+        group_vec[pl.ds(n, 1), :] = group_ref[pl.ds(0, 1), n * part : (n + 1) * part]
+    ffn_z = AllSum(moves, ffn_vec, ffn_slots_z, z_others)
+    group_tok = AllSum(moves, group_vec, group_slots, tok_others)
+    ffn_z.start()
+    group_tok.start()
     grad_loads[0].wait()
     for side in range(2):
         strip_loads[2 * side].wait()
@@ -785,6 +833,10 @@
     ring_term(1, 1)
     for i in (3, 1, 2, 0):
         scatters[0].odd(i)
+    group_out[...] = group_tok.total()
+    ffn_vec2[...] = ffn_z.total()
+    ffn_tok = AllSum(moves, ffn_vec2, ffn_slots, tok_others)
+    ffn_tok.start()
     ring_send(1, 0)
     scatters[0].far()
     for i in (3, 1):
@@ -805,20 +857,13 @@
         scatters[2].odd(i)
     scatters[0].done()
     scatters[2].far()
+    ffn_out[...] = ffn_tok.total()
     ring_term(3, 0)
     ring_term(3, 1)
     scatters[1].done()
     scatters[2].close()
     scatters[2].done()
 
-    gains[...] = jnp.zeros_like(gains)
-    gains[pl.ds(2, 1), pl.ds(0, group_ref.shape[1])] = group_ref[pl.ds(0, 1), :]
-    for r, place in enumerate(xor_places(tok)):
-        at = pl.ds(pl.multiple_of(place * part, part), part)
-        gains[pl.ds(1, 1), at] = (
-            ffn_ref[pl.ds(0, 1), r * part : (r + 1) * part]
-            + ffn_ref[pl.ds(1, 1), r * part : (r + 1) * part]
-        )
     size = 16
     for side in range(2):
         ring[2, side].wait_recv()
@@ -843,20 +888,13 @@
 
     total = lax.fori_loop(0, rows // size, block, jnp.zeros((1, width), F32))
     for r, place in enumerate(xor_places(tok)):
-        at = pl.ds(pl.multiple_of(place * part, part), part)
-        gains[pl.ds(0, 1), at] = total[:, r * part : (r + 1) * part]
-
-    for i, way in enumerate(("core", "x", "y")):
-        move = moves.go(gains, gains_in.at[i], near[way])
-        move.wait_recv()
-        moves.sent(move)
-        gains[...] += gains_in[i]
-    last = [moves.go(gains, gains_z.at[i], others[i]) for i in range(count - 1)]
-    total = gains[...]
-    gains_out[...] = total
-    for i, move in enumerate(last):
-        move.wait_recv()
-        gains_out[pl.ds(0, 2), :] += gains_z[i, pl.ds(0, 2), :]
+        norm_vec[pl.ds(place, 1), :] = total[:, r * part : (r + 1) * part]
+    norm_z = AllSum(moves, norm_vec, norm_slots_z, z_others)
+    norm_z.start()
+    norm_vec2[...] = norm_z.total()
+    norm_tok = AllSum(moves, norm_vec2, norm_slots, tok_others)
+    norm_tok.start()
+    norm_out[...] = norm_tok.total()
     moves.finish()
 
 
@@ -865,8 +903,8 @@
     count = lax.axis_size("head")
     cols = grads.shape[1] // 3
     part = width // 8
-    moves = 6 + 3 * 8 + 3 + count - 1
-    sums = (8, width)
+    moves = 6 + 3 * 8 + 2 * (count - 1) + 3 * 7
+    vector = (8, part)
     return pl.pallas_call(
         leave_kernel,
         out_shape=(
@@ -875,10 +913,12 @@
             jax.ShapeDtypeStruct((part, cols // 2), F32),
             jax.ShapeDtypeStruct((part, cols), F32),
             jax.ShapeDtypeStruct((part, cols), F32),
-            jax.ShapeDtypeStruct(sums, F32),
+            jax.ShapeDtypeStruct(vector, F32),
+            jax.ShapeDtypeStruct(vector, F32),
+            jax.ShapeDtypeStruct(vector, F32),
         ),
         in_specs=[ANY] * 3 + [VMEM] * 5,
-        out_specs=[VMEM] * 6,
+        out_specs=[VMEM] * 8,
         scratch_shapes=[
             pltpu.VMEM(grads.shape, BF),
             pltpu.VMEM(weights.shape, BF),
@@ -892,9 +932,16 @@
             pltpu.VMEM((3, 2, part // 2, cols), BF),
             pltpu.VMEM((2, 2, part, cols), BF),
             pltpu.VMEM((3, 2, part, cols), BF),
-            pltpu.VMEM(sums, F32),
-            pltpu.VMEM((3,) + sums, F32),
-            pltpu.VMEM((count - 1,) + sums, F32),
+            pltpu.VMEM(vector, F32),
+            pltpu.VMEM(vector, F32),
+            pltpu.VMEM((count - 1,) + vector, F32),
+            pltpu.VMEM((7,) + vector, F32),
+            pltpu.VMEM(vector, F32),
+            pltpu.VMEM(vector, F32),
+            pltpu.VMEM((count - 1,) + vector, F32),
+            pltpu.VMEM((7,) + vector, F32),
+            pltpu.VMEM(vector, F32),
+            pltpu.VMEM((7,) + vector, F32),
             pltpu.VMEM((1, width), F32),
             pltpu.SemaphoreType.DMA((moves,)),
             pltpu.SemaphoreType.DMA((moves,)),
@@ -943,20 +990,28 @@
     gain_ref,
     qk_ref,
     v_ref,
+    wu_ref,
+    wd_ref,
+    gate_hbm,
+    tok_hbm,
+    cot_hbm,
+    wo_ref,
+    resid_out,
+    inverse_out,
+    unit_hbm,
+    states_hbm,
+    cot_out,
+    turned_hbm,
+    up_full,
+    down_full,
     gate_ref,
     tok_ref,
-    wo_ref,
     cot_ref,
-    wu_ref,
-    wd_ref,
-    resid_out,
+    cot_rows,
     unit_out,
-    inverse_out,
     states_out,
     cot_pair,
     mixed_turned,
-    up_full,
-    down_full,
     mixed_out,
     out_weights,
     retained,
@@ -966,7 +1021,6 @@
     held,
     ring_out,
     ring_in,
-    cot_rows,
     docs_col,
     docs_row,
     scale_ref,
@@ -978,12 +1032,11 @@
     tok = lax.axis_index("tok")
     z = lax.axis_index("head")
     count = lax.axis_size("head")
-    rows, width = tok_ref.shape
+    rows, width = tok_hbm.shape
     group_rows = rows * count
     part = width // 8
     heads = v_ref.shape[1] // VAL
     blocks = group_rows // SPAN
-    side_rows = rows // 2
     slice_ = wu_ref.shape[1]
     own = [
         pltpu.make_async_copy(
@@ -993,6 +1046,15 @@
             wd_ref, down_full.at[pl.ds(0, slice_), pl.ds(0, part)], own_sem.at[1]
         ),
         pltpu.make_async_copy(wo_ref, out_weights, own_sem.at[2]),
+        pltpu.make_async_copy(gate_hbm, gate_ref, own_sem.at[3]),
+        pltpu.make_async_copy(tok_hbm, tok_ref, own_sem.at[4]),
+        pltpu.make_async_copy(cot_hbm, cot_ref, own_sem.at[5]),
+    ]
+    keeps = [
+        pltpu.make_async_copy(unit_out, unit_hbm, own_sem.at[7]),
+        pltpu.make_async_copy(states_out, states_hbm, own_sem.at[8]),
+        pltpu.make_async_copy(mixed_turned, turned_hbm, own_sem.at[9]),
+        pltpu.make_async_copy(cot_pair, cot_out, own_sem.at[10]),
     ]
     for copy in own:
         copy.start()
@@ -1022,6 +1084,37 @@
     def v_cols(h):
         return pl.ds(h * VAL, VAL)
 
+    def up_view(s):
+        def view(r, side=None):
+            if r == 0 and s == 0:
+                return wu_ref
+            if side is None:
+                return up_full.at[pl.ds(r * part, part), pl.ds(s * slice_, slice_)]
+            size = part // 2
+            return up_full.at[
+                pl.ds(r * part + side * size, size), pl.ds(s * slice_, slice_)
+            ]
+
+        return view
+
+    def down_view(s):
+        def view(r, side=None):
+            if r == 0 and s == 0:
+                return wd_ref
+            if side is None:
+                return down_full.at[pl.ds(s * slice_, slice_), pl.ds(r * part, part)]
+            size = slice_ // 2
+            return down_full.at[
+                pl.ds(s * slice_ + side * size, size), pl.ds(r * part, part)
+            ]
+
+        return view
+
+    wide = [
+        Gather(moves, near, view) for view in (up_view(0), down_view(0), up_view(1), down_view(1))
+    ]
+
+    states = [Gather(moves, near, state_view(gathered, h)) for h in range(heads)]
     for h in range(heads):
         total = jnp.zeros((KEY, VAL), F32)
         for b in range(blocks):
@@ -1032,45 +1125,9 @@
             terms[b, pl.ds(h * KEY, KEY), :] = term
             total = across[h][b] * total + term
         gathered[0, pl.ds(h * KEY, KEY), :] = total.astype(BF)
-
-    def state_view(r, side=None):
-        if side is None:
-            return gathered.at[r]
-        size = gathered.shape[1] // 2
-        return gathered.at[r, pl.ds(side * size, size), :]
-
-    def up_view(s):
-        def view(r, side=None):
-            if r == 0 and s == 0:
-                return wu_ref
-            if side is None:
-                return up_full.at[pl.ds(r * part, part), pl.ds(s * slice_, slice_)]
-            size = part // 2
-            return up_full.at[
-                pl.ds(r * part + side * size, size), pl.ds(s * slice_, slice_)
-            ]
-
-        return view
-
-    def down_view(s):
-        def view(r, side=None):
-            if r == 0 and s == 0:
-                return wd_ref
-            if side is None:
-                return down_full.at[pl.ds(s * slice_, slice_), pl.ds(r * part, part)]
-            size = slice_ // 2
-            return down_full.at[
-                pl.ds(s * slice_ + side * size, size), pl.ds(r * part, part)
-            ]
-
-        return view
-
-    states = Gather(moves, near, state_view)
-    wide = [
-        Gather(moves, near, view) for view in (up_view(0), down_view(0), up_view(1), down_view(1))
-    ]
-    states.first()
+        states[h].first()
     wide[0].first()
+    own[5].wait()
     cot_move = moves.go(cot_ref, cot_rows, near["pair"])
 
     def intra(h):
@@ -1112,87 +1169,90 @@
             mixed_out[at, v_cols(h)] = mixed
             mixed_turned[v_cols(h), at] = mixed.T
 
-    intra(0)
-    states.second()
+    for h in range(heads):
+        intra(h)
+        states[h].second()
     wide[1].first()
-    for h in range(1, heads):
-        intra(h)
-    states.third()
+    for h in range(heads):
+        states[h].third()
     wide[0].second()
-    states.done()
+    own[3].wait()
     for h in range(heads):
+        states[h].done()
         finish_head(h)
-
-    def ring_term(step):
+    for keep in keeps[:3]:
+        keep.start()
+
+    def ring_term(step, side):
         owner = lax.rem(z + 2 * count - 1 - step, count)
         at = pl.ds(pl.multiple_of(owner * rows, rows), rows)
 
-        @pl.loop(0, width // 256)
+        @pl.loop(side * (width // 512), (side + 1) * (width // 512))
         def _(i):
             to = pl.ds(pl.multiple_of(i * 256, 256), 256)
             held[:, to] = dot_nn(mixed_out[at, :], out_weights[:, to])
 
     ring = {}
+    half = width // 2
 
     def ring_send(step, side):
-        at = pl.ds(side * side_rows, side_rows)
-        value = held[at, :]
+        at = pl.ds(side * half, half)
+        value = held[:, at]
         if step:
             ring[step - 1, side].wait_recv()
-            value = value + ring_in[step - 1, at, :].astype(F32)
-        ring_out[step, at, :] = value.astype(BF)
+            value = value + ring_in[step - 1, :, at].astype(F32)
+        ring_out[step, :, at] = value.astype(BF)
         ring[step, side] = moves.go(
-            ring_out.at[step, at, :], ring_in.at[step, at, :], near["up"]
+            ring_out.at[step, :, at], ring_in.at[step, :, at], near["up"]
         )
 
     own[2].wait()
-    ring_term(0)
-    ring_send(0, 0)
-    ring_send(0, 1)
+    for side in range(2):
+        ring_term(0, side)
+        ring_send(0, side)
     wide[1].second()
+    ring_term(1, 0)
+    ring_term(1, 1)
     far_up.wait_recv()
     wide[2].first()
     wide[0].third()
-    ring_term(1)
     ring_send(1, 0)
     far_down.wait_recv()
     wide[3].first()
     wide[1].third()
     ring_send(1, 1)
-    ring_term(2)
+    ring_term(2, 0)
+    ring_term(2, 1)
     wide[2].second()
     ring_send(2, 0)
     wide[3].second()
     ring_send(2, 1)
-    ring_term(3)
+    ring_term(3, 0)
+    ring_term(3, 1)
     wide[2].third()
     wide[3].third()
-    size = 32
-    for side in range(2):
-        ring[2, side].wait_recv()
-
-        @pl.loop(0, side_rows // size)
-        def _(i):
-            at = pl.ds(pl.multiple_of(side * side_rows + i * size, size), size)
-            values = jnp.concatenate(
-                [
-                    tok_ref[at, pl.ds(pl.multiple_of(place * part, part), part)]
-                    for place in xor_places(tok)
-                ],
-                axis=1,
-            ).astype(F32)
-            resid_out[at, :] = values + held[at, :] + ring_in[2, at, :].astype(F32)
-
+    own[4].wait()
     cot_move.wait_recv()
     for ref, first in ((cot_ref, 0), (cot_rows, rows)):
         for r, place in enumerate(xor_places(tok)):
             cot_pair[pl.ds(first, rows), pl.ds(r * part, part)] = ref[
                 :, pl.ds(pl.multiple_of(place * part, part), part)
             ]
+    keeps[3].start()
+    for side in range(2):
+        ring[2, side].wait_recv()
+        for n in range(4):
+            r = side * 4 + n
+            place = xor_places(tok)[r]
+            at = pl.ds(r * part, part)
+            values = tok_ref[:, pl.ds(pl.multiple_of(place * part, part), part)].astype(F32)
+            resid_out[:, at] = values + held[:, at] + ring_in[2, :, at].astype(F32)
     for gather in wide:
         gather.done()
     own[0].wait()
     own[1].wait()
+    for keep in keeps:
+        keep.wait()
     moves.finish()
 
 
@@ -1205,23 +1265,29 @@
     heads = v.shape[1] // VAL
     blocks = group_rows // SPAN
     wide = 2 * w_up.shape[1]
-    moves = 3 + 5 * 8 + 6
+    moves = 3 + (4 + heads) * 8 + 6
     struct = jax.ShapeDtypeStruct
+    kept = (
+        struct(v.shape, BF),
+        struct((heads * blocks * KEY, VAL), BF),
+        struct((2 * rows, width), BF),
+        struct((heads * VAL, group_rows), BF),
+    )
     return pl.pallas_call(
         retain_kernel,
         out_shape=(
             struct((rows, width), F32),
-            struct(v.shape, BF),
             struct((group_rows, heads), F32),
-            struct((heads * blocks * KEY, VAL), BF),
-            struct((2 * rows, width), BF),
-            struct((heads * VAL, group_rows), BF),
+            *kept,
             struct((width, wide), BF),
             struct((wide, width), BF),
         ),
-        in_specs=[SMEM] * 2 + [VMEM] * 5 + [ANY] + [VMEM] * 3,
-        out_specs=[VMEM] * 6 + [ANY] * 2,
+        in_specs=[SMEM] * 2 + [VMEM] * 5 + [ANY] * 4,
+        out_specs=[VMEM] * 2 + [ANY] * 6,
         scratch_shapes=[
+            pltpu.VMEM(gate.shape, BF),
+            *[pltpu.VMEM(tokens.shape, BF)] * 3,
+            *[pltpu.VMEM(array.shape, BF) for array in kept],
             pltpu.VMEM(v.shape, BF),
             pltpu.VMEM(out_full.shape, BF),
             pltpu.VMEM((group_rows, heads * VAL), F32),
@@ -1231,13 +1297,12 @@
             pltpu.VMEM((rows, width), F32),
             pltpu.VMEM((3, rows, width), BF),
             pltpu.VMEM((3, rows, width), BF),
-            pltpu.VMEM((rows, width), BF),
             pltpu.VMEM((group_rows, 1), jnp.int32),
             pltpu.VMEM((8, group_rows), jnp.int32),
             pltpu.VMEM((group_rows, 2 * heads), F32),
             pltpu.SemaphoreType.DMA((moves,)),
             pltpu.SemaphoreType.DMA((moves,)),
-            pltpu.SemaphoreType.DMA((3,)),
+            pltpu.SemaphoreType.DMA((11,)),
         ],
         compiler_params=pltpu.CompilerParams(
             collective_id=2, has_side_effects=True, vmem_limit_bytes=LIMIT
@@ -1246,8 +1311,8 @@
             flops=12 << 30, bytes_accessed=40 << 20, transcendentals=0
         ),
     )(
-        doc_lengths, head_order, gain[None, :], qk, v, gate, tokens, out_full, cotangent, w_up,
-        w_down,
+        doc_lengths, head_order, gain[None, :], qk, v, w_up, w_down, gate, tokens, cotangent,
+        out_full,
     )
 
 
@@ -1682,36 +1747,9 @@
     for load in loads[:5]:
         load.wait()
 
-    def tile_back(i, totals):
-        at = pl.ds(pl.multiple_of(i * 128, 128), 128)
-        sums = []
-        for h in range(heads):
-            grad = dot_nt(branch[at, :], out_weights[v_cols(h), :]).astype(BF).astype(F32)
-            gate = gate_ref[at, v_cols(h)].astype(F32)
-            sigma = 1.0 / (1.0 + jnp.exp(-gate))
-            swish = gate * sigma
-            unit = unit_ref[at, v_cols(h)].astype(F32)
-            gain = gain_ref[:, h * VAL : (h + 1) * VAL]
-            grads[at, pl.ds(2 * heads * KEY + cols + h * VAL, VAL)] = (
-                grad * unit * gain * (sigma + swish * (1.0 - sigma))
-            ).astype(BF)
-            inner = grad * swish
-            scaled = inner * gain
-            first = jnp.mean(scaled, axis=-1, keepdims=True)
-            second = jnp.mean(scaled * unit, axis=-1, keepdims=True)
-            back[at, v_cols(h)] = (
-                inverse_ref[at, h : h + 1] * (scaled - first - unit * second)
-            ).astype(BF)
-            sums.append(totals[h] + jnp.sum(inner * unit, axis=0, keepdims=True))
-        return tuple(sums)
-
-    totals = lax.fori_loop(
-        0, group_rows // 128, tile_back, tuple(jnp.zeros((1, VAL), F32) for _ in range(heads))
-    )
+    first_gate = 2 * heads * KEY + cols
+    states = [Gather(moves, near, state_view(gathered, h)) for h in range(heads)]
     gains[...] = jnp.zeros_like(gains)
-    for h in range(heads):
-        gains[pl.ds(0, 1), v_cols(h)] = totals[h]
-    first_gate = 2 * heads * KEY + cols
     kept = [
         pltpu.make_async_copy(
             grads.at[:, pl.ds(first_gate, cols)],
@@ -1722,11 +1760,34 @@
             grads.at[:, pl.ds(0, first_gate)], grads_out.at[:, pl.ds(0, first_gate)], keep_sem.at[1]
         ),
     ]
-    kept[0].start()
-    for load in loads[5:]:
-        load.wait()
-
     for h in range(heads):
+        gain = gain_ref[:, h * VAL : (h + 1) * VAL]
+
+        def tile_back(i, total):
+            at = pl.ds(pl.multiple_of(i * 128, 128), 128)
+            grad = dot_nt(branch[at, :], out_weights[v_cols(h), :]).astype(BF).astype(F32)
+            gate = gate_ref[at, v_cols(h)].astype(F32)
+            sigma = 1.0 / (1.0 + jnp.exp(-gate))
+            swish = gate * sigma
+            unit = unit_ref[at, v_cols(h)].astype(F32)
+            grads[at, pl.ds(first_gate + h * VAL, VAL)] = (
+                grad * unit * gain * (sigma + swish * (1.0 - sigma))
+            ).astype(BF)
+            inner = grad * swish
+            scaled = inner * gain
+            first = jnp.mean(scaled, axis=-1, keepdims=True)
+            second = jnp.mean(scaled * unit, axis=-1, keepdims=True)
+            back[at, v_cols(h)] = (
+                inverse_ref[at, h : h + 1] * (scaled - first - unit * second)
+            ).astype(BF)
+            return total + jnp.sum(inner * unit, axis=0, keepdims=True)
+
+        gains[pl.ds(0, 1), v_cols(h)] = lax.fori_loop(
+            0, group_rows // 128, tile_back, jnp.zeros((1, VAL), F32)
+        )
+        if h == 0:
+            for load in loads[5:]:
+                load.wait()
         total = jnp.zeros((KEY, VAL), F32)
         for b in reversed(range(blocks)):
             weighed = back[block_rows(b), v_cols(h)].astype(F32) * scale_ref[
@@ -1736,15 +1797,8 @@
             terms[b, pl.ds(h * KEY, KEY), :] = term
             total = across[h][b] * total + term
         gathered[0, pl.ds(h * KEY, KEY), :] = total.astype(BF)
-
-    def state_view(r, side=None):
-        if side is None:
-            return gathered.at[r]
-        size = gathered.shape[1] // 2
-        return gathered.at[r, pl.ds(side * size, size), :]
-
-    states = Gather(moves, near, state_view)
-    states.first()
+        states[h].first()
+    kept[0].start()
 
     def out_term(r):
         return dot_nn(turned_ref[...], branch[:, r * part : (r + 1) * part])
@@ -1809,20 +1863,22 @@
             found = dv[at, v_cols(h)] + leave * dot_nn(qk_ref[at, k_cols(h)], folded[b])
             grads[at, pl.ds(2 * heads * KEY + h * VAL, VAL)] = found.astype(BF)
 
-    for i in (3, 1):
-        outward.odd(i)
     intra(0)
-    states.second()
-    for i in (2, 0):
+    states[0].second()
+    for i in (3, 1, 2, 0):
         outward.odd(i)
     for h in range(1, heads):
+        states[h].second()
         intra(h)
-    states.third()
     outward.far()
-    states.done()
+    states[0].third()
+    for h in range(1, heads):
+        states[h].third()
+    states[0].done()
     finish_head(0)
     outward.close()
     for h in range(1, heads):
+        states[h].done()
         finish_head(h)
     kept[1].start()
     swaps[0].wait_recv()
@@ -1849,7 +1905,7 @@
     width = branch.shape[1]
     part = width // 8
     piece = (cols, part)
-    moves = 3 + 8 + 8
+    moves = 3 + 8 + 8 * heads
     struct = jax.ShapeDtypeStruct
     loaded = (
         out_full, branch, gate, unit, inverse, qk, v, mixed_turned, states, cosine, sine, layer_own
@@ -2244,7 +2300,7 @@
     turned, qkvg_full, out_full, qk_rows, v_rows, gate, cosine, sine = enter(
         tokens, norm_gain, doc_lengths, w_query, w_key, w_value, w_gate, w_out
     )
-    resid, unit_g, inverse_g, states, cot_pair, mixed_turned, up_full, down_full = retain(
+    resid, inverse_g, unit_g, states, cot_pair, mixed_turned, up_full, down_full = retain(
         doc_lengths, head_order, group_gain, qk_rows, v_rows, gate, tokens, out_full, cotangent,
         w_up, w_down,
     )
@@ -2257,20 +2313,20 @@
     )
     w_up_grad = up_own + up_in.astype(F32)
     w_down_grad = down_own + down_in.astype(F32)
-    tokens_grad, w_query_grad, w_key_grad, w_value_grad, w_gate_grad, sums = depart(
-        all_grad, qkvg_full, turned, tokens, resid_grad, norm_gain, ffn_terms, group_terms
-    )
+    (
+        tokens_grad, w_query_grad, w_key_grad, w_value_grad, w_gate_grad, norm_sum, ffn_sum, group_sum
+    ) = depart(all_grad, qkvg_full, turned, tokens, resid_grad, norm_gain, ffn_terms, group_terms)
     return (
         layer_out,
         tokens_grad,
-        sums[0],
+        norm_sum.reshape(-1),
         w_query_grad,
         w_key_grad,
         w_value_grad,
         w_gate_grad,
-        sums[2, : group_gain.shape[0]],
+        group_sum.reshape(-1)[: group_gain.shape[0]],
         w_out_grad,
-        sums[1],
+        ffn_sum.reshape(-1),
         w_up_grad,
         w_down_grad,
     )

time: 544 us -> 531 us (0.976)
  Pallas kernels: 521 us -> 507 us
    pallas_call x1, Pallas kernels: 139 us -> 131 us  [feed_forward(): pl.pallas_call(feed_kernel, out_shape=(struct((rows, width), F32), struct...]
    unnamed x27 -> x31, local copies, waits for them, and re-layouts: 6.87 us -> 10.9 us
where the time goes in v5:
time: 531 us; the launch traced here: 522 us
  Pallas kernels  507 us (95%)
  local copies, waits for them, and re-layouts  10.9 us (2%)
    pallas_call x1, Pallas kernels, feed_forward(): pl.pallas_call(feed_kernel, out_shape=(struct((rows, width), F32), struct...  131 us
    pallas_call x1, Pallas kernels, retain(): pl.pallas_call(retain_kernel, out_shape=(struct((rows, width), F32), stru...  121 us
    pallas_call x1, Pallas kernels, depart(): pl.pallas_call(leave_kernel, out_shape=(jax.ShapeDtypeStruct((rows, width...  104 us
    pallas_call x1, Pallas kernels, enter(): pl.pallas_call(enter_kernel, out_shape=(jax.ShapeDtypeStruct((width, grou...  91.5 us
    pallas_call x1, Pallas kernels, recall(): pl.pallas_call(recall_kernel, out_shape=(struct(piece, F32), struct((8, c...  58.9 us
    unnamed x31, local copies, waits for them, and re-layouts  10.9 us

profile of v5, /device:TPU:0, one launch (start us, length us, event | category | flops | bytes accessed | tf_op | source)
XLA Modules:
  0.0 522.0 jit_solution(5088062784728831540)
XLA Ops:
  0.6 91.5 %shard_map.229 = (bf16[2048,1024]{1,0:T(8,128)(2,1)}, bf16[2048,3072]{1,0:T(8,128)(2,1)}, bf16[1024,2048]{1,0:T(8,128)(2,1)}, bf16[1024,1024]{1,0:T(8,128)(2,1)}...) custom-call(bf16[256,2048]{1,0:T(8,128)(2,1)} %tok_ref.3, ...), custom_call_target="tpu_custom_call" | custom-call | flops 12884901888 | bytes 41943040 | tf_op jit(solution)/shard_map/pallas_call | solution.py:550
  92.2 121.3 %shard_map.230 = (f32[256,2048]{1,0:T(8,128)}, f32[1024,2]{1,0:T(8,128)}, bf16[1024,1024]{1,0:T(8,128)(2,1)}, bf16[1024,512]{1,0:T(8,128)(2,1)}, bf16[512,2048]{...) custom-call(s32[4]{0:T(128)} %lengths_ref.5, s32[8]{0:T(128)} %order_ref.3, ...), custom_call_target="tpu_custom_call" | custom-call | flops 12884901888 | bytes 41943040 | tf_op jit(solution)/shard_map/pallas_call | solution.py:1276
  213.5 130.9 %shard_map.231 = (f32[256,2048]{1,0:T(8,128)}, bf16[256,2048]{1,0:T(8,128)(2,1)}, f32[256,2048]{1,0:T(8,128)}, f32[8,2048]{1,0:T(8,128)}, f32[256,1024]{1,0:T(8,...) custom-call(f32[256,2048]{1,0:T(8,128)} %get-tuple-element.55.resid_, ...), custom_call_target="tpu_custom_call" | custom-call | flops 27917287424 | bytes 41943040 | tf_op jit(solution)/shard_map/pallas_call | solution.py:1588
  344.4 0.0 copy-start.4
  344.4 58.9 %shard_map.232 = (f32[1024,256]{1,0:T(8,128)}, f32[8,1024]{1,0:T(8,128)}, bf16[256,2048]{1,0:T(8,128)(2,1)}, bf16[1024,3072]{1,0:T(8,128)(2,1)}, bf16[256,1024]{1,0:T(8,128)(2,1)}, /*index=5*/bf16[1024,256]{1,0:T(8,128)(2,1)}) custom-call(s32[4]{0:T(128)} %lengths_ref.5, s32[8]{0:T(128)} %order_ref.3, f32[1,1024]{1,0:T(1,128)} %bitcast.19, ...), custom_call_target="tpu_custom_call" | custom-call | flops 21474836480 | bytes 41943040 | tf_op jit(solution)/shard_map/pallas_call | solution.py:1913
  403.3 0.0 copy-start.3
  403.3 0.0 copy-start.7
  403.3 0.0 copy-done.4
  403.3 2.2 convert_add_fusion
  405.5 0.0 copy-done.3
  405.5 0.0 copy-done.7
  405.5 1.1 convert_add_fusion.1
  406.6 0.0 copy-start.2
  406.6 104.0 %shard_map.233 = (f32[256,2048]{1,0:T(8,128)}, f32[256,512]{1,0:T(8,128)}, f32[256,512]{1,0:T(8,128)}, f32[256,1024]{1,0:T(8,128)}, f32[256,1024]{1,0:T(8,128)},...) custom-call(bf16[1024,3072]{1,0:T(8,128)(2,1)} %get-tuple-element.71.grads_ref, ...), custom_call_target="tpu_custom_call" | custom-call | flops 21474836480 | bytes 41943040 | tf_op jit(solution)/shard_map/pallas_call | solution.py:908
  510.7 0.0 copy-start
  510.7 1.4 copy.26
  512.1 0.7 slice_bitcast_fusion
  512.8 0.6 copy.27
  513.4 1.3 copy.28
  514.7 0.0 copy-done.2
  514.7 1.0 copy.36
  515.7 0.0 copy-done
  515.7 0.0 copy-start.9
  515.7 0.0 copy-start.8
  515.7 1.3 copy.37
  517.0 0.1 copy-done.9
  517.1 0.0 copy-start.6
  517.1 0.0 copy-start.5
  517.1 0.8 copy.38
  517.9 0.0 copy-done.8
  517.9 0.8 copy.39
  518.7 0.0 copy-done.6
  518.7 0.0 copy-start.1
  518.7 1.0 copy.40
  519.6 0.0 copy-done.5
  519.6 1.0 copy.41
  520.6 0.0 copy-done.1
  520.6 1.0 copy.42
Async XLA Ops:
  344.4 58.9 %copy-start.4 = (f32[1024,256]{1,0:T(8,128)S(1)}, f32[1024,256]{1,0:T(8,128)}, u32[]{:S(2)}) copy-start(f32[1024,256]{1,0:T(8,128)} %get-tuple-element.88) | copy-start | bytes 3145732
  403.3 2.3 copy-start.3
  403.3 2.3 copy-start.7
  406.6 108.1 %copy-start.2 = (bf16[256,2048]{1,0:T(8,128)(2,1)S(1)}, bf16[256,2048]{1,0:T(8,128)(2,1)}, u32[]{:S(2)}) copy-start(bf16[256,2048]{1,0:T(8,128)(2,1)} %get-tuple-element.102) | copy-start | bytes 3145732
  510.7 5.0 copy-start
  515.7 1.4 copy-start.9
  515.7 2.2 copy-start.8
  517.1 1.6 copy-start.6
  517.1 2.6 copy-start.5
  518.7 1.9 copy-start.1

commit v6 on v5

--- a/solution.py
+++ b/solution.py
@@ -170,7 +170,10 @@
     barrier = pltpu.get_barrier_semaphore()
     for device in devices:
         pl.semaphore_signal(barrier, inc=1, device_id=device, device_id_type=MESH)
-    pl.semaphore_wait(barrier, len(devices))
+
+
+def greeted(*devices):
+    pl.semaphore_wait(pltpu.get_barrier_semaphore(), len(devices))
 
 
 def doc_starts(lengths):
@@ -331,6 +334,11 @@
     turned_out,
     weights_out,
     out_full,
+    qk_hbm,
+    v_hbm,
+    gate_hbm,
+    cos_hbm,
+    sin_hbm,
     qk_out,
     v_out,
     gate_out,
@@ -345,6 +353,7 @@
     recv,
     own_sem,
     keep_sem,
+    rows_sem,
 ):
     near = peers()
     tok = lax.axis_index("tok")
@@ -366,7 +375,9 @@
     ]
     for copy in own:
         copy.start()
-    greet(*everyone())
+    reached = everyone()
+    greet(*reached)
+    gain[...] = arranged(gain_ref, tok)
     moves = Moves(send, recv)
 
     def chunk_view(c):
@@ -387,32 +398,16 @@
 
     chunks = [Gather(moves, near, chunk_view(c)) for c in range(3)]
     outward = Gather(moves, near, out_view)
-    own[0].wait()
-    own[1].wait()
-    chunks[0].first()
-    own[2].wait()
-    chunks[1].first()
-    own[3].wait()
-    own[4].wait()
-    kept = [pltpu.make_async_copy(own_out, out_full.at[:, pl.ds(0, part)], keep_sem.at[4])]
-    kept[0].start()
-    gain[...] = arranged(gain_ref, tok)
-
-    @pl.loop(0, rows // 16)
-    def _(i):
-        at = pl.ds(pl.multiple_of(i * 16, 16), 16)
-        values = jnp.concatenate(
-            [
-                tok_ref[at, pl.ds(pl.multiple_of(place * part, part), part)]
-                for place in xor_places(tok)
-            ],
-            axis=1,
-        ).astype(F32)
-        mean = jnp.mean(values, axis=-1, keepdims=True)
-        centred = values - mean
-        inverse = lax.rsqrt(jnp.mean(centred * centred, axis=-1, keepdims=True) + EPS)
-        lifted = (centred * inverse * gain[...]).astype(BF)
-        group[pl.ds(pl.multiple_of(z * rows + i * 16, 16), 16), :] = lifted
+    def lift(side):
+        @pl.loop(side * (rows // 32), (side + 1) * (rows // 32))
+        def _(i):
+            at = pl.ds(pl.multiple_of(i * 16, 16), 16)
+            values = arranged(tok_ref.at[at, :], tok).astype(F32)
+            mean = jnp.mean(values, axis=-1, keepdims=True)
+            centred = values - mean
+            inverse = lax.rsqrt(jnp.mean(centred * centred, axis=-1, keepdims=True) + EPS)
+            lifted = (centred * inverse * gain[...]).astype(BF)
+            group[pl.ds(pl.multiple_of(z * rows + i * 16, 16), 16), :] = lifted
 
     def shard(step, side):
         owner = lax.rem(z - step + count, count)
@@ -427,15 +422,28 @@
         if step < count - 1:
             ring[step, side] = moves.go(shard(step, side), shard(step, side), near["up"])
 
-    def project(c, steps):
+    def keep_rows(step):
+        owner = lax.rem(z - step + count, count)
+        at = pl.ds(pl.multiple_of(owner * rows, rows), rows)
+        for n, (source, target) in enumerate(
+            ((qk_out, qk_hbm), (v_out, v_hbm), (gate_out, gate_hbm))
+        ):
+            copy = pltpu.make_async_copy(
+                source.at[at, :], target.at[at, :], rows_sem.at[3 * step + n]
+            )
+            copy.start()
+            kept.append(copy)
+
+    def project(c, steps, part_rows=None):
         first, number = steps
+        offset, size = part_rows or (0, rows)
 
         @pl.loop(0, number * (cols // 256))
         def _(i):
             step = first + lax.div(i, cols // 256)
             tile = lax.rem(i, cols // 256)
             owner = lax.rem(z - step + count, count)
-            at = pl.ds(pl.multiple_of(owner * rows, rows), rows)
+            at = pl.ds(pl.multiple_of(owner * rows + offset, size), size)
             to = pl.ds(pl.multiple_of(tile * 256, 256), 256)
             found = jnp.dot(group[at, :], weights[c, :, to], preferred_element_type=F32)
             if c == 0:
@@ -465,8 +473,20 @@
         copy.start()
         kept.append(copy)
 
+    lift(0)
+    greeted(*reached)
     pass_on(0, 0)
+    own[0].wait()
+    own[1].wait()
+    chunks[0].first()
+    own[2].wait()
+    chunks[1].first()
+    lift(1)
     pass_on(0, 1)
+    own[3].wait()
+    own[4].wait()
+    kept = [pltpu.make_async_copy(own_out, out_full.at[:, pl.ds(0, part)], keep_sem.at[4])]
+    kept[0].start()
     group_rows = rows * count
     starts = doc_starts(lengths_ref)
     index = lax.broadcasted_iota(jnp.int32, (1, KEY // 2), 1).astype(F32)
@@ -479,6 +499,11 @@
         turn = (row - doc_first(row, starts)).astype(F32) * freq
         cos_ref[at, :] = jnp.cos(turn)
         sin_ref[at, :] = jnp.sin(turn)
+
+    for n, (source, target) in enumerate(((cos_ref, cos_hbm), (sin_ref, sin_hbm))):
+        copy = pltpu.make_async_copy(source, target, keep_sem.at[5 + n])
+        copy.start()
+        kept.append(copy)
 
     chunks[0].second()
     chunks[2].first()
@@ -506,17 +531,21 @@
     chunks[2].third()
     chunks[2].done()
     keep(2)
+    project(2, (0, 3))
+    for step in range(3):
+        keep_rows(step)
+    outward.third()
     pass_on(3, 0)
-    outward.third()
-    project(2, (0, 3))
+    for c in range(3):
+        project(c, (3, 1), (0, rows // 2))
     pass_on(3, 1)
+    for c in range(3):
+        project(c, (3, 1), (rows // 2, rows // 2))
+    keep_rows(3)
     turn(3)
     copy = pltpu.make_async_copy(turned, turned_out, keep_sem.at[3])
     copy.start()
     kept.append(copy)
-    project(0, (3, 1))
-    project(1, (3, 1))
-    project(2, (3, 1))
     outward.done()
     for copy in kept:
         copy.wait()
@@ -560,8 +589,10 @@
             jax.ShapeDtypeStruct((group_rows, KEY // 2), F32),
         ),
         in_specs=[VMEM] * 2 + [SMEM] + [ANY] * 5,
-        out_specs=[ANY] * 3 + [VMEM] * 5,
+        out_specs=[ANY] * 8,
         scratch_shapes=[
+            *[pltpu.VMEM((group_rows, cols), BF)] * 3,
+            *[pltpu.VMEM((group_rows, KEY // 2), F32)] * 2,
             pltpu.VMEM((width, group_rows), BF),
             pltpu.VMEM((group_rows, width), BF),
             pltpu.VMEM((3, width, cols), BF),
@@ -570,7 +601,8 @@
             pltpu.SemaphoreType.DMA((moves,)),
             pltpu.SemaphoreType.DMA((moves,)),
             pltpu.SemaphoreType.DMA((5,)),
-            pltpu.SemaphoreType.DMA((5,)),
+            pltpu.SemaphoreType.DMA((7,)),
+            pltpu.SemaphoreType.DMA((12,)),
         ],
         compiler_params=pltpu.CompilerParams(
             collective_id=0, has_side_effects=True, vmem_limit_bytes=LIMIT
@@ -682,7 +714,6 @@
     gain_ref,
     ffn_ref,
     group_ref,
-    tokens_grad,
     wq_out,
     wk_out,
     wv_out,
@@ -690,6 +721,10 @@
     norm_out,
     ffn_out,
     group_out,
+    tokens_hbm,
+    tokens_grad,
+    units,
+    spreads,
     grads,
     weights,
     turned,
@@ -753,6 +788,7 @@
     z_others = [{"tok": tok, "head": lax.rem(z + step, count)} for step in range(1, count)]
     tok_others = [{"tok": place, "head": z} for place in xor_places(tok)[1:]]
     greet(*z_others, *tok_others)
+    gain[...] = arranged(gain_ref, tok)
     moves = Moves(send, recv)
 
     def ring_term(step, side):
@@ -807,6 +843,10 @@
     )
     scatters[0].frees = free_sem
 
+    def spread(ref, value):
+        for n in range(8):
+            ref[:, n * part : (n + 1) * part] = value[n : n + 1, :]
+
     ffn_vec[...] = jnp.zeros_like(ffn_vec)
     group_vec[...] = jnp.zeros_like(group_vec)
     for r, place in enumerate(xor_places(tok)):
@@ -818,68 +858,73 @@
         group_vec[pl.ds(n, 1), :] = group_ref[pl.ds(0, 1), n * part : (n + 1) * part]
     ffn_z = AllSum(moves, ffn_vec, ffn_slots_z, z_others)
     group_tok = AllSum(moves, group_vec, group_slots, tok_others)
-    ffn_z.start()
-    group_tok.start()
     grad_loads[0].wait()
-    for side in range(2):
-        strip_loads[2 * side].wait()
-        strip_loads[2 * side + 1].wait()
-        ring_term(0, side)
-        ring_send(0, side)
+    strip_loads[0].wait()
+    strip_loads[1].wait()
+    ring_term(0, 0)
+    greeted(*z_others, *tok_others)
+    ring_send(0, 0)
+    strip_loads[2].wait()
+    strip_loads[3].wait()
+    ring_term(0, 1)
+    ring_send(0, 1)
     for load in grad_loads[1:]:
         load.wait()
     turned_load.wait()
+    for i in (3, 1, 2, 0):
+        scatters[0].odd(i)
+    for i in (3, 1):
+        scatters[1].odd(i)
+    scatters[0].far()
     ring_term(1, 0)
     ring_term(1, 1)
-    for i in (3, 1, 2, 0):
-        scatters[0].odd(i)
-    group_out[...] = group_tok.total()
-    ffn_vec2[...] = ffn_z.total()
-    ffn_tok = AllSum(moves, ffn_vec2, ffn_slots, tok_others)
-    ffn_tok.start()
     ring_send(1, 0)
-    scatters[0].far()
-    for i in (3, 1):
-        scatters[1].odd(i)
-    ring_send(1, 1)
     for i in (2, 0):
         scatters[1].odd(i)
+    scatters[1].far()
+    ring_send(1, 1)
+    scatters[0].close()
     ring_term(2, 0)
-    scatters[0].close()
     ring_term(2, 1)
-    ring_send(2, 0)
-    scatters[1].far()
     for i in (3, 1):
         scatters[2].odd(i)
-    ring_send(2, 1)
-    scatters[1].close()
+    ring_send(2, 0)
     for i in (2, 0):
         scatters[2].odd(i)
+    scatters[2].far()
+    scatters[1].close()
+    ring_send(2, 1)
     scatters[0].done()
-    scatters[2].far()
-    ffn_out[...] = ffn_tok.total()
     ring_term(3, 0)
     ring_term(3, 1)
-    scatters[1].done()
     scatters[2].close()
-    scatters[2].done()
-
     size = 16
-    for side in range(2):
-        ring[2, side].wait_recv()
-
-    def block(i, total):
+
+    @pl.loop(0, rows // size)
+    def _(i):
         at = pl.ds(pl.multiple_of(i * size, size), size)
         values = arranged(tok_ref.at[at, :], tok).astype(F32)
         mean = jnp.mean(values, axis=-1, keepdims=True)
         centred = values - mean
         inverse = lax.rsqrt(jnp.mean(centred * centred, axis=-1, keepdims=True) + EPS)
-        unit = centred * inverse
+        units[at, :] = centred * inverse
+        spreads[at, :] = inverse
+
+    scatters[1].done()
+    scatters[2].done()
+    for side in range(2):
+        ring[2, side].wait_recv()
+    ffn_z.start()
+    group_tok.start()
+
+    def block(i, total):
+        at = pl.ds(pl.multiple_of(i * size, size), size)
+        unit = units[at, :]
         grad = held[at, :] + ring_in[2, at, :].astype(F32)
         scaled = grad * gain[...]
         first = jnp.mean(scaled, axis=-1, keepdims=True)
         second = jnp.mean(scaled * unit, axis=-1, keepdims=True)
-        found = resid_ref[at, :] + inverse * (scaled - first - unit * second)
+        found = resid_ref[at, :] + spreads[at, :] * (scaled - first - unit * second)
         for r, place in enumerate(xor_places(tok)):
             tokens_grad[at, pl.ds(pl.multiple_of(place * part, part), part)] = found[
                 :, r * part : (r + 1) * part
@@ -887,14 +932,22 @@
         return total + jnp.sum(grad * unit, axis=0, keepdims=True)
 
     total = lax.fori_loop(0, rows // size, block, jnp.zeros((1, width), F32))
+    keep = pltpu.make_async_copy(tokens_grad, tokens_hbm, load_sem.at[count + 5])
+    keep.start()
     for r, place in enumerate(xor_places(tok)):
         norm_vec[pl.ds(place, 1), :] = total[:, r * part : (r + 1) * part]
     norm_z = AllSum(moves, norm_vec, norm_slots_z, z_others)
     norm_z.start()
+    ffn_vec2[...] = ffn_z.total()
+    ffn_tok = AllSum(moves, ffn_vec2, ffn_slots, tok_others)
+    ffn_tok.start()
     norm_vec2[...] = norm_z.total()
     norm_tok = AllSum(moves, norm_vec2, norm_slots, tok_others)
     norm_tok.start()
-    norm_out[...] = norm_tok.total()
+    spread(group_out, group_tok.total())
+    spread(ffn_out, ffn_tok.total())
+    spread(norm_out, norm_tok.total())
+    keep.wait()
     moves.finish()
 
 
@@ -908,18 +961,21 @@
     return pl.pallas_call(
         leave_kernel,
         out_shape=(
-            jax.ShapeDtypeStruct((rows, width), F32),
             jax.ShapeDtypeStruct((part, cols // 2), F32),
             jax.ShapeDtypeStruct((part, cols // 2), F32),
             jax.ShapeDtypeStruct((part, cols), F32),
             jax.ShapeDtypeStruct((part, cols), F32),
-            jax.ShapeDtypeStruct(vector, F32),
-            jax.ShapeDtypeStruct(vector, F32),
-            jax.ShapeDtypeStruct(vector, F32),
+            jax.ShapeDtypeStruct((1, width), F32),
+            jax.ShapeDtypeStruct((1, width), F32),
+            jax.ShapeDtypeStruct((1, width), F32),
+            jax.ShapeDtypeStruct((rows, width), F32),
         ),
         in_specs=[ANY] * 3 + [VMEM] * 5,
-        out_specs=[VMEM] * 8,
+        out_specs=[VMEM] * 7 + [ANY],
         scratch_shapes=[
+            pltpu.VMEM((rows, width), F32),
+            pltpu.VMEM((rows, width), F32),
+            pltpu.VMEM((rows, 1), F32),
             pltpu.VMEM(grads.shape, BF),
             pltpu.VMEM(weights.shape, BF),
             pltpu.VMEM(turned.shape, BF),
@@ -945,7 +1001,7 @@
             pltpu.VMEM((1, width), F32),
             pltpu.SemaphoreType.DMA((moves,)),
             pltpu.SemaphoreType.DMA((moves,)),
-            pltpu.SemaphoreType.DMA((count + 5,)),
+            pltpu.SemaphoreType.DMA((count + 6,)),
             pltpu.SemaphoreType.REGULAR,
         ],
         compiler_params=pltpu.CompilerParams(
@@ -1058,7 +1114,13 @@
     ]
     for copy in own:
         copy.start()
-    greet(*everyone())
+    reached = everyone()
+    greet(*reached)
+    rate = decays(order_ref, heads)
+    across = block_scales(lengths_ref, rate, group_rows, scale_ref, docs_col)
+    docs_row[...] = row_docs(lengths_ref, group_rows)
+    fold = group_weights(lengths_ref, rate, group_rows, False)
+    greeted(*reached)
     moves = Moves(send, recv)
     far_up = moves.go(
         wu_ref, up_full.at[pl.ds(0, part), pl.ds(slice_, slice_)], near["cross"]
@@ -1070,10 +1132,6 @@
     def block_rows(b):
         return pl.ds(pl.multiple_of(b * SPAN, SPAN), SPAN)
 
-    rate = decays(order_ref, heads)
-    across = block_scales(lengths_ref, rate, group_rows, scale_ref, docs_col)
-    docs_row[...] = row_docs(lengths_ref, group_rows)
-    fold = group_weights(lengths_ref, rate, group_rows, False)
 
     def q_cols(h):
         return pl.ds(h * KEY, KEY)
@@ -1322,15 +1380,18 @@
     cot_ref,
     up_ref,
     down_ref,
-    layer_out,
-    far_out,
-    resid_grad,
     gain_out,
     up_own,
     up_far,
     down_own,
     down_far,
+    layer_hbm,
+    far_hbm,
+    resid_hbm,
     branch,
+    layer_out,
+    far_out,
+    resid_grad,
     up,
     down,
     lifted,
@@ -1361,7 +1422,6 @@
     free_sem,
 ):
     near = peers()
-    gain[...] = arranged(gain_ref, lax.axis_index("tok"))
     z = lax.axis_index("head")
     count = lax.axis_size("head")
     rows, width = resid_ref.shape
@@ -1376,7 +1436,9 @@
     ]
     for load in loads:
         load.start()
-    greet(*everyone())
+    reached = everyone()
+    greet(*reached)
+    gain[...] = arranged(gain_ref, lax.axis_index("tok"))
     moves = Moves(send, recv)
     size = 16
 
@@ -1392,6 +1454,8 @@
             inverse = lax.rsqrt(jnp.mean(centred * centred, axis=-1, keepdims=True) + EPS)
             lifted[at, :] = (centred * inverse * gain[...]).astype(BF)
 
+        if side == 0:
+            greeted(*reached)
         pairs.append(
             moves.go(
                 lifted.at[pl.ds(side * side_rows, side_rows), :],
@@ -1519,45 +1583,53 @@
         back_in, branch.at[pl.ds(pl.multiple_of(z * rows, rows), rows), :], load_sem.at[3]
     )
     mine.start()
+    keeps = [pltpu.make_async_copy(resid_grad, resid_hbm, load_sem.at[4])]
+    keeps[0].start()
     sums[0].far()
     for i in (2, 0):
         sums[1].odd(i)
+    sums[1].far()
     pass_on(1, 0)
-    sums[1].far()
     sums[0].close()
-    pass_on(1, 1)
     for i in (3, 1, 2, 0):
         sums[2].odd(i)
+    sums[2].far()
+    pass_on(1, 1)
     sums[1].close()
-    sums[2].far()
+    for i in (3, 1, 2, 0):
+        sums[3].odd(i)
+    sums[3].far()
     pass_on(2, 0)
+    sums[2].close()
 
     @pl.loop(0, width // 256)
     def _(i):
         to = pl.ds(pl.multiple_of(i * 256, 256), 256)
         layer_out[:, to] = resid_ref[:, to] + dot_nn(hidden[pl.ds(0, rows), :], down[:, to])
 
-    for i in (3, 1, 2, 0):
-        sums[3].odd(i)
+    keeps.append(pltpu.make_async_copy(layer_out, layer_hbm, load_sem.at[5]))
+    keeps[-1].start()
     pass_on(2, 1)
-    sums[2].close()
-    sums[3].far()
-    sums[0].done()
-    sums[1].done()
 
     @pl.loop(0, width // 256)
     def _(i):
         to = pl.ds(pl.multiple_of(i * 256, 256), 256)
         far_out[:, to] = dot_nn(hidden[pl.ds(rows, rows), :], down[:, to]).astype(BF)
 
+    keeps.append(pltpu.make_async_copy(far_out, far_hbm, load_sem.at[6]))
+    keeps[-1].start()
+    sums[0].done()
+    sums[1].done()
     sums[3].close()
     pass_on(3, 0)
     sums[2].done()
     down_far[...] = down_sum[...].astype(BF)
+    pass_on(3, 1)
     sums[3].done()
     up_far[...] = up_sum[...].astype(BF)
-    pass_on(3, 1)
     mine.wait()
+    for keep in keeps:
+        keep.wait()
     moves.finish()
 
 
@@ -1588,19 +1660,22 @@
     return pl.pallas_call(
         feed_kernel,
         out_shape=(
-            struct((rows, width), F32),
-            struct((rows, width), BF),
-            struct((rows, width), F32),
             struct((8, width), F32),
             struct(up_piece, F32),
             struct(up_piece, BF),
             struct(down_piece, F32),
             struct(down_piece, BF),
+            struct((rows, width), F32),
+            struct((rows, width), BF),
+            struct((rows, width), F32),
             struct((count * rows, width), BF),
         ),
         in_specs=[VMEM] * 2 + [ANY] * 3,
-        out_specs=[VMEM] * 8 + [ANY],
+        out_specs=[VMEM] * 5 + [ANY] * 4,
         scratch_shapes=[
+            pltpu.VMEM((rows, width), F32),
+            pltpu.VMEM((rows, width), BF),
+            pltpu.VMEM((rows, width), F32),
             pltpu.VMEM((width, wide), BF),
             pltpu.VMEM((wide, width), BF),
             pltpu.VMEM((2 * rows, width), BF),
@@ -1621,7 +1696,7 @@
             pltpu.VMEM((1, width), F32),
             pltpu.SemaphoreType.DMA((moves,)),
             pltpu.SemaphoreType.DMA((moves,)),
-            pltpu.SemaphoreType.DMA((4,)),
+            pltpu.SemaphoreType.DMA((7,)),
             pltpu.SemaphoreType.REGULAR((2,)),
         ],
         compiler_params=pltpu.CompilerParams(
@@ -1720,7 +1795,13 @@
     ]
     for load in loads:
         load.start()
-    greet(*everyone())
+    reached = everyone()
+    greet(*reached)
+    rate = decays(order_ref, heads)
+    across = block_scales(lengths_ref, rate, group_rows, scale_ref, docs_col)
+    docs_row[...] = row_docs(lengths_ref, group_rows)
+    fold = group_weights(lengths_ref, rate, group_rows, True)
+    greeted(*reached)
     moves = Moves(send, recv)
     swaps = [
         moves.go(far_ref, far_in, near["pair"]),
@@ -1740,10 +1821,6 @@
     def v_cols(h):
         return pl.ds(h * VAL, VAL)
 
-    rate = decays(order_ref, heads)
-    across = block_scales(lengths_ref, rate, group_rows, scale_ref, docs_col)
-    docs_row[...] = row_docs(lengths_ref, group_rows)
-    fold = group_weights(lengths_ref, rate, group_rows, True)
     for load in loads[:5]:
         load.wait()
 
@@ -2305,7 +2382,7 @@
         w_up, w_down,
     )
     (
-        layer_own, far_out, resid_grad, ffn_terms, up_own, up_far, down_own, down_far, branch
+        ffn_terms, up_own, up_far, down_own, down_far, layer_own, far_out, resid_grad, branch
     ) = feed_forward(resid, ffn_gain, cot_pair, up_full, down_full)
     w_out_grad, group_terms, layer_out, all_grad, up_in, down_in = recall(
         doc_lengths, head_order, group_gain, qk_rows, v_rows, gate, unit_g, inverse_g, states,
@@ -2314,7 +2391,7 @@
     w_up_grad = up_own + up_in.astype(F32)
     w_down_grad = down_own + down_in.astype(F32)
     (
-        tokens_grad, w_query_grad, w_key_grad, w_value_grad, w_gate_grad, norm_sum, ffn_sum, group_sum
+        w_query_grad, w_key_grad, w_value_grad, w_gate_grad, norm_sum, ffn_sum, group_sum, tokens_grad
     ) = depart(all_grad, qkvg_full, turned, tokens, resid_grad, norm_gain, ffn_terms, group_terms)
     return (
         layer_out,

time: 531 us -> 507 us (0.955)
  Pallas kernels: 507 us -> 485 us
    pallas_call x2, Pallas kernels: 235 us -> 215 us  [the longest x1 127 us: feed_forward(): pl.pallas_call(feed_kernel, out_shape=(struct((8, width), F32), struct(up...]
    unnamed x31 -> x33, local copies, waits for them, and re-layouts: 10.9 us -> 8.03 us
where the time goes in v6:
time: 507 us; the launch traced here: 499 us
  Pallas kernels  485 us (96%)
  local copies, waits for them, and re-layouts  9.45 us (2%)
    pallas_call x1, Pallas kernels, feed_forward(): pl.pallas_call(feed_kernel, out_shape=(struct((8, width), F32), struct(up...  127 us
    pallas_call x1, Pallas kernels, retain(): pl.pallas_call(retain_kernel, out_shape=(struct((rows, width), F32), stru...  122 us
    pallas_call x1, Pallas kernels, enter(): pl.pallas_call(enter_kernel, out_shape=(jax.ShapeDtypeStruct((width, grou...  88.7 us
    pallas_call x1, Pallas kernels, depart(): pl.pallas_call(leave_kernel, out_shape=(jax.ShapeDtypeStruct((part, cols...  88.3 us
    pallas_call x1, Pallas kernels, recall(): pl.pallas_call(recall_kernel, out_shape=(struct(piece, F32), struct((8, c...  58.6 us

profile of v6, /device:TPU:0, one launch (start us, length us, event | category | flops | bytes accessed | tf_op | source)
XLA Modules:
  0.0 498.6 jit_solution(2954126117938886895)
XLA Ops:
  0.6 88.7 %shard_map.229 = (bf16[2048,1024]{1,0:T(8,128)(2,1)}, bf16[2048,3072]{1,0:T(8,128)(2,1)}, bf16[1024,2048]{1,0:T(8,128)(2,1)}, bf16[1024,1024]{1,0:T(8,128)(2,1)}...) custom-call(bf16[256,2048]{1,0:T(8,128)(2,1)} %tok_ref.3, ...), custom_call_target="tpu_custom_call" | custom-call | flops 12884901888 | bytes 41943040 | tf_op jit(solution)/shard_map/pallas_call | solution.py:579
  89.4 122.4 %shard_map.230 = (f32[256,2048]{1,0:T(8,128)}, f32[1024,2]{1,0:T(8,128)}, bf16[1024,1024]{1,0:T(8,128)(2,1)}, bf16[1024,512]{1,0:T(8,128)(2,1)}, bf16[512,2048]{...) custom-call(s32[4]{0:T(128)} %lengths_ref.5, s32[8]{0:T(128)} %order_ref.3, ...), custom_call_target="tpu_custom_call" | custom-call | flops 12884901888 | bytes 41943040 | tf_op jit(solution)/shard_map/pallas_call | solution.py:1334
  211.7 126.7 %shard_map.231 = (f32[8,2048]{1,0:T(8,128)}, f32[256,1024]{1,0:T(8,128)}, bf16[256,1024]{1,0:T(8,128)(2,1)}, f32[1024,256]{1,0:T(8,128)}, bf16[1024,256]{1,0:T(8...) custom-call(f32[256,2048]{1,0:T(8,128)} %get-tuple-element.55.resid_, ...), custom_call_target="tpu_custom_call" | custom-call | flops 27917287424 | bytes 41943040 | tf_op jit(solution)/shard_map/pallas_call | solution.py:1660
  338.5 0.0 copy-start.4
  338.5 58.6 %shard_map.232 = (f32[1024,256]{1,0:T(8,128)}, f32[8,1024]{1,0:T(8,128)}, bf16[256,2048]{1,0:T(8,128)(2,1)}, bf16[1024,3072]{1,0:T(8,128)(2,1)}, bf16[256,1024]{1,0:T(8,128)(2,1)}, /*index=5*/bf16[1024,256]{1,0:T(8,128)(2,1)}) custom-call(s32[4]{0:T(128)} %lengths_ref.5, s32[8]{0:T(128)} %order_ref.3, f32[1,1024]{1,0:T(1,128)} %bitcast.13, ...), custom_call_target="tpu_custom_call" | custom-call | flops 21474836480 | bytes 41943040 | tf_op jit(solution)/shard_map/pallas_call | solution.py:1990
  397.1 0.0 copy-start.3
  397.1 0.0 copy-start.7
  397.1 0.0 copy-done.4
  397.1 2.2 convert_add_fusion
  399.3 0.0 copy-done.3
  399.3 0.0 copy-done.7
  399.3 1.1 convert_add_fusion.1
  400.4 0.0 copy-start.2
  400.4 88.3 %shard_map.233 = (f32[256,512]{1,0:T(8,128)}, f32[256,512]{1,0:T(8,128)}, f32[256,1024]{1,0:T(8,128)}, f32[256,1024]{1,0:T(8,128)}, f32[1,2048]{1,0:T(1,128)}, /...) custom-call(bf16[1024,3072]{1,0:T(8,128)(2,1)} %get-tuple-element.71.grads_ref, ...), custom_call_target="tpu_custom_call" | custom-call | flops 21474836480 | bytes 41943040 | tf_op jit(solution)/shard_map/pallas_call | solution.py:961
  488.7 0.0 copy-start
  488.7 1.4 slice.6
  490.1 0.0 copy-done.2
  490.1 1.0 copy.35
  491.1 0.0 copy-done
  491.1 0.0 copy-start.11
  491.1 0.0 copy-start.9
  491.1 0.0 copy-start.8
  491.1 1.3 copy.36
  492.4 0.0 copy-done.11
  492.5 0.0 copy-start.6
  492.5 0.6 copy.37
  493.1 0.0 copy-done.9
  493.1 0.0 copy-start.5
  493.1 0.8 copy.38
  493.9 0.0 copy-done.8
  493.9 0.8 copy.39
  494.6 0.0 copy-done.6
  494.7 0.0 copy-start.1
  494.7 1.0 copy.40
  495.6 0.0 copy-done.5
  495.6 0.0 copy-start.10
  495.6 1.0 copy.41
  496.6 0.0 copy-done.1
  496.6 1.0 copy.42
  497.6 0.0 copy-done.10
  497.6 0.6 copy.43
Async XLA Ops:
  338.5 58.6 %copy-start.4 = (f32[1024,256]{1,0:T(8,128)S(1)}, f32[1024,256]{1,0:T(8,128)}, u32[]{:S(2)}) copy-start(f32[1024,256]{1,0:T(8,128)} %get-tuple-element.88) | copy-start | bytes 3145732
  397.1 2.3 copy-start.3
  397.1 2.3 copy-start.7
  400.4 89.7 %copy-start.2 = (bf16[256,2048]{1,0:T(8,128)(2,1)S(1)}, bf16[256,2048]{1,0:T(8,128)(2,1)}, u32[]{:S(2)}) copy-start(bf16[256,2048]{1,0:T(8,128)(2,1)} %get-tuple-element.102) | copy-start | bytes 3145732
  488.7 2.4 copy-start
  491.1 1.3 copy-start.11
  491.1 1.9 copy-start.9
  491.1 2.7 copy-start.8
  492.5 2.2 copy-start.6
  493.1 2.6 copy-start.5
  494.7 1.9 copy-start.1
  495.6 1.9 copy-start.10

commit v7 on v6

--- a/solution.py
+++ b/solution.py
@@ -457,14 +457,23 @@
             else:
                 gate_out[at, to] = found.astype(BF)
 
-    def turn(step):
+    def turn(step, offset, size):
         owner = lax.rem(z - step + count, count)
+        to = pl.ds(pl.multiple_of(owner * rows + offset, size), size)
 
         @pl.loop(0, width // 256)
         def _(i):
             at = pl.ds(pl.multiple_of(i * 256, 256), 256)
-            to = pl.ds(pl.multiple_of(owner * rows, rows), rows)
             turned[at, to] = group[to, at].T
+
+    def keep_turned(step):
+        owner = lax.rem(z - step + count, count)
+        to = pl.ds(pl.multiple_of(owner * rows, rows), rows)
+        copy = pltpu.make_async_copy(
+            turned.at[:, to], turned_out.at[:, to], rows_sem.at[3 * count + step]
+        )
+        copy.start()
+        kept.append(copy)
 
     def keep(c):
         copy = pltpu.make_async_copy(
@@ -516,8 +525,9 @@
     keep(0)
     project(0, (0, 2))
     pass_on(2, 0)
-    turn(0)
-    turn(1)
+    for step in range(2):
+        turn(step, 0, rows)
+        keep_turned(step)
     chunks[2].second()
     pass_on(2, 1)
     chunks[1].third()
@@ -527,7 +537,8 @@
     outward.second()
     project(0, (2, 1))
     project(1, (2, 1))
-    turn(2)
+    turn(2, 0, rows)
+    keep_turned(2)
     chunks[2].third()
     chunks[2].done()
     keep(2)
@@ -536,16 +547,15 @@
         keep_rows(step)
     outward.third()
     pass_on(3, 0)
+    turn(3, 0, rows // 2)
     for c in range(3):
         project(c, (3, 1), (0, rows // 2))
     pass_on(3, 1)
+    turn(3, rows // 2, rows // 2)
+    keep_turned(3)
     for c in range(3):
         project(c, (3, 1), (rows // 2, rows // 2))
     keep_rows(3)
-    turn(3)
-    copy = pltpu.make_async_copy(turned, turned_out, keep_sem.at[3])
-    copy.start()
-    kept.append(copy)
     outward.done()
     for copy in kept:
         copy.wait()
@@ -602,7 +612,7 @@
             pltpu.SemaphoreType.DMA((moves,)),
             pltpu.SemaphoreType.DMA((5,)),
             pltpu.SemaphoreType.DMA((7,)),
-            pltpu.SemaphoreType.DMA((12,)),
+            pltpu.SemaphoreType.DMA((16,)),
         ],
         compiler_params=pltpu.CompilerParams(
             collective_id=0, has_side_effects=True, vmem_limit_bytes=LIMIT
@@ -844,7 +854,7 @@
     scatters[0].frees = free_sem
 
     def spread(ref, value):
-        for n in range(8):
+        for n in range(ref.shape[1] // part):
             ref[:, n * part : (n + 1) * part] = value[n : n + 1, :]
 
     ffn_vec[...] = jnp.zeros_like(ffn_vec)
@@ -967,7 +977,7 @@
             jax.ShapeDtypeStruct((part, cols), F32),
             jax.ShapeDtypeStruct((1, width), F32),
             jax.ShapeDtypeStruct((1, width), F32),
-            jax.ShapeDtypeStruct((1, width), F32),
+            jax.ShapeDtypeStruct((1, cols), F32),
             jax.ShapeDtypeStruct((rows, width), F32),
         ),
         in_specs=[ANY] * 3 + [VMEM] * 5,
@@ -1840,9 +1850,14 @@
     for h in range(heads):
         gain = gain_ref[:, h * VAL : (h + 1) * VAL]
 
+        @pl.loop(0, group_rows // 256)
+        def _(i):
+            at = pl.ds(pl.multiple_of(i * 256, 256), 256)
+            dv[at, v_cols(h)] = dot_nt(branch[at, :], out_weights[v_cols(h), :])
+
         def tile_back(i, total):
-            at = pl.ds(pl.multiple_of(i * 128, 128), 128)
-            grad = dot_nt(branch[at, :], out_weights[v_cols(h), :]).astype(BF).astype(F32)
+            at = pl.ds(pl.multiple_of(i * 16, 16), 16)
+            grad = dv[at, v_cols(h)].astype(BF).astype(F32)
             gate = gate_ref[at, v_cols(h)].astype(F32)
             sigma = 1.0 / (1.0 + jnp.exp(-gate))
             swish = gate * sigma
@@ -1860,7 +1875,7 @@
             return total + jnp.sum(inner * unit, axis=0, keepdims=True)
 
         gains[pl.ds(0, 1), v_cols(h)] = lax.fori_loop(
-            0, group_rows // 128, tile_back, jnp.zeros((1, VAL), F32)
+            0, group_rows // 16, tile_back, jnp.zeros((1, VAL), F32), unroll=2
         )
         if h == 0:
             for load in loads[5:]:
@@ -2401,7 +2416,7 @@
         w_key_grad,
         w_value_grad,
         w_gate_grad,
-        group_sum.reshape(-1)[: group_gain.shape[0]],
+        group_sum.reshape(-1),
         w_out_grad,
         ffn_sum.reshape(-1),
         w_up_grad,

time: 507 us -> 506 us (level)
  no operation moved by 1% of the time
where the time goes in v7:
time: 506 us; the launch traced here: 498 us
  Pallas kernels  483 us (95%)
  local copies, waits for them, and re-layouts  9.61 us (2%)
    pallas_call x1, Pallas kernels, feed_forward(): pl.pallas_call(feed_kernel, out_shape=(struct((8, width), F32), struct(up...  127 us
    pallas_call x1, Pallas kernels, retain(): pl.pallas_call(retain_kernel, out_shape=(struct((rows, width), F32), stru...  122 us
    pallas_call x1, Pallas kernels, depart(): pl.pallas_call(leave_kernel, out_shape=(jax.ShapeDtypeStruct((part, cols...  88.2 us
    pallas_call x1, Pallas kernels, enter(): pl.pallas_call(enter_kernel, out_shape=(jax.ShapeDtypeStruct((width, grou...  88.1 us
    pallas_call x1, Pallas kernels, recall(): pl.pallas_call(recall_kernel, out_shape=(struct(piece, F32), struct((8, c...  58.2 us

profile of v7, /device:TPU:0, one launch (start us, length us, event | category | flops | bytes accessed | tf_op | source)
XLA Modules:
  0.0 497.5 jit_solution(5225765382301402372)
XLA Ops:
  0.6 88.1 %shard_map.229 = (bf16[2048,1024]{1,0:T(8,128)(2,1)}, bf16[2048,3072]{1,0:T(8,128)(2,1)}, bf16[1024,2048]{1,0:T(8,128)(2,1)}, bf16[1024,1024]{1,0:T(8,128)(2,1)}...) custom-call(bf16[256,2048]{1,0:T(8,128)(2,1)} %tok_ref.3, ...), custom_call_target="tpu_custom_call" | custom-call | flops 12884901888 | bytes 41943040 | tf_op jit(solution)/shard_map/pallas_call | solution.py:589
  88.7 122.4 %shard_map.230 = (f32[256,2048]{1,0:T(8,128)}, f32[1024,2]{1,0:T(8,128)}, bf16[1024,1024]{1,0:T(8,128)(2,1)}, bf16[1024,512]{1,0:T(8,128)(2,1)}, bf16[512,2048]{...) custom-call(s32[4]{0:T(128)} %lengths_ref.5, s32[8]{0:T(128)} %order_ref.3, ...), custom_call_target="tpu_custom_call" | custom-call | flops 12884901888 | bytes 41943040 | tf_op jit(solution)/shard_map/pallas_call | solution.py:1344
  211.1 126.6 %shard_map.231 = (f32[8,2048]{1,0:T(8,128)}, f32[256,1024]{1,0:T(8,128)}, bf16[256,1024]{1,0:T(8,128)(2,1)}, f32[1024,256]{1,0:T(8,128)}, bf16[1024,256]{1,0:T(8...) custom-call(f32[256,2048]{1,0:T(8,128)} %get-tuple-element.55.resid_, ...), custom_call_target="tpu_custom_call" | custom-call | flops 27917287424 | bytes 41943040 | tf_op jit(solution)/shard_map/pallas_call | solution.py:1670
  337.7 0.0 copy-start.4
  337.7 58.2 %shard_map.232 = (f32[1024,256]{1,0:T(8,128)}, f32[8,1024]{1,0:T(8,128)}, bf16[256,2048]{1,0:T(8,128)(2,1)}, bf16[1024,3072]{1,0:T(8,128)(2,1)}, bf16[256,1024]{1,0:T(8,128)(2,1)}, /*index=5*/bf16[1024,256]{1,0:T(8,128)(2,1)}) custom-call(s32[4]{0:T(128)} %lengths_ref.5, s32[8]{0:T(128)} %order_ref.3, f32[1,1024]{1,0:T(1,128)} %bitcast.13, ...), custom_call_target="tpu_custom_call" | custom-call | flops 21474836480 | bytes 41943040 | tf_op jit(solution)/shard_map/pallas_call | solution.py:2005
  395.9 0.0 copy-start.3
  395.9 0.0 copy-start.7
  395.9 0.0 copy-done.4
  395.9 2.2 convert_add_fusion
  398.2 0.0 copy-done.3
  398.2 0.0 copy-done.7
  398.2 1.1 convert_add_fusion.1
  399.3 0.0 copy-start.2
  399.3 88.2 %shard_map.233 = (f32[256,512]{1,0:T(8,128)}, f32[256,512]{1,0:T(8,128)}, f32[256,1024]{1,0:T(8,128)}, f32[256,1024]{1,0:T(8,128)}, f32[1,2048]{1,0:T(1,128)}, /...) custom-call(bf16[1024,3072]{1,0:T(8,128)(2,1)} %get-tuple-element.71.grads_ref, ...), custom_call_target="tpu_custom_call" | custom-call | flops 21474836480 | bytes 41943040 | tf_op jit(solution)/shard_map/pallas_call | solution.py:971
  487.5 0.0 copy-start
  487.5 0.0 copy-done.2
  487.5 1.0 copy.36
  488.5 1.0 copy-done
  489.5 0.0 copy-start.11
  489.5 0.0 copy-start.9
  489.5 0.0 copy-start.8
  489.5 1.3 copy.37
  490.8 0.0 copy-done.11
  490.8 0.0 copy-start.6
  490.8 0.6 copy.38
  491.4 0.0 copy-done.9
  491.4 0.0 copy-start.5
  491.4 0.8 copy.39
  492.2 0.0 copy-done.8
  492.2 0.8 copy.40
  493.0 0.0 copy-done.6
  493.0 0.0 copy-start.12
  493.0 0.0 copy-start.1
  493.0 1.0 copy.41
  494.0 0.0 copy-done.5
  494.0 0.0 copy-start.10
  494.0 1.0 copy.42
  494.9 0.0 copy-done.12
  494.9 0.6 copy.43
  495.5 0.0 copy-done.1
  495.5 1.0 copy.44
  496.5 0.0 copy-done.10
  496.5 0.6 copy.45
Async XLA Ops:
  337.7 58.3 %copy-start.4 = (f32[1024,256]{1,0:T(8,128)S(1)}, f32[1024,256]{1,0:T(8,128)}, u32[]{:S(2)}) copy-start(f32[1024,256]{1,0:T(8,128)} %get-tuple-element.88) | copy-start | bytes 3145732
  395.9 2.3 copy-start.3
  395.9 2.3 copy-start.7
  399.3 88.2 %copy-start.2 = (bf16[256,2048]{1,0:T(8,128)(2,1)S(1)}, bf16[256,2048]{1,0:T(8,128)(2,1)}, u32[]{:S(2)}) copy-start(bf16[256,2048]{1,0:T(8,128)(2,1)} %get-tuple-element.102) | copy-start | bytes 3145732
  487.5 2.0 copy-start
  489.5 1.3 copy-start.11
  489.5 1.9 copy-start.9
  489.5 2.7 copy-start.8
  490.8 2.2 copy-start.6
  491.4 2.6 copy-start.5
  493.0 2.0 copy-start.12
  493.0 2.5 copy-start.1
  494.0 2.5 copy-start.10
